TPU v7x, 512 devices: a whole 4x4x16 slice. The times are simulated.
512 devices in a mesh: head: 8 (over z_hi, core), blk: 64 (over z_lo, x, y).
Axes of the slice: x: 4, y: 4, z: 16 (z_hi: 4, z_lo: 4; z = z_hi * 4 + z_lo), core: 2. Of those that a mesh axis runs over, the one named last changes fastest.
Arguments:
- queries: bfloat16 [8192, 3072], P(('blk', 'head'))
- keys_in: bfloat16 [8192, 3072], P(('blk', 'head'))
- values: bfloat16 [8192, 3072], P(('blk', 'head')), may hold values from -6 to 6
- block_mask: int32 [24, 64, 64], P('head', 'blk'), may hold values from 0 to 1, as said below
- w_out: bfloat16 [3072, 3072], P('head'), may hold values from -0.109375 to 0.109375
Outputs:
- mixed: bfloat16 [8192, 3072], P(('blk', 'head'))
Inputs may be any that keep to these rules, and one draw needn't show every extreme that they name: block_mask[h, i, i] = 1, block_mask[h, i, i - 1] = 1 and block_mask[h, i, i + 1] = 1 where those blocks exist, and block_mask[h, i, 0] = 1, for every head and query block; elsewhere the share of ones falls with the distance |i - j| and differs from head to head and from query block to query block.
All inputs are finite; a program needn't handle non-finite values.
Results may differ from a plain program's by a relative error of at most 0.02.
Values may be sent and summed in bfloat16 or wider, within the bound.
No kernel may reach another device: no remote copies, remote signals or barrier semaphores. Data moves between devices by JAX's collectives and lax.ppermute only.
A program may use at most 128 MiB of HBM per device.

v0:
```python
import jax
import jax.numpy as jnp
from jax import lax
from jax.sharding import PartitionSpec as P


def attend(state, query_heads, key_heads, value_heads, allowed, inv_root):
    old_largest, old_total, old_summed = state
    scores = (
        jnp.einsum("qhd,khd->hqk", query_heads, key_heads, preferred_element_type=jnp.float32)
        * inv_root
    )
    masked = jnp.where(allowed, scores, -1e30)
    new_largest = jnp.maximum(old_largest, jnp.max(masked, axis=2))
    weights = jnp.where(allowed, jnp.exp(scores - new_largest[:, :, None]), 0.0)
    rescale = jnp.exp(old_largest - new_largest)
    new_total = old_total * rescale + jnp.sum(weights, axis=2)
    product = jnp.einsum(
        "hqk,khd->hqd",
        weights.astype(jnp.bfloat16),
        value_heads,
        preferred_element_type=jnp.float32,
    )
    return (new_largest, new_total, old_summed * rescale[:, :, None] + product)


def fold_keys(state, query_heads, key_heads, value_heads, row_mask, block_rows, inv_root):
    amount = key_heads.shape[0]
    width = 1024

    def one_part(current, begin):
        key_part = lax.dynamic_slice_in_dim(key_heads, begin, width, 0)
        value_part = lax.dynamic_slice_in_dim(value_heads, begin, width, 0)
        key_blocks = (begin + jnp.arange(width, dtype=jnp.int32)) // block_rows
        allowed = jnp.take(row_mask, key_blocks, axis=2) > 0
        return attend(current, query_heads, key_part, value_part, allowed, inv_root)

    return lax.fori_loop(
        0,
        amount // width,
        lambda step, current: one_part(current, (step * width).astype(jnp.int32)),
        state,
    )


def start_state(heads, rows, head_size):
    return (
        jnp.full((heads, rows), -1e30, jnp.float32),
        jnp.zeros((heads, rows), jnp.float32),
        jnp.zeros((heads, rows, head_size), jnp.float32),
    )


def finish(state):
    largest, total, summed = state
    safe_total = jnp.where(total > 0.0, total, 1.0)
    return (summed / safe_total[:, :, None]).astype(jnp.bfloat16)


def local(queries, keys_in, values, block_mask, w_out):
    query_all, key_all, value_all = (
        lax.all_to_all(queries, "head", split_axis=1, concat_axis=0, tiled=True),
        lax.all_to_all(keys_in, "head", split_axis=1, concat_axis=0, tiled=True),
        lax.all_to_all(values, "head", split_axis=1, concat_axis=0, tiled=True),
    )
    local_rows = query_all.shape[0]
    heads_here, blocks_here, block_count = block_mask.shape
    head_size = query_all.shape[1] // heads_here
    block_rows = local_rows // blocks_here
    inv_root = 1.0 / head_size**0.5
    query_heads = query_all.reshape(local_rows, heads_here, head_size)
    row_mask = jnp.repeat(block_mask, block_rows, axis=1)
    begin = start_state(heads_here, local_rows, head_size)
    key_piece = lax.all_gather(key_all, "blk", axis=0, tiled=True)
    value_piece = lax.all_gather(value_all, "blk", axis=0, tiled=True)
    amount = key_piece.shape[0]
    key_heads = key_piece.reshape(amount, heads_here, head_size)
    value_heads = value_piece.reshape(amount, heads_here, head_size)
    folded = fold_keys(begin, query_heads, key_heads, value_heads, row_mask, block_rows, inv_root)
    attended_heads = finish(folded)
    attended = attended_heads.transpose(1, 0, 2).reshape(local_rows, heads_here * head_size)
    return lax.psum_scatter(
        jnp.dot(attended, w_out, preferred_element_type=jnp.float32).astype(jnp.bfloat16),
        "head",
        scatter_dimension=0,
        tiled=True,
    )


def solution(mesh):
    placed = (
        P(("blk", "head"), None),
        P(("blk", "head"), None),
        P(("blk", "head"), None),
        P("head", "blk", None),
        P("head", None),
    )
    return jax.shard_map(
        local, mesh=mesh, in_specs=placed, out_specs=P(("blk", "head"), None), check_vma=False
    )
```

profile of v0, /device:TPU:1, one launch (start us, length us, event | category | flops | bytes accessed | tf_op | source)
XLA Modules:
  0.0 964.1 jit_solution(4029569379335705117)
XLA Ops:
  7.6 29.2 %all_to_all.54 = bf16[16,8,384]{2,0,1:T(8,128)(2,1)} all-to-all(bf16[16,8,384]{2,0,1:T(8,128)(2,1)S(1)} %bitcast.64), channel_id=1, replica_groups=mesh['head'=8,'blk'=64] {'head'}, dimensions={1} | all-to-all | bytes 196608 | tf_op jit(solution)/shard_map/all_to_all | solution.py:63
  37.7 19.5 %all_to_all.55 = bf16[16,8,384]{2,0,1:T(8,128)(2,1)} all-to-all(bf16[16,8,384]{2,0,1:T(8,128)(2,1)S(1)} %bitcast.65), channel_id=1, replica_groups=mesh['head'=8,'blk'=64] {'head'}, dimensions={1} | all-to-all | bytes 196608 | tf_op jit(solution)/shard_map/all_to_all | solution.py:64
  58.8 4.8 all-to-all-start.1
  64.3 14.2 %all-to-all-done.1 = bf16[16,8,384]{2,0,1:T(8,128)(2,1)S(1)} async-done(((bf16[16,8,384]{2,0,1:T(8,128)(2,1)}), bf16[16,8,384]{2,0,1:T(8,128)(2,1)S(1)}, u32[]{:S(2)}, u32[]{:S(2)}) %all-to-all-start.1) | async-done | bytes 98336 | tf_op jit(solution)/shard_map/all_to_all | solution.py:62
  78.6 276.5 %all-gather.3.cloned.1.call-done = bf16[8192,384]{1,0:T(8,128)(2,1)} async-done(((bf16[128,384]{1,0:T(8,128)(2,1)}), bf16[8192,384]{1,0:T(8,128)(2,1)}) %all-gather.3.cloned.1.call-update) | async-done | bytes 6291472 | tf_op jit(solution)/shard_map/all_gather | solution.py:74
  355.1 8.7 copy.32
  363.8 353.2 %all-gather.5.cloned.1.call-done = bf16[8192,384]{1,0:T(8,128)(2,1)} async-done(((bf16[128,384]{1,0:T(8,128)(2,1)}), bf16[8192,384]{1,0:T(8,128)(2,1)}) %all-gather.5.cloned.1.call-update) | async-done | bytes 6291472 | tf_op jit(solution)/shard_map/all_gather | solution.py:75
  717.0 8.6 copy.35
  725.6 137.5 %while.20 = (s32[]{:T(128)}, f32[3,128]{1,0:T(4,128)S(1)}, f32[3,128]{1,0:T(4,128)S(1)}, f32[3,128,128]{2,1,0:T(8,128)S(1)}, bf16[8192,3,128]{0,2,1:T(8,128)(2,1...) while((s32[]{:T(128)}, f32[3,128]{1,0:T(4,128)S(1)}, ...), condition=%wide.region_3.4_spmd.clone, body=%wide.region_0.3_spmd.clone.sunk | while | flops 205844352 | bytes 20687832 | solution.py:38
  728.5 7.9 gather_fusion
  742.8 2.7 convolution_multiply_fusion.2
  745.7 7.9 gather_fusion
  760.0 2.7 convolution_multiply_fusion.2
  762.9 7.9 gather_fusion
  777.2 2.7 convolution_multiply_fusion.2
  780.1 7.9 gather_fusion
  794.4 2.7 convolution_multiply_fusion.2
  797.3 7.9 gather_fusion
  811.6 2.7 convolution_multiply_fusion.2
  814.5 7.9 gather_fusion
  828.8 2.7 convolution_multiply_fusion.2
  831.7 7.9 gather_fusion
  848.9 7.9 gather_fusion
  864.9 92.7 %reduce-scatter.2.cloned.1.call-done = bf16[16,3072]{1,0:T(8,128)(2,1)} async-done(((bf16[128,3072]{1,0:T(8,128)(2,1)}), bf16[16,3072]{1,0:T(8,128)(2,1)}) %reduce-scatter.2.cloned.1.call-update) | async-done | bytes 98320 | tf_op jit(solution)/shard_map/reduce_scatter | solution.py:82
  (119 shorter events, 63.0 us)
Async XLA Ops:
  6.5 856.8 %copy-start = (bf16[384,3072]{1,0:T(8,128)(2,1)S(1)}, bf16[384,3072]{1,0:T(8,128)(2,1)}, u32[]{:S(2)}) copy-start(bf16[384,3072]{1,0:T(8,128)(2,1)} %param.11) | copy-start | bytes 7077892
  6.5 348.6 %all-gather.3.cloned.1.call-start = ((), (), s32[]{:S(2)}) async-start(), calls=%async_computation.4 | async-start | bytes 6389760 | tf_op jit(solution)/shard_map/all_gather | solution.py:74
  36.8 680.2 %all-gather.5.cloned.1.call-start = ((), (), s32[]{:S(2)}) async-start(), calls=%async_computation.5 | async-start | bytes 6389760 | tf_op jit(solution)/shard_map/all_gather | solution.py:75
  58.8 19.8 %all-to-all-start.1 = ((bf16[16,8,384]{2,0,1:T(8,128)(2,1)}), bf16[16,8,384]{2,0,1:T(8,128)(2,1)S(1)}, u32[]{:S(2)}, u32[]{:S(2)}) async-start(bf16[16,8,384]{2,0,1:T(8,128)(2,1)} %bitcast.44), calls=%async_computation.1 | async-start | bytes 196608 | tf_op jit(solution)/shard_map/all_to_all | solution.py:62
  63.6 894.0 %reduce-scatter.2.cloned.1.call-start = ((), (), s32[]{:S(2)}) async-start(), calls=%async_computation.6 | async-start | bytes 884736 | tf_op jit(solution)/shard_map/reduce_scatter | solution.py:82
  739.0 1.9 copy-start.1
  756.2 1.9 copy-start.1
  773.4 1.9 copy-start.1
  790.6 1.9 copy-start.1
  807.8 1.9 copy-start.1
  825.0 1.9 copy-start.1
  842.2 1.9 copy-start.1
  859.4 1.9 copy-start.1
Sparse Core Ops, SparseCore 0:
  36.9 318.1 all-gather.2
  357.2 359.7 all-gather.4
  865.0 92.5 reduce-scatter.1
where the time goes:
time: 967 us; the launch traced here: 964 us
  waiting for transfers between devices  737 us (76%)
  local copies, waits for them, and re-layouts  86.3 us (9%)
  blocking collectives  48.6 us (5%)
  matrix products  37.8 us (4%)
  other arithmetic  36.1 us (4%)
  between operations  13.2 us (1%)
    all_gather x1, waiting for transfers between devices, local(): value_piece = lax.all_gather(value_all, 'blk', axis=0, tiled=True)  353 us
    all_gather x1, waiting for transfers between devices, local(): key_piece = lax.all_gather(key_all, 'blk', axis=0, tiled=True)  276 us
    reduce_scatter x1, waiting for transfers between devices, local(): lax.psum_scatter(jnp.dot(attended, w_out, preferred_element_type=jnp.floa...  92.7 us
    gather x8, local copies, waits for them, and re-layouts, one_part(): allowed = jnp.take(row_mask, key_blocks, axis=2) > 0  63.5 us
    all_to_all x1, blocking collectives, local(): lax.all_to_all(keys_in, 'head', split_axis=1, concat_axis=0, tiled=True)  29.2 us
    dot_general x8, matrix products, attend(): jnp.einsum('qhd,khd->hqk', query_heads, key_heads, preferred_element_type...  21.9 us
    reduce_max x8, other arithmetic, attend(): new_largest = jnp.maximum(old_largest, jnp.max(masked, axis=2))  20.3 us
    all_to_all x1, blocking collectives, local(): lax.all_to_all(values, 'head', split_axis=1, concat_axis=0, tiled=True)  19.5 us
  transfers between devices with their start and end apart: 4, of which 4 were waited for; matrix products, arithmetic and copies ran while one was open for 1% of the time, Pallas kernels for 0%

commit v1 on v0

v1 whole, which is shorter than its diff:
```python
import functools

import jax
import jax.numpy as jnp
from jax import lax
from jax.experimental import pallas as pl
from jax.experimental.pallas import tpu as pltpu
from jax.sharding import Mesh, PartitionSpec as P

BF = jnp.bfloat16
F32 = jnp.float32
AXES = ("z_hi", "core", "z_lo", "x", "y")
LOW = -1e30
LOG2E = 1.4426950408889634


def pack_kernel(q_ref, k_ref, v_ref, mask_ref, out_ref):
    seen = jnp.concatenate([mask_ref[...].astype(F32), jnp.zeros((3, 64), F32)], axis=1)
    for slot in range(4):
        row = seen[min(slot, 2) : min(slot, 2) + 1]
        tail = jnp.concatenate([row, jnp.zeros((7, 128), F32)], axis=0).astype(BF)
        for core in range(2):
            for z_hi in range(4):
                head = 3 * (2 * z_hi + core) + slot
                place = slot * 8 + core * 4 + z_hi
                for part, ref in enumerate((q_ref, k_ref, v_ref)):
                    rows = slice(part * 16, part * 16 + 16)
                    if slot < 3:
                        out_ref[place, rows, :] = ref[:, head * 128 : head * 128 + 128]
                    else:
                        out_ref[place, rows, :] = jnp.zeros((16, 128), BF)
                out_ref[place, 48:56, :] = tail


def pack(queries, keys, values, mask):
    return pl.pallas_call(
        pack_kernel,
        out_shape=jax.ShapeDtypeStruct((32, 56, 128), BF),
        name="pack",
    )(queries, keys, values, mask)


def spread_kernel(at_ref, in_ref, q_ref, kv_ref):
    mine = at_ref[4] * 4 + at_ref[3]
    for place in range(32):
        rows = slice(place * 16, place * 16 + 16)
        q_ref[rows, :] = in_ref[place, 0:16, :]
        for there in range(4):
            kv_ref[there, rows, 0:128] = in_ref[place, 16:32, :]
            kv_ref[there, rows, 128:256] = in_ref[place, 32:48, :]
    tails = [in_ref[z * 8 + mine, 48:56, :].astype(F32)[0:1] for z in range(4)]
    q_ref[512:528, :] = jnp.concatenate(tails + [jnp.zeros((12, 128), F32)], axis=0).astype(BF)


def spread(at, mine):
    return pl.pallas_call(
        spread_kernel,
        out_shape=[
            jax.ShapeDtypeStruct((528, 128), BF),
            jax.ShapeDtypeStruct((4, 512, 256), BF),
        ],
        in_specs=[
            pl.BlockSpec(memory_space=pltpu.SMEM),
            pl.BlockSpec(memory_space=pltpu.VMEM),
        ],
        name="spread",
    )(at, mine)


def attend_kernel(
    at_ref, q0, q1, q2, q3, kv_ref, out_ref, vt_ref, rows_ref, list_ref, mask_ref, sem
):
    x = at_ref[0]
    qs = (q0, q1, q2, q3)
    scale = LOG2E / 128**0.5
    for dq in range(4):
        rows_ref[dq * 8 : dq * 8 + 8, :] = qs[dq][512:528, :].astype(F32)[0:8].astype(jnp.int32)
    to_scalars = pltpu.make_async_copy(rows_ref, mask_ref, sem)
    to_scalars.start()
    for block in range(16):
        vt_ref[block] = kv_ref[block, :, 128:].T
    to_scalars.wait()

    for dq in range(4):
        xq = (x + 4 - dq) % 4
        counts = []
        for zq in range(4):
            count = jnp.int32(0)
            for block in range(16):
                list_ref[zq, count] = block
                seen = mask_ref[dq * 8 + zq, (block % 4) * 16 + 4 * x + block // 4]
                count = count + jnp.where(seen > 0, 1, 0)
            counts.append(count)
        most = jnp.maximum(jnp.maximum(counts[0], counts[1]), jnp.maximum(counts[2], counts[3]))
        queries = [qs[dq][zq * 128 : zq * 128 + 128, :] for zq in range(4)]

        def fold(step, states, queries=queries, counts=counts):
            after = []
            for zq in range(4):
                largest, total, acc = states[zq]
                blocks, pieces = [], []
                for part in range(4):
                    place = step * 4 + part
                    here = place < counts[zq]
                    block = jnp.where(here, list_ref[zq, jnp.where(here, place, 0)], 0)
                    piece = lax.dot_general(
                        kv_ref[block, :, :128],
                        queries[zq],
                        (((1,), (1,)), ((), ())),
                        preferred_element_type=F32,
                    )
                    pieces.append(piece * scale + jnp.where(here, 0.0, LOW))
                    blocks.append(block)
                scores = jnp.concatenate(pieces, axis=0)
                new = jnp.maximum(largest, jnp.max(scores, axis=0, keepdims=True))
                weights = jnp.exp2(scores - new)
                again = jnp.exp2(largest - new)
                total = total * again + jnp.sum(weights, axis=0, keepdims=True)
                turned = jnp.concatenate([vt_ref[block] for block in blocks], axis=1)
                product = jnp.dot(turned, weights.astype(BF), preferred_element_type=F32)
                after.append((new, total, acc * again + product))
            return tuple(after)

        start = (
            jnp.full((1, 128), LOW, F32),
            jnp.zeros((1, 128), F32),
            jnp.zeros((128, 128), F32),
        )
        states = lax.fori_loop(0, (most + 3) // 4, fold, (start,) * 4)
        for zq in range(4):
            largest, total, acc = states[zq]
            empty = total == 0.0
            inverse = jnp.where(empty, 0.0, 1.0 / jnp.where(empty, 1.0, total))
            o = (acc * inverse).T.astype(BF)
            lse = largest + jnp.log2(jnp.where(empty, 1.0, total))
            hi = lse.astype(BF)
            rest = lse - hi.astype(F32)
            mid = rest.astype(BF)
            lo = (rest - mid.astype(F32)).astype(BF)
            coded = jnp.concatenate(
                [hi.astype(F32), mid.astype(F32), lo.astype(F32), jnp.zeros((13, 128), F32)], axis=0
            )
            turned = jnp.concatenate([coded[:, 64:], coded[:, :64]], axis=1)
            place = (xq * 4 + zq) * 2
            out_ref[place, 0:64, :] = o[0:64]
            out_ref[place, 64:80, :] = coded.astype(BF)
            out_ref[place + 1, 0:64, :] = o[64:128]
            out_ref[place + 1, 64:80, :] = turned.astype(BF)


def attend(at, qs, kv):
    smem = pl.BlockSpec(memory_space=pltpu.SMEM)
    vmem = pl.BlockSpec(memory_space=pltpu.VMEM)
    return pl.pallas_call(
        attend_kernel,
        out_shape=jax.ShapeDtypeStruct((32, 80, 128), BF),
        in_specs=[smem] + [vmem] * 5,
        out_specs=vmem,
        scratch_shapes=[
            pltpu.VMEM((16, 128, 128), BF),
            pltpu.VMEM((32, 128), jnp.int32),
            pltpu.SMEM((4, 17), jnp.int32),
            pltpu.SMEM((32, 128), jnp.int32),
            pltpu.SemaphoreType.DMA,
        ],
        compiler_params=pltpu.CompilerParams(vmem_limit_bytes=48 * 1024 * 1024),
        cost_estimate=pl.CostEstimate(flops=1 << 30, bytes_accessed=2 << 20, transcendentals=1 << 21),
        name="attend",
    )(at, *qs, kv)


def project_kernel(at_ref, parts_ref, own_ref, other_ref, y0, y1, y2, y3, att_ref):
    z_hi, core = at_ref[3], at_ref[4]

    @pl.when(pl.program_id(0) == 0)
    def _():
        coded = [parts_ref[i, 64:80, :].astype(F32) for i in range(32)]
        lse = jnp.concatenate([c[0:1] + c[1:2] + c[2:3] for c in coded], axis=0)
        groups = [lse[8 * i : 8 * i + 8] for i in range(4)]
        top = jnp.maximum(jnp.maximum(groups[0], groups[1]), jnp.maximum(groups[2], groups[3]))
        shares = [jnp.exp2(g - top) for g in groups]
        total = shares[0] + shares[1] + shares[2] + shares[3]
        inverse = 1.0 / total
        share = jnp.concatenate([s * inverse for s in shares], axis=0)
        share = jnp.concatenate([share, jnp.zeros((96, 128), F32)], axis=0).T
        for slot in range(3):
            for there in range(2):
                summed = None
                for xk in range(4):
                    i = xk * 8 + slot * 2 + there
                    term = parts_ref[i, 0:64, :].astype(F32) * share[0:64, i : i + 1]
                    summed = term if summed is None else summed + term
                att_ref[there, :, slot * 128 : slot * 128 + 128] = summed.astype(BF)

    for d, y_ref in enumerate((y0, y1, y2, y3)):
        rows = pl.ds(pl.multiple_of(((z_hi + d) % 4) * 16, 16), 16)
        y_ref[...] = (
            jnp.dot(att_ref[core, rows, :], own_ref[...], preferred_element_type=F32)
            + jnp.dot(att_ref[1 - core, rows, :], other_ref[...], preferred_element_type=F32)
        ).astype(BF)


def project(at, parts, own, other):
    width = 768
    return pl.pallas_call(
        project_kernel,
        grid=(3072 // width,),
        out_shape=[jax.ShapeDtypeStruct((16, 3072), BF)] * 4,
        in_specs=[
            pl.BlockSpec(memory_space=pltpu.SMEM),
            pl.BlockSpec((32, 80, 128), lambda n: (0, 0, 0)),
            pl.BlockSpec((384, width), lambda n: (0, n)),
            pl.BlockSpec((384, width), lambda n: (0, n)),
        ],
        out_specs=[pl.BlockSpec((16, width), lambda n: (0, n))] * 4,
        scratch_shapes=[pltpu.VMEM((2, 64, 384), BF)],
        compiler_params=pltpu.CompilerParams(vmem_limit_bytes=32 * 1024 * 1024),
        name="project",
    )(at, parts, own, other)


def turn(array, axis, step):
    return lax.ppermute(array, axis, [(i, (i + step) % 4) for i in range(4)])


def local(queries, keys_in, values, block_mask, w_out):
    x, y, z = lax.axis_index("x"), lax.axis_index("y"), lax.axis_index("z_lo")
    z_hi, core = lax.axis_index("z_hi"), lax.axis_index("core")
    at = jnp.stack([x, y, jnp.minimum(z, 2), z_hi, core]).astype(jnp.int32)
    w_other = lax.ppermute(w_out, "core", [(0, 1), (1, 0)])
    packed = pack(queries, keys_in, values, block_mask.reshape(3, 64))
    mine = lax.all_to_all(packed, ("z_lo", "core", "z_hi"), split_axis=0, concat_axis=0, tiled=True)
    q, kv = spread(at, mine)
    qs = [q] + [turn(q, "x", d) for d in (1, 2, 3)]
    kv = lax.all_to_all(kv, "y", split_axis=0, concat_axis=0, tiled=True).reshape(16, 128, 256)
    parts = attend(at, qs, kv)
    parts = lax.all_to_all(parts, ("x", "z_lo", "core"), split_axis=0, concat_axis=0, tiled=True)
    ys = project(at, parts, w_out, w_other)
    summed = ys[0].astype(F32)
    for d in (1, 2, 3):
        summed = summed + turn(ys[d], "z_hi", d).astype(F32)
    return summed.astype(BF)


def solution(mesh):
    fine = Mesh(mesh.devices.reshape(4, 2, 4, 4, 4), AXES)
    tokens = P(("z_lo", "x", "y", "z_hi", "core"), None)
    placed = (
        tokens,
        tokens,
        tokens,
        P(("z_hi", "core"), ("z_lo", "x", "y"), None),
        P(("z_hi", "core"), None),
    )
    return jax.shard_map(local, mesh=fine, in_specs=placed, out_specs=tokens, check_vma=False)
```

time: 967 us -> 148 us (0.15)
  waiting for transfers between devices: 737 us -> 65.1 us
  local copies, waits for them, and re-layouts: 86.3 us -> 9.69 us
  starting transfers between devices: 4.82 us -> 54.9 us
  blocking collectives: 48.6 us -> 0 us
  matrix products: 37.8 us -> 0 us
  other arithmetic: 36.1 us -> 0.69 us
  Pallas kernels: 0 us -> 16.1 us
  between operations: 13.2 us -> 0.14 us
    all_gather x2 -> x0, waiting for transfers between devices: 630 us -> none  [the longest x1 353 us: local(): value_piece = lax.all_gather(value_all, 'blk', axis=0, tiled=True)]
    reduce_scatter x1 -> x0, waiting for transfers between devices: 92.7 us -> none  [local(): lax.psum_scatter(jnp.dot(attended, w_out, preferred_element_type=jnp.floa...]
    gather x8 -> x0, local copies, waits for them, and re-layouts: 63.5 us -> none  [one_part(): allowed = jnp.take(row_mask, key_blocks, axis=2) > 0]
    all_to_all x2 -> x0, blocking collectives: 48.6 us -> none  [the longest x1 29.2 us: local(): lax.all_to_all(keys_in, 'head', split_axis=1, concat_axis=0, tiled=True)]
    dot_general x17 -> x0, matrix products: 37.8 us -> none  [the longest x8 21.9 us: attend(): jnp.einsum('qhd,khd->hqk', query_heads, key_heads, preferred_element_type...]
    ppermute x0 -> x7, waiting for transfers between devices: none -> 27.4 us  [the longest x6 23.2 us: turn(): return lax.ppermute(array, axis, [(i, (i + step) % 4) for i in range(4)])]
    all_to_all x1 -> x3, starting transfers between devices: 4.77 us -> 30 us  [the longest x1 16.8 us: local(): lax.all_to_all(packed, ('z_lo', 'core', 'z_hi'), split_axis=0, concat_axi...]
    ppermute x0 -> x7, starting transfers between devices: none -> 24.9 us  [the longest x6 22.7 us: turn(): return lax.ppermute(array, axis, [(i, (i + step) % 4) for i in range(4)])]
  transfers between devices with their start and end apart: 4 -> 10, of which waited for: 4 -> 8; matrix products, arithmetic and copies ran while one was open for 1% -> 0% of each run, Pallas kernels for 0% -> 0%
where the time goes in v1:
time: 148 us; the launch traced here: 147 us
  waiting for transfers between devices  65.1 us (44%)
  starting transfers between devices  54.9 us (37%)
  Pallas kernels  16.1 us (11%)
  local copies, waits for them, and re-layouts  9.69 us (7%)
    all_to_all x1, waiting for transfers between devices, local(): lax.all_to_all(packed, ('z_lo', 'core', 'z_hi'), split_axis=0, concat_axi...  25.9 us
    ppermute x6, waiting for transfers between devices, turn(): return lax.ppermute(array, axis, [(i, (i + step) % 4) for i in range(4)])  23.2 us
    ppermute x6, starting transfers between devices, turn(): return lax.ppermute(array, axis, [(i, (i + step) % 4) for i in range(4)])  22.7 us
    all_to_all x1, starting transfers between devices, local(): lax.all_to_all(packed, ('z_lo', 'core', 'z_hi'), split_axis=0, concat_axi...  16.8 us
    all_to_all x1, waiting for transfers between devices, local(): lax.all_to_all(parts, ('x', 'z_lo', 'core'), split_axis=0, concat_axis=0,...  11.7 us
    unnamed x19, local copies, waits for them, and re-layouts  9.12 us
    all_to_all x1, starting transfers between devices, local(): lax.all_to_all(parts, ('x', 'z_lo', 'core'), split_axis=0, concat_axis=0,...  9.11 us
    pallas_call x1, Pallas kernels, attend(): pl.pallas_call(attend_kernel, out_shape=jax.ShapeDtypeStruct((32, 80, 128...  7.82 us
  transfers between devices with their start and end apart: 10, of which 8 were waited for; matrix products, arithmetic and copies ran while one was open for 0% of the time, Pallas kernels for 0%

profile of v1, /device:TPU:1, one launch (start us, length us, event | category | flops | bytes accessed | tf_op | source)
XLA Modules:
  0.0 146.7 jit_solution(4435208903722258916)
XLA Ops:
  1.3 1.8 %pack.1 = bf16[32,56,128]{2,1,0:T(8,128)(2,1)} custom-call(bf16[16,3072]{1,0:T(8,128)(2,1)} %q_ref.1, bf16[16,3072]{1,0:T(8,128)(2,1)} %k_ref.1, bf16[16,3072]{1,0:T(8,128)(2,1)} %v_ref.1, s32[3,64]{1,0:T(4,128)} %bitcast.10), custom_call_target="tpu_custom_call" | custom-call | tf_op jit(solution)/shard_map/pack/pallas_call | solution.py:36
  3.1 16.8 %all-to-all-start = ((bf16[32,56,128]{2,1,0:T(8,128)(2,1)}), bf16[32,56,128]{2,1,0:T(8,128)(2,1)S(1)}, u32[]{:S(2)}, u32[]{:S(2)}) async-start(bf16[32,56,128]{2,1,0:T(8,128)(2,1)} %pack.1), calls=%async_computation | async-start | bytes 917504 | tf_op jit(solution)/shard_map/all_to_all | solution.py:232
  20.4 25.9 %all-to-all-done.in_ref = bf16[32,56,128]{2,1,0:T(8,128)(2,1)S(1)} async-done(((bf16[32,56,128]{2,1,0:T(8,128)(2,1)}), bf16[32,56,128]{2,1,0:T(8,128)(2,1)S(1)}, u32[]{:S(2)}, u32[]{:S(2)}) %all-to-all-start) | async-done | bytes 458784 | tf_op jit(solution)/shard_map/all_to_all | solution.py:232
  47.1 2.2 %spread.1 = (bf16[528,128]{1,0:T(8,128)(2,1)}, bf16[4,512,256]{2,1,0:T(8,128)(2,1)}) custom-call(s32[5]{0:T(128)} %stack.23.at_ref, bf16[32,56,128]{2,1,0:T(8,128)(2,1)} %copy-done.8), custom_call_target="tpu_custom_call" | custom-call | tf_op jit(solution)/shard_map/spread/pallas_call | solution.py:56
  49.4 4.2 %all-to-all-start.1 = ((bf16[4,512,256]{2,1,0:T(8,128)(2,1)}), bf16[4,512,256]{2,1,0:T(8,128)(2,1)S(1)}, u32[]{:S(2)}, u32[]{:S(2)}) async-start(bf16[4,512,256]{2,1,0:T(8,128)(2,1)} %get-tuple-element.12), calls=%async_computation.1 | async-start | bytes 2097152 | tf_op jit(solution)/shard_map/all_to_all | solution.py:235
  53.5 4.4 %collective-permute-start.2 = (bf16[528,128]{1,0:T(8,128)(2,1)}, bf16[528,128]{1,0:T(8,128)(2,1)S(1)}, u32[]{:S(2)}, u32[]{:S(2)}) collective-permute-start(bf16[528,128]{1,0:T(8,128)(2,1)} %get-tuple-element.11.q0), channel_id=1, source_target_pairs={{0,12},{4,0},{8,4},{12,8},{1,13},{5,1},{9,5},{13,9},{2,14},{6,2},{... | collective-permute-start | bytes 405512 | tf_op jit(solution)/shard_map/ppermute | solution.py:223
  57.9 2.4 %collective-permute-start.1 = (bf16[528,128]{1,0:T(8,128)(2,1)}, bf16[528,128]{1,0:T(8,128)(2,1)S(1)}, u32[]{:S(2)}, u32[]{:S(2)}) collective-permute-start(bf16[528,128]{1,0:T(8,128)(2,1)} %get-tuple-element.11.q0), channel_id=1, source_target_pairs={{0,8},{4,12},{8,0},{12,4},{1,9},{5,13},{9,1},{13,5},{2,10},{6,14},... | collective-permute-start | bytes 405512 | tf_op jit(solution)/shard_map/ppermute | solution.py:223
  60.4 2.5 %collective-permute-start = (bf16[528,128]{1,0:T(8,128)(2,1)}, bf16[528,128]{1,0:T(8,128)(2,1)S(1)}, u32[]{:S(2)}, u32[]{:S(2)}) collective-permute-start(bf16[528,128]{1,0:T(8,128)(2,1)} %get-tuple-element.11.q0), channel_id=1, source_target_pairs={{0,4},{4,8},{8,12},{12,0},{1,5},{5,9},{9,13},{13,1},{2,6},{6,10},{... | collective-permute-start | bytes 405512 | tf_op jit(solution)/shard_map/ppermute | solution.py:223
  62.9 2.8 %collective-permute-done.1.q2 = bf16[528,128]{1,0:T(8,128)(2,1)S(1)} collective-permute-done((bf16[528,128]{1,0:T(8,128)(2,1)}, bf16[528,128]{1,0:T(8,128)(2,1)S(1)}, u32[]{:S(2)}, u32[]{:S(2)}) %collective-permute-start.1) | collective-permute-done | bytes 135200 | tf_op jit(solution)/shard_map/ppermute | solution.py:223
  65.7 3.6 %collective-permute-done.q1 = bf16[528,128]{1,0:T(8,128)(2,1)S(1)} collective-permute-done((bf16[528,128]{1,0:T(8,128)(2,1)}, bf16[528,128]{1,0:T(8,128)(2,1)S(1)}, u32[]{:S(2)}, u32[]{:S(2)}) %collective-permute-start) | collective-permute-done | bytes 135200 | tf_op jit(solution)/shard_map/ppermute | solution.py:223
  72.4 7.8 %attend.1 = bf16[32,80,128]{2,1,0:T(8,128)(2,1)S(1)} custom-call(s32[5]{0:T(128)S(1)} %copy-done.6, bf16[528,128]{1,0:T(8,128)(2,1)S(1)} %copy-done.7, bf16[528,128]{1,0:T(8,128)(2,1)S(1)} %collective-permute-done.q1, bf16[528,128]{1,0:T(8,128)(2,1)S(1)} %collective-permute-done.1.q2, bf16[528,128]{1,0:T(8,128)(2,1)S(1)} %collective-permute-done.2.q3, ...), custom_call_target="tpu_custom_call" | custom-call | flops 1073741824 | bytes 2097152 | tf_op jit(solution)/shard_map/attend/pallas_call | solution.py:154
  81.1 9.1 %all-to-all-start.2 = ((bf16[32,80,128]{2,1,0:T(8,128)(2,1)}), bf16[32,80,128]{2,1,0:T(8,128)(2,1)S(1)}, u32[]{:S(2)}, u32[]{:S(2)}) async-start(bf16[32,80,128]{2,1,0:T(8,128)(2,1)} %copy-done.5), calls=%async_computation.2 | async-start | bytes 1310720 | tf_op jit(solution)/shard_map/all_to_all | solution.py:237
  90.2 2.1 %collective-permute-start.3 = (bf16[384,3072]{1,0:T(8,128)(2,1)S(1)}, bf16[384,3072]{1,0:T(8,128)(2,1)S(1)}, u32[]{:S(2)}, u32[]{:S(2)}) collective-permute-start(bf16[384,3072]{1,0:T(8,128)(2,1)S(1)} %copy-done), channel_id=1, source_target_pairs={{0,64},{64,0},{1,65},{65,1},{2,66},{66,2},{3,67},{67,3},{4,68},{68... | collective-permute-start | bytes 7077896 | tf_op jit(solution)/shard_map/ppermute | solution.py:230
  92.4 4.3 %collective-permute-done.3.other_ref = bf16[384,3072]{1,0:T(8,128)(2,1)S(1)} collective-permute-done((bf16[384,3072]{1,0:T(8,128)(2,1)S(1)}, bf16[384,3072]{1,0:T(8,128)(2,1)S(1)}, u32[]{:S(2)}, u32[]{:S(2)}) %collective-permute-start.3) | collective-permute-done | bytes 2359328 | tf_op jit(solution)/shard_map/ppermute | solution.py:230
  96.6 1.4 copy-done.1
  98.1 11.7 %all-to-all-done.2.parts_ref = bf16[32,80,128]{2,1,0:T(8,128)(2,1)S(1)} async-done(((bf16[32,80,128]{2,1,0:T(8,128)(2,1)}), bf16[32,80,128]{2,1,0:T(8,128)(2,1)S(1)}, u32[]{:S(2)}, u32[]{:S(2)}) %all-to-all-start.2) | async-done | bytes 655392 | tf_op jit(solution)/shard_map/all_to_all | solution.py:237
  109.8 1.7 %copy-done.2 = bf16[384,3072]{1,0:T(8,128)(2,1)S(1)} copy-done((bf16[384,3072]{1,0:T(8,128)(2,1)S(1)}, bf16[384,3072]{1,0:T(8,128)(2,1)}, u32[]{:S(2)}) %copy-start.2) | copy-done | bytes 2359320
  111.4 4.3 %project.1 = (bf16[16,3072]{1,0:T(8,128)(2,1)S(1)}, bf16[16,3072]{1,0:T(8,128)(2,1)S(1)}, bf16[16,3072]{1,0:T(8,128)(2,1)S(1)}, bf16[16,3072]{1,0:T(8,128)(2,1)S(1)}) custom-call(s32[5]{0:T(128)S(1)} %copy-done.6, bf16[32,80,128]{2,1,0:T(8,128)(2,1)S(1)} %all-to-all-done.2.parts_ref, bf16[384,3072]{1,0:T(8,128)(2,1)S(1)} %copy-done, ...), custom_call_target="tpu_custom_call" | custom-call | tf_op jit(solution)/shard_map/project/pallas_call | solution.py:205
  115.7 3.5 %collective-permute-start.4 = (bf16[16,3072]{1,0:T(8,128)(2,1)S(1)}, bf16[16,3072]{1,0:T(8,128)(2,1)S(1)}, u32[]{:S(2)}, u32[]{:S(2)}) collective-permute-start(bf16[16,3072]{1,0:T(8,128)(2,1)S(1)} %get-tuple-element.14), channel_id=1, source_target_pairs={{0,128},{128,256},{256,384},{384,0},{1,129},{129,257},{257,385},{3... | collective-permute-start | bytes 294920 | tf_op jit(solution)/shard_map/ppermute | solution.py:223
  119.3 6.9 %collective-permute-start.5 = (bf16[16,3072]{1,0:T(8,128)(2,1)S(1)}, bf16[16,3072]{1,0:T(8,128)(2,1)S(1)}, u32[]{:S(2)}, u32[]{:S(2)}) collective-permute-start(bf16[16,3072]{1,0:T(8,128)(2,1)S(1)} %get-tuple-element.15), channel_id=1, source_target_pairs={{0,256},{128,384},{256,0},{384,128},{1,257},{129,385},{257,1},{385... | collective-permute-start | bytes 294920 | tf_op jit(solution)/shard_map/ppermute | solution.py:223
  126.2 2.9 %collective-permute-start.6 = (bf16[16,3072]{1,0:T(8,128)(2,1)S(1)}, bf16[16,3072]{1,0:T(8,128)(2,1)S(1)}, u32[]{:S(2)}, u32[]{:S(2)}) collective-permute-start(bf16[16,3072]{1,0:T(8,128)(2,1)S(1)} %get-tuple-element.16), channel_id=1, source_target_pairs={{0,384},{128,0},{256,128},{384,256},{1,385},{129,1},{257,129},{385... | collective-permute-start | bytes 294920 | tf_op jit(solution)/shard_map/ppermute | solution.py:223
  129.2 1.7 %collective-permute-done.4 = bf16[16,3072]{1,0:T(8,128)(2,1)S(1)} collective-permute-done((bf16[16,3072]{1,0:T(8,128)(2,1)S(1)}, bf16[16,3072]{1,0:T(8,128)(2,1)S(1)}, u32[]{:S(2)}, u32[]{:S(2)}) %collective-permute-start.4) | collective-permute-done | bytes 98336 | tf_op jit(solution)/shard_map/ppermute | solution.py:223
  130.9 2.9 %collective-permute-done.5 = bf16[16,3072]{1,0:T(8,128)(2,1)S(1)} collective-permute-done((bf16[16,3072]{1,0:T(8,128)(2,1)S(1)}, bf16[16,3072]{1,0:T(8,128)(2,1)S(1)}, u32[]{:S(2)}, u32[]{:S(2)}) %collective-permute-start.5) | collective-permute-done | bytes 98336 | tf_op jit(solution)/shard_map/ppermute | solution.py:223
  133.8 12.2 %collective-permute-done.6 = bf16[16,3072]{1,0:T(8,128)(2,1)S(1)} collective-permute-done((bf16[16,3072]{1,0:T(8,128)(2,1)S(1)}, bf16[16,3072]{1,0:T(8,128)(2,1)S(1)}, u32[]{:S(2)}, u32[]{:S(2)}) %collective-permute-start.6) | collective-permute-done | bytes 98336 | tf_op jit(solution)/shard_map/ppermute | solution.py:223
  (21 shorter events, 7.3 us)
Async XLA Ops:
  3.1 43.3 %all-to-all-start = ((bf16[32,56,128]{2,1,0:T(8,128)(2,1)}), bf16[32,56,128]{2,1,0:T(8,128)(2,1)S(1)}, u32[]{:S(2)}, u32[]{:S(2)}) async-start(bf16[32,56,128]{2,1,0:T(8,128)(2,1)} %pack.1), calls=%async_computation | async-start | bytes 917504 | tf_op jit(solution)/shard_map/all_to_all | solution.py:232
  20.4 49.8 %copy-start.6 = (s32[5]{0:T(128)S(1)}, s32[5]{0:T(128)}, u32[]{:S(2)}) copy-start(s32[5]{0:T(128)} %stack.23.at_ref) | copy-start | bytes 64
  46.4 0.8 copy-start.8
  49.4 19.9 %all-to-all-start.1 = ((bf16[4,512,256]{2,1,0:T(8,128)(2,1)}), bf16[4,512,256]{2,1,0:T(8,128)(2,1)S(1)}, u32[]{:S(2)}, u32[]{:S(2)}) async-start(bf16[4,512,256]{2,1,0:T(8,128)(2,1)} %get-tuple-element.12), calls=%async_computation.1 | async-start | bytes 2097152 | tf_op jit(solution)/shard_map/all_to_all | solution.py:235
  53.5 9.3 %collective-permute-start.2 = (bf16[528,128]{1,0:T(8,128)(2,1)}, bf16[528,128]{1,0:T(8,128)(2,1)S(1)}, u32[]{:S(2)}, u32[]{:S(2)}) collective-permute-start(bf16[528,128]{1,0:T(8,128)(2,1)} %get-tuple-element.11.q0), channel_id=1, source_target_pairs={{0,12},{4,0},{8,4},{12,8},{1,13},{5,1},{9,5},{13,9},{2,14},{6,2},{... | collective-permute-start | bytes 405512 | tf_op jit(solution)/shard_map/ppermute | solution.py:223
  57.9 7.8 %collective-permute-start.1 = (bf16[528,128]{1,0:T(8,128)(2,1)}, bf16[528,128]{1,0:T(8,128)(2,1)S(1)}, u32[]{:S(2)}, u32[]{:S(2)}) collective-permute-start(bf16[528,128]{1,0:T(8,128)(2,1)} %get-tuple-element.11.q0), channel_id=1, source_target_pairs={{0,8},{4,12},{8,0},{12,4},{1,9},{5,13},{9,1},{13,5},{2,10},{6,14},... | collective-permute-start | bytes 405512 | tf_op jit(solution)/shard_map/ppermute | solution.py:223
  60.4 8.9 %collective-permute-start = (bf16[528,128]{1,0:T(8,128)(2,1)}, bf16[528,128]{1,0:T(8,128)(2,1)S(1)}, u32[]{:S(2)}, u32[]{:S(2)}) collective-permute-start(bf16[528,128]{1,0:T(8,128)(2,1)} %get-tuple-element.11.q0), channel_id=1, source_target_pairs={{0,4},{4,8},{8,12},{12,0},{1,5},{5,9},{9,13},{13,1},{2,6},{6,10},{... | collective-permute-start | bytes 405512 | tf_op jit(solution)/shard_map/ppermute | solution.py:223
  69.3 1.0 copy-start.3
  70.3 1.2 copy-start.4
  71.5 0.9 copy-start.7
  72.4 17.8 %copy-start = (bf16[384,3072]{1,0:T(8,128)(2,1)S(1)}, bf16[384,3072]{1,0:T(8,128)(2,1)}, u32[]{:S(2)}) copy-start(bf16[384,3072]{1,0:T(8,128)(2,1)} %own_ref.1) | copy-start | bytes 7077892
  80.2 0.9 copy-start.5
  81.1 28.7 %all-to-all-start.2 = ((bf16[32,80,128]{2,1,0:T(8,128)(2,1)}), bf16[32,80,128]{2,1,0:T(8,128)(2,1)S(1)}, u32[]{:S(2)}, u32[]{:S(2)}) async-start(bf16[32,80,128]{2,1,0:T(8,128)(2,1)} %copy-done.5), calls=%async_computation.2 | async-start | bytes 1310720 | tf_op jit(solution)/shard_map/all_to_all | solution.py:237
  90.2 6.4 %collective-permute-start.3 = (bf16[384,3072]{1,0:T(8,128)(2,1)S(1)}, bf16[384,3072]{1,0:T(8,128)(2,1)S(1)}, u32[]{:S(2)}, u32[]{:S(2)}) collective-permute-start(bf16[384,3072]{1,0:T(8,128)(2,1)S(1)} %copy-done), channel_id=1, source_target_pairs={{0,64},{64,0},{1,65},{65,1},{2,66},{66,2},{3,67},{67,3},{4,68},{68... | collective-permute-start | bytes 7077896 | tf_op jit(solution)/shard_map/ppermute | solution.py:230
  96.6 1.4 copy-start.1
  109.8 1.7 %copy-start.2 = (bf16[384,3072]{1,0:T(8,128)(2,1)S(1)}, bf16[384,3072]{1,0:T(8,128)(2,1)}, u32[]{:S(2)}) copy-start(bf16[384,3072]{1,0:T(8,128)(2,1)} %copy-done.1) | copy-start | bytes 7077892
  115.7 15.1 %collective-permute-start.4 = (bf16[16,3072]{1,0:T(8,128)(2,1)S(1)}, bf16[16,3072]{1,0:T(8,128)(2,1)S(1)}, u32[]{:S(2)}, u32[]{:S(2)}) collective-permute-start(bf16[16,3072]{1,0:T(8,128)(2,1)S(1)} %get-tuple-element.14), channel_id=1, source_target_pairs={{0,128},{128,256},{256,384},{384,0},{1,129},{129,257},{257,385},{3... | collective-permute-start | bytes 294920 | tf_op jit(solution)/shard_map/ppermute | solution.py:223
  119.3 14.5 %collective-permute-start.5 = (bf16[16,3072]{1,0:T(8,128)(2,1)S(1)}, bf16[16,3072]{1,0:T(8,128)(2,1)S(1)}, u32[]{:S(2)}, u32[]{:S(2)}) collective-permute-start(bf16[16,3072]{1,0:T(8,128)(2,1)S(1)} %get-tuple-element.15), channel_id=1, source_target_pairs={{0,256},{128,384},{256,0},{384,128},{1,257},{129,385},{257,1},{385... | collective-permute-start | bytes 294920 | tf_op jit(solution)/shard_map/ppermute | solution.py:223
  126.2 19.7 %collective-permute-start.6 = (bf16[16,3072]{1,0:T(8,128)(2,1)S(1)}, bf16[16,3072]{1,0:T(8,128)(2,1)S(1)}, u32[]{:S(2)}, u32[]{:S(2)}) collective-permute-start(bf16[16,3072]{1,0:T(8,128)(2,1)S(1)} %get-tuple-element.16), channel_id=1, source_target_pairs={{0,384},{128,0},{256,128},{384,256},{1,385},{129,1},{257,129},{385... | collective-permute-start | bytes 294920 | tf_op jit(solution)/shard_map/ppermute | solution.py:223

commit v2 on v1

v2 whole, which is shorter than its diff:
```python
import jax
import jax.numpy as jnp
from jax import lax
from jax.experimental import pallas as pl
from jax.experimental.pallas import tpu as pltpu
from jax.sharding import Mesh, PartitionSpec as P

BF = jnp.bfloat16
F32 = jnp.float32
AXES = ("z_hi", "core", "z_lo", "x", "y")
LOW = -1e30
LOG2E = 1.4426950408889634
ROWS = 72


def pack_kernel(q_ref, k_ref, v_ref, out_ref):
    for slot in range(4):
        for core in range(2):
            for z_hi in range(4):
                head = 3 * (2 * z_hi + core) + slot
                place = slot * 8 + core * 4 + z_hi
                for part, ref in enumerate((q_ref, k_ref, v_ref)):
                    rows = slice(part * 16, part * 16 + 16)
                    if slot < 3:
                        out_ref[place, rows, :] = ref[:, head * 128 : head * 128 + 128]
                    else:
                        out_ref[place, rows, :] = jnp.zeros((16, 128), BF)


def pack(queries, keys, values):
    return pl.pallas_call(
        pack_kernel,
        out_shape=jax.ShapeDtypeStruct((32, 48, 128), BF),
        name="pack",
    )(queries, keys, values)


def spread_kernel(at_ref, m0, m1, m2, m3, in_ref, q_ref, kv_ref, held, tail, sems):
    into = pltpu.make_async_copy(in_ref, held, sems.at[0])
    into.start()
    slot, z = at_ref[2], at_ref[5]
    row = lax.broadcasted_iota(jnp.int32, (16, 64), 0)
    total = jnp.zeros((16, 64), F32)
    for d, ref in enumerate((m0, m1, m2, m3)):
        seen = ref[slot].astype(F32)
        total = total + jnp.where(row == (z + 4 - d) % 4, seen, 0.0)
    tail[...] = jnp.concatenate([total, jnp.zeros((16, 64), F32)], axis=1).astype(BF)
    into.wait()
    copies = [
        pltpu.make_async_copy(held.at[:, 16:48], kv_ref.at[there], sems.at[there])
        for there in range(4)
    ]
    copies.append(pltpu.make_async_copy(held.at[:, 0:16], q_ref.at[0:32], sems.at[4]))
    copies.append(pltpu.make_async_copy(tail, q_ref.at[32], sems.at[5]))
    for copy in copies:
        copy.start()
    for copy in copies:
        copy.wait()


def spread(at, masks, mine):
    smem = pl.BlockSpec(memory_space=pltpu.SMEM)
    vmem = pl.BlockSpec(memory_space=pltpu.VMEM)
    anywhere = pl.BlockSpec(memory_space=pl.ANY)
    return pl.pallas_call(
        spread_kernel,
        out_shape=[
            jax.ShapeDtypeStruct((33, 16, 128), BF),
            jax.ShapeDtypeStruct((4, 32, 32, 128), BF),
        ],
        in_specs=[smem, vmem, vmem, vmem, vmem, anywhere],
        out_specs=[anywhere, anywhere],
        scratch_shapes=[
            pltpu.VMEM((32, 48, 128), BF),
            pltpu.VMEM((16, 128), BF),
            pltpu.SemaphoreType.DMA((6,)),
        ],
        compiler_params=pltpu.CompilerParams(vmem_limit_bytes=56 * 1024 * 1024),
        name="spread",
    )(at, *masks, mine)


def attend_kernel(
    at_ref, q0, q1, q2, q3, kv_in, out_ref,
    q_ref, kv_ref, vt_ref, rows_ref, held, list_ref, mask_ref, sems,
):
    x = at_ref[0]
    scale = LOG2E / 128**0.5
    to_q = [pltpu.make_async_copy(q, q_ref.at[d], sems.at[d]) for d, q in enumerate((q0, q1, q2, q3))]
    to_kv = [pltpu.make_async_copy(kv_in.at[d], kv_ref.at[d], sems.at[4 + d]) for d in range(4)]
    for copy in to_q + to_kv:
        copy.start()
    for dq in range(4):
        to_q[dq].wait()
        rows_ref[dq * 8 : dq * 8 + 8, :] = q_ref[dq, 32].astype(F32)[0:8].astype(jnp.int32)
    to_scalars = pltpu.make_async_copy(rows_ref, mask_ref, sems.at[8])
    to_scalars.start()
    for yk in range(4):
        to_kv[yk].wait()
        for zk in range(4):
            value = kv_ref[yk, zk * 8 : zk * 8 + 8, 16:32, :].reshape(128, 128)
            vt_ref[yk * 4 + zk] = value.T
    to_scalars.wait()

    outs = []
    for dq in range(4):
        xq = (x + 4 - dq) % 4
        counts = []
        for zq in range(4):
            count = jnp.int32(0)
            for block in range(16):
                list_ref[zq, count] = block
                seen = mask_ref[dq * 8 + zq, (block % 4) * 16 + 4 * x + block // 4]
                count = count + jnp.where(seen > 0, 1, 0)
            counts.append(count)
        most = jnp.maximum(jnp.maximum(counts[0], counts[1]), jnp.maximum(counts[2], counts[3]))
        queries = [
            q_ref[dq, zq * 8 : zq * 8 + 8].reshape(128, 128).T for zq in range(4)
        ]

        def fold(step, states, queries=queries, counts=counts):
            after = []
            for zq in range(4):
                largest, total, acc = states[zq]
                keys, turned, biases = [], [], []
                for part in range(4):
                    place = step * 4 + part
                    here = place < counts[zq]
                    block = jnp.where(here, list_ref[zq, jnp.where(here, place, 0)], 0)
                    cut = pl.ds(pl.multiple_of((block % 4) * 8, 8), 8)
                    keys.append(kv_ref[block // 4, cut, 0:16, :].reshape(128, 128))
                    turned.append(vt_ref[block])
                    biases.append(jnp.where(here, 0.0, LOW))
                raw = jnp.dot(
                    jnp.concatenate(keys, axis=0), queries[zq], preferred_element_type=F32
                )
                scores = jnp.concatenate(
                    [raw[i * 128 : i * 128 + 128] * scale + biases[i] for i in range(4)], axis=0
                )
                new = jnp.maximum(largest, jnp.max(scores, axis=0, keepdims=True))
                weights = jnp.exp2(scores - new)
                again = jnp.exp2(largest - new)
                total = total * again + jnp.sum(weights, axis=0, keepdims=True)
                product = jnp.dot(
                    jnp.concatenate(turned, axis=1),
                    weights.astype(BF),
                    preferred_element_type=F32,
                )
                after.append((new, total, acc * again + product))
            return tuple(after)

        start = (
            jnp.full((1, 128), LOW, F32),
            jnp.zeros((1, 128), F32),
            jnp.zeros((128, 128), F32),
        )
        states = lax.fori_loop(0, (most + 3) // 4, fold, (start,) * 4)
        for zq in range(4):
            largest, total, acc = states[zq]
            empty = total == 0.0
            inverse = jnp.where(empty, 0.0, 1.0 / jnp.where(empty, 1.0, total))
            o = (acc * inverse).T.astype(BF)
            lse = largest + jnp.log2(jnp.where(empty, 1.0, total))
            hi = lse.astype(BF)
            rest = lse - hi.astype(F32)
            mid = rest.astype(BF)
            lo = (rest - mid.astype(F32)).astype(BF)
            coded = jnp.concatenate(
                [hi.astype(F32), mid.astype(F32), lo.astype(F32), jnp.zeros((5, 128), F32)], axis=0
            )
            other = jnp.concatenate([coded[:, 64:], coded[:, :64]], axis=1)
            held[dq, zq * 2, 0:64, :] = o[0:64]
            held[dq, zq * 2, 64:72, :] = coded.astype(BF)
            held[dq, zq * 2 + 1, 0:64, :] = o[64:128]
            held[dq, zq * 2 + 1, 64:72, :] = other.astype(BF)
        out = pltpu.make_async_copy(held.at[dq], out_ref.at[xq], sems.at[9 + dq])
        out.start()
        outs.append(out)
    for out in outs:
        out.wait()


def attend(at, qs, kv):
    smem = pl.BlockSpec(memory_space=pltpu.SMEM)
    anywhere = pl.BlockSpec(memory_space=pl.ANY)
    return pl.pallas_call(
        attend_kernel,
        out_shape=jax.ShapeDtypeStruct((4, 8, ROWS, 128), BF),
        in_specs=[smem] + [anywhere] * 5,
        out_specs=anywhere,
        scratch_shapes=[
            pltpu.VMEM((4, 33, 16, 128), BF),
            pltpu.VMEM((4, 32, 32, 128), BF),
            pltpu.VMEM((16, 128, 128), BF),
            pltpu.VMEM((32, 128), jnp.int32),
            pltpu.VMEM((4, 8, ROWS, 128), BF),
            pltpu.SMEM((4, 17), jnp.int32),
            pltpu.SMEM((32, 128), jnp.int32),
            pltpu.SemaphoreType.DMA((13,)),
        ],
        compiler_params=pltpu.CompilerParams(vmem_limit_bytes=56 * 1024 * 1024),
        cost_estimate=pl.CostEstimate(flops=1 << 30, bytes_accessed=2 << 20, transcendentals=1 << 21),
        name="attend",
    )(at, *qs, kv)


def project_kernel(at_ref, parts_in, own_ref, other_ref, y0, y1, y2, y3, parts_ref, att_ref, sem):
    into = pltpu.make_async_copy(parts_in, parts_ref, sem)
    into.start()
    z_hi, core = at_ref[3], at_ref[4]
    into.wait()
    coded = [parts_ref[i // 8, i % 8, 64:72, :].astype(F32) for i in range(32)]
    lse = jnp.concatenate([c[0:1] + c[1:2] + c[2:3] for c in coded], axis=0)
    groups = [lse[8 * i : 8 * i + 8] for i in range(4)]
    top = jnp.maximum(jnp.maximum(groups[0], groups[1]), jnp.maximum(groups[2], groups[3]))
    shares = [jnp.exp2(g - top) for g in groups]
    inverse = 1.0 / (shares[0] + shares[1] + shares[2] + shares[3])
    share = jnp.concatenate([s * inverse for s in shares], axis=0)
    share = jnp.concatenate([share, jnp.zeros((96, 128), F32)], axis=0).T
    for slot in range(3):
        for there in range(2):
            summed = None
            for xk in range(4):
                i = slot * 2 + there
                term = parts_ref[xk, i, 0:64, :].astype(F32) * share[0:64, xk * 8 + i : xk * 8 + i + 1]
                summed = term if summed is None else summed + term
            att_ref[there, :, slot * 128 : slot * 128 + 128] = summed.astype(BF)

    rows = [pl.ds(pl.multiple_of(((z_hi + d) % 4) * 16, 16), 16) for d in range(4)]
    own = jnp.concatenate([att_ref[core, r, :] for r in rows], axis=0)
    other = jnp.concatenate([att_ref[1 - core, r, :] for r in rows], axis=0)
    for cut in range(0, 3072, 512):
        columns = slice(cut, cut + 512)
        y = jnp.dot(own, own_ref[:, columns], preferred_element_type=F32)
        y = (y + jnp.dot(other, other_ref[:, columns], preferred_element_type=F32)).astype(BF)
        for d, y_ref in enumerate((y0, y1, y2, y3)):
            y_ref[:, columns] = y[d * 16 : d * 16 + 16]


def project(at, parts, own, other):
    vmem = pl.BlockSpec(memory_space=pltpu.VMEM)
    return pl.pallas_call(
        project_kernel,
        out_shape=[jax.ShapeDtypeStruct((16, 3072), BF)] * 4,
        in_specs=[
            pl.BlockSpec(memory_space=pltpu.SMEM),
            pl.BlockSpec(memory_space=pl.ANY),
            vmem,
            vmem,
        ],
        scratch_shapes=[
            pltpu.VMEM((4, 8, ROWS, 128), BF),
            pltpu.VMEM((2, 64, 384), BF),
            pltpu.SemaphoreType.DMA,
        ],
        compiler_params=pltpu.CompilerParams(vmem_limit_bytes=32 * 1024 * 1024),
        name="project",
    )(at, parts, own, other)


def turn(array, axis, step):
    return lax.ppermute(array, axis, [(i, (i + step) % 4) for i in range(4)])


def local(queries, keys_in, values, block_mask, w_out):
    x, y, z = lax.axis_index("x"), lax.axis_index("y"), lax.axis_index("z_lo")
    z_hi, core = lax.axis_index("z_hi"), lax.axis_index("core")
    at = jnp.stack([x, y, jnp.minimum(z, 2), z_hi, core, z]).astype(jnp.int32)
    w_other = lax.ppermute(w_out, "core", [(0, 1), (1, 0)])
    masks = [block_mask] + [turn(block_mask, "z_lo", d) for d in (1, 2, 3)]
    packed = pack(queries, keys_in, values)
    mine = lax.all_to_all(packed, ("z_lo", "core", "z_hi"), split_axis=0, concat_axis=0, tiled=True)
    q, kv = spread(at, masks, mine)
    qs = [q] + [turn(q, "x", d) for d in (1, 2, 3)]
    kv = lax.all_to_all(kv, "y", split_axis=0, concat_axis=0, tiled=True)
    parts = attend(at, qs, kv).reshape(32, ROWS, 128)
    parts = lax.all_to_all(parts, ("x", "z_lo", "core"), split_axis=0, concat_axis=0, tiled=True)
    ys = project(at, parts.reshape(4, 8, ROWS, 128), w_out, w_other)
    summed = ys[0].astype(F32)
    for d in (1, 2, 3):
        summed = summed + turn(ys[d], "z_hi", d).astype(F32)
    return summed.astype(BF)


def solution(mesh):
    fine = Mesh(mesh.devices.reshape(4, 2, 4, 4, 4), AXES)
    tokens = P(("z_lo", "x", "y", "z_hi", "core"), None)
    placed = (
        tokens,
        tokens,
        tokens,
        P(("z_hi", "core"), ("z_lo", "x", "y"), None),
        P(("z_hi", "core"), None),
    )
    return jax.shard_map(local, mesh=fine, in_specs=placed, out_specs=tokens, check_vma=False)
```

time: 148 us -> 137 us (0.926)
  waiting for transfers between devices: 65.1 us -> 46.1 us
  starting transfers between devices: 54.9 us -> 67.7 us
  local copies, waits for them, and re-layouts: 9.69 us -> 3.04 us
  Pallas kernels: 16.1 us -> 18.1 us
    all_to_all x1, waiting for transfers between devices: 25.9 us -> 6.74 us  [local(): lax.all_to_all(packed, ('z_lo', 'core', 'z_hi'), split_axis=0, concat_axi...]
    ppermute x6 -> x9, starting transfers between devices: 22.7 us -> 38.1 us  [turn(): return lax.ppermute(array, axis, [(i, (i + step) % 4) for i in range(4)])]
    unnamed x19 -> x18, local copies, waits for them, and re-layouts: 9.12 us -> 2.45 us
    all_to_all x1, waiting for transfers between devices: 11.7 us -> 18.3 us  [local(): lax.all_to_all(parts, ('x', 'z_lo', 'core'), split_axis=0, concat_axis=0,...]
    ppermute x1, waiting for transfers between devices: 4.28 us -> 0.01 us  [local(): w_other = lax.ppermute(w_out, 'core', [(0, 1), (1, 0)])]
    all_to_all x1, starting transfers between devices: 9.11 us -> 4.98 us  [local(): lax.all_to_all(parts, ('x', 'z_lo', 'core'), split_axis=0, concat_axis=0,...]
    ppermute x6 -> x9, waiting for transfers between devices: 23.2 us -> 21.1 us  [turn(): return lax.ppermute(array, axis, [(i, (i + step) % 4) for i in range(4)])]
    pallas_call x4, Pallas kernels: 16.1 us -> 18.1 us  [the longest x1 10.1 us: attend(): pl.pallas_call(attend_kernel, out_shape=jax.ShapeDtypeStruct((4, 8, ROWS,...]
  transfers between devices with their start and end apart: 10 -> 13, of which waited for: 8 -> 7; matrix products, arithmetic and copies ran while one was open for 0% -> 0% of each run, Pallas kernels for 0% -> 7%
where the time goes in v2:
time: 137 us; the launch traced here: 136 us
  starting transfers between devices  67.7 us (49%)
  waiting for transfers between devices  46.1 us (34%)
  Pallas kernels  18.1 us (13%)
  local copies, waits for them, and re-layouts  3.04 us (2%)
    ppermute x9, starting transfers between devices, turn(): return lax.ppermute(array, axis, [(i, (i + step) % 4) for i in range(4)])  38.1 us
    ppermute x9, waiting for transfers between devices, turn(): return lax.ppermute(array, axis, [(i, (i + step) % 4) for i in range(4)])  21.1 us
    all_to_all x1, waiting for transfers between devices, local(): lax.all_to_all(parts, ('x', 'z_lo', 'core'), split_axis=0, concat_axis=0,...  18.3 us
    all_to_all x1, starting transfers between devices, local(): lax.all_to_all(packed, ('z_lo', 'core', 'z_hi'), split_axis=0, concat_axi...  16.8 us
    pallas_call x1, Pallas kernels, attend(): pl.pallas_call(attend_kernel, out_shape=jax.ShapeDtypeStruct((4, 8, ROWS,...  10.1 us
    all_to_all x1, waiting for transfers between devices, local(): lax.all_to_all(packed, ('z_lo', 'core', 'z_hi'), split_axis=0, concat_axi...  6.74 us
    all_to_all x1, starting transfers between devices, local(): lax.all_to_all(parts, ('x', 'z_lo', 'core'), split_axis=0, concat_axis=0,...  4.98 us
    all_to_all x1, starting transfers between devices, local(): kv = lax.all_to_all(kv, 'y', split_axis=0, concat_axis=0, tiled=True)  4.2 us
  transfers between devices with their start and end apart: 13, of which 7 were waited for; matrix products, arithmetic and copies ran while one was open for 0% of the time, Pallas kernels for 7%

profile of v2, /device:TPU:1, one launch (start us, length us, event | category | flops | bytes accessed | tf_op | source)
XLA Modules:
  0.0 136.0 jit_solution(11003250373988095692)
XLA Ops:
  0.0 1.9 %pack.1 = bf16[32,48,128]{2,1,0:T(8,128)(2,1)} custom-call(bf16[16,3072]{1,0:T(8,128)(2,1)} %q_ref.1, bf16[16,3072]{1,0:T(8,128)(2,1)} %k_ref.1, bf16[16,3072]{1,0:T(8,128)(2,1)} %v_ref.1), custom_call_target="tpu_custom_call" | custom-call | tf_op jit(solution)/shard_map/pack/pallas_call | solution.py:31
  1.9 16.8 %all-to-all-start = ((bf16[32,48,128]{2,1,0:T(8,128)(2,1)}), bf16[32,48,128]{2,1,0:T(8,128)(2,1)S(1)}, u32[]{:S(2)}, u32[]{:S(2)}) async-start(bf16[32,48,128]{2,1,0:T(8,128)(2,1)} %pack.1), calls=%async_computation | async-start | bytes 786432 | tf_op jit(solution)/shard_map/all_to_all | solution.py:272
  18.7 4.2 %collective-permute-start.1 = (s32[3,1,64]{2,1,0:T(1,128)}, s32[3,1,64]{2,1,0:T(1,128)S(1)}, u32[]{:S(2)}, u32[]{:S(2)}) collective-permute-start(s32[3,1,64]{2,1,0:T(1,128)} %m0.1), channel_id=1, source_target_pairs={{0,32},{16,48},{32,0},{48,16},{1,33},{17,49},{33,1},{49,17},{2,34}... | collective-permute-start | bytes 2312 | tf_op jit(solution)/shard_map/ppermute | solution.py:262
  22.9 3.1 %collective-permute-start = (s32[3,1,64]{2,1,0:T(1,128)}, s32[3,1,64]{2,1,0:T(1,128)S(1)}, u32[]{:S(2)}, u32[]{:S(2)}) collective-permute-start(s32[3,1,64]{2,1,0:T(1,128)} %m0.1), channel_id=1, source_target_pairs={{0,16},{16,32},{32,48},{48,0},{1,17},{17,33},{33,49},{49,1},{2,18}... | collective-permute-start | bytes 2312 | tf_op jit(solution)/shard_map/ppermute | solution.py:262
  26.1 3.9 %collective-permute-start.2 = (s32[3,1,64]{2,1,0:T(1,128)}, s32[3,1,64]{2,1,0:T(1,128)S(1)}, u32[]{:S(2)}, u32[]{:S(2)}) collective-permute-start(s32[3,1,64]{2,1,0:T(1,128)} %m0.1), channel_id=1, source_target_pairs={{0,48},{16,0},{32,16},{48,32},{1,49},{17,1},{33,17},{49,33},{2,50}... | collective-permute-start | bytes 2312 | tf_op jit(solution)/shard_map/ppermute | solution.py:262
  30.6 4.2 %collective-permute-done.1.m2 = s32[3,1,64]{2,1,0:T(1,128)S(1)} collective-permute-done((s32[3,1,64]{2,1,0:T(1,128)}, s32[3,1,64]{2,1,0:T(1,128)S(1)}, u32[]{:S(2)}, u32[]{:S(2)}) %collective-permute-start.1) | collective-permute-done | bytes 800 | tf_op jit(solution)/shard_map/ppermute | solution.py:262
  34.8 1.3 collective-permute-done.2.m3
  36.1 6.7 %all-to-all-done.in_ref = bf16[32,48,128]{2,1,0:T(8,128)(2,1)S(1)} async-done(((bf16[32,48,128]{2,1,0:T(8,128)(2,1)}), bf16[32,48,128]{2,1,0:T(8,128)(2,1)S(1)}, u32[]{:S(2)}, u32[]{:S(2)}) %all-to-all-start) | async-done | bytes 393248 | tf_op jit(solution)/shard_map/all_to_all | solution.py:272
  43.6 2.9 %spread.1 = (bf16[33,16,128]{2,1,0:T(8,128)(2,1)}, bf16[4,32,32,128]{3,2,1,0:T(8,128)(2,1)}) custom-call(s32[6]{0:T(128)} %stack.27.at_ref, s32[3,1,64]{2,1,0:T(1,128)} %m0.1, s32[3,1,64]{2,1,0:T(1,128)} %copy-done.5, s32[3,1,64]{2,1,0:T(1,128)} %copy-done.4, s32[3,1,64]{2,1,0:T(1,128)} %copy-done.6, bf16[32,48,128]{2,1,0:T(8,128)(2,1)} %copy-done.2), custom_call_target="tpu_custom_call" | custom-call | tf_op jit(solution)/shard_map/spread/pallas_call | solution.py:65
  46.5 4.2 %all-to-all-start.1 = ((bf16[4,32,32,128]{3,2,1,0:T(8,128)(2,1)}), bf16[4,32,32,128]{3,2,1,0:T(8,128)(2,1)S(1)}, u32[]{:S(2)}, u32[]{:S(2)}) async-start(bf16[4,32,32,128]{3,2,1,0:T(8,128)(2,1)} %get-tuple-element.12), calls=%async_computation.1 | async-start | bytes 2097152 | tf_op jit(solution)/shard_map/all_to_all | solution.py:275
  50.7 4.5 %collective-permute-start.5 = (bf16[33,16,128]{2,1,0:T(8,128)(2,1)}, bf16[33,16,128]{2,1,0:T(8,128)(2,1)S(1)}, u32[]{:S(2)}, u32[]{:S(2)}) collective-permute-start(bf16[33,16,128]{2,1,0:T(8,128)(2,1)} %get-tuple-element.11.q0), channel_id=1, source_target_pairs={{0,12},{4,0},{8,4},{12,8},{1,13},{5,1},{9,5},{13,9},{2,14},{6,2},{... | collective-permute-start | bytes 405512 | tf_op jit(solution)/shard_map/ppermute | solution.py:262
  55.2 2.4 %collective-permute-start.4 = (bf16[33,16,128]{2,1,0:T(8,128)(2,1)}, bf16[33,16,128]{2,1,0:T(8,128)(2,1)S(1)}, u32[]{:S(2)}, u32[]{:S(2)}) collective-permute-start(bf16[33,16,128]{2,1,0:T(8,128)(2,1)} %get-tuple-element.11.q0), channel_id=1, source_target_pairs={{0,8},{4,12},{8,0},{12,4},{1,9},{5,13},{9,1},{13,5},{2,10},{6,14},... | collective-permute-start | bytes 405512 | tf_op jit(solution)/shard_map/ppermute | solution.py:262
  57.6 2.5 %collective-permute-start.3 = (bf16[33,16,128]{2,1,0:T(8,128)(2,1)}, bf16[33,16,128]{2,1,0:T(8,128)(2,1)}, u32[]{:S(2)}, u32[]{:S(2)}) collective-permute-start(bf16[33,16,128]{2,1,0:T(8,128)(2,1)} %get-tuple-element.11.q0), channel_id=1, source_target_pairs={{0,4},{4,8},{8,12},{12,0},{1,5},{5,9},{9,13},{13,1},{2,6},{6,10},{... | collective-permute-start | bytes 405512 | tf_op jit(solution)/shard_map/ppermute | solution.py:262
  60.2 3.7 %collective-permute-start.6 = (bf16[384,3072]{1,0:T(8,128)(2,1)S(1)}, bf16[384,3072]{1,0:T(8,128)(2,1)}, u32[]{:S(2)}, u32[]{:S(2)}) collective-permute-start(bf16[384,3072]{1,0:T(8,128)(2,1)S(1)} %copy-done), channel_id=1, source_target_pairs={{0,64},{64,0},{1,65},{65,1},{2,66},{66,2},{3,67},{67,3},{4,68},{68... | collective-permute-start | bytes 7077896 | tf_op jit(solution)/shard_map/ppermute | solution.py:269
  64.6 2.1 %collective-permute-done.3.q1 = bf16[33,16,128]{2,1,0:T(8,128)(2,1)} collective-permute-done((bf16[33,16,128]{2,1,0:T(8,128)(2,1)}, bf16[33,16,128]{2,1,0:T(8,128)(2,1)}, u32[]{:S(2)}, u32[]{:S(2)}) %collective-permute-start.3) | collective-permute-done | bytes 135200 | tf_op jit(solution)/shard_map/ppermute | solution.py:262
  67.7 10.1 %attend.1 = bf16[4,8,72,128]{3,2,1,0:T(8,128)(2,1)} custom-call(s32[6]{0:T(128)} %stack.27.at_ref, bf16[33,16,128]{2,1,0:T(8,128)(2,1)} %get-tuple-element.11.q0, bf16[33,16,128]{2,1,0:T(8,128)(2,1)} %collective-permute-done.3.q1, bf16[33,16,128]{2,1,0:T(8,128)(2,1)} %copy-done.8, bf16[33,16,128]{2,1,0:T(8,128)(2,1)} %copy-done.7, ...), custom_call_target="tpu_custom_call" | custom-call | flops 1073741824 | bytes 2097152 | tf_op jit(solution)/shard_map/attend/pallas_call | solution.py:186
  77.8 5.0 %all-to-all-start.2 = ((bf16[32,72,128]{2,1,0:T(8,128)(2,1)}), bf16[32,72,128]{2,1,0:T(8,128)(2,1)S(1)}, u32[]{:S(2)}, u32[]{:S(2)}) async-start(bf16[32,72,128]{2,1,0:T(8,128)(2,1)} %bitcast.9), calls=%async_computation.2 | async-start | bytes 1179648 | tf_op jit(solution)/shard_map/all_to_all | solution.py:277
  82.8 18.3 %all-to-all-done.2 = bf16[32,72,128]{2,1,0:T(8,128)(2,1)S(1)} async-done(((bf16[32,72,128]{2,1,0:T(8,128)(2,1)}), bf16[32,72,128]{2,1,0:T(8,128)(2,1)S(1)}, u32[]{:S(2)}, u32[]{:S(2)}) %all-to-all-start.2) | async-done | bytes 589856 | tf_op jit(solution)/shard_map/all_to_all | solution.py:277
  101.1 3.2 %project.1 = (bf16[16,3072]{1,0:T(8,128)(2,1)S(1)}, bf16[16,3072]{1,0:T(8,128)(2,1)S(1)}, bf16[16,3072]{1,0:T(8,128)(2,1)S(1)}, bf16[16,3072]{1,0:T(8,128)(2,1)S(1)}) custom-call(s32[6]{0:T(128)S(1)} %copy-done.1, bf16[4,8,72,128]{3,2,1,0:T(8,128)(2,1)S(1)} %bitcast.8, bf16[384,3072]{1,0:T(8,128)(2,1)S(1)} %copy-done, ...), custom_call_target="tpu_custom_call" | custom-call | tf_op jit(solution)/shard_map/project/pallas_call | solution.py:242
  104.3 5.6 %collective-permute-start.7 = (bf16[16,3072]{1,0:T(8,128)(2,1)S(1)}, bf16[16,3072]{1,0:T(8,128)(2,1)S(1)}, u32[]{:S(2)}, u32[]{:S(2)}) collective-permute-start(bf16[16,3072]{1,0:T(8,128)(2,1)S(1)} %get-tuple-element.14), channel_id=1, source_target_pairs={{0,128},{128,256},{256,384},{384,0},{1,129},{129,257},{257,385},{3... | collective-permute-start | bytes 294920 | tf_op jit(solution)/shard_map/ppermute | solution.py:262
  109.9 7.4 %collective-permute-start.8 = (bf16[16,3072]{1,0:T(8,128)(2,1)S(1)}, bf16[16,3072]{1,0:T(8,128)(2,1)S(1)}, u32[]{:S(2)}, u32[]{:S(2)}) collective-permute-start(bf16[16,3072]{1,0:T(8,128)(2,1)S(1)} %get-tuple-element.15), channel_id=1, source_target_pairs={{0,256},{128,384},{256,0},{384,128},{1,257},{129,385},{257,1},{385... | collective-permute-start | bytes 294920 | tf_op jit(solution)/shard_map/ppermute | solution.py:262
  117.3 4.4 %collective-permute-start.9 = (bf16[16,3072]{1,0:T(8,128)(2,1)S(1)}, bf16[16,3072]{1,0:T(8,128)(2,1)S(1)}, u32[]{:S(2)}, u32[]{:S(2)}) collective-permute-start(bf16[16,3072]{1,0:T(8,128)(2,1)S(1)} %get-tuple-element.16), channel_id=1, source_target_pairs={{0,384},{128,0},{256,128},{384,256},{1,385},{129,1},{257,129},{385... | collective-permute-start | bytes 294920 | tf_op jit(solution)/shard_map/ppermute | solution.py:262
  121.8 8.8 %collective-permute-done.8 = bf16[16,3072]{1,0:T(8,128)(2,1)S(1)} collective-permute-done((bf16[16,3072]{1,0:T(8,128)(2,1)S(1)}, bf16[16,3072]{1,0:T(8,128)(2,1)S(1)}, u32[]{:S(2)}, u32[]{:S(2)}) %collective-permute-start.8) | collective-permute-done | bytes 98336 | tf_op jit(solution)/shard_map/ppermute | solution.py:262
  130.6 4.7 %collective-permute-done.9 = bf16[16,3072]{1,0:T(8,128)(2,1)S(1)} collective-permute-done((bf16[16,3072]{1,0:T(8,128)(2,1)S(1)}, bf16[16,3072]{1,0:T(8,128)(2,1)S(1)}, u32[]{:S(2)}, u32[]{:S(2)}) %collective-permute-start.9) | collective-permute-done | bytes 98336 | tf_op jit(solution)/shard_map/ppermute | solution.py:262
  (26 shorter events, 3.8 us)
Async XLA Ops:
  0.0 60.1 %copy-start = (bf16[384,3072]{1,0:T(8,128)(2,1)S(1)}, bf16[384,3072]{1,0:T(8,128)(2,1)}, u32[]{:S(2)}) copy-start(bf16[384,3072]{1,0:T(8,128)(2,1)} %own_ref.1) | copy-start | bytes 7077892
  1.9 40.9 %all-to-all-start = ((bf16[32,48,128]{2,1,0:T(8,128)(2,1)}), bf16[32,48,128]{2,1,0:T(8,128)(2,1)S(1)}, u32[]{:S(2)}, u32[]{:S(2)}) async-start(bf16[32,48,128]{2,1,0:T(8,128)(2,1)} %pack.1), calls=%async_computation | async-start | bytes 786432 | tf_op jit(solution)/shard_map/all_to_all | solution.py:272
  18.7 16.1 %collective-permute-start.1 = (s32[3,1,64]{2,1,0:T(1,128)}, s32[3,1,64]{2,1,0:T(1,128)S(1)}, u32[]{:S(2)}, u32[]{:S(2)}) collective-permute-start(s32[3,1,64]{2,1,0:T(1,128)} %m0.1), channel_id=1, source_target_pairs={{0,32},{16,48},{32,0},{48,16},{1,33},{17,49},{33,1},{49,17},{2,34}... | collective-permute-start | bytes 2312 | tf_op jit(solution)/shard_map/ppermute | solution.py:262
  22.9 11.9 %collective-permute-start = (s32[3,1,64]{2,1,0:T(1,128)}, s32[3,1,64]{2,1,0:T(1,128)S(1)}, u32[]{:S(2)}, u32[]{:S(2)}) collective-permute-start(s32[3,1,64]{2,1,0:T(1,128)} %m0.1), channel_id=1, source_target_pairs={{0,16},{16,32},{32,48},{48,0},{1,17},{17,33},{33,49},{49,1},{2,18}... | collective-permute-start | bytes 2312 | tf_op jit(solution)/shard_map/ppermute | solution.py:262
  26.1 10.0 %collective-permute-start.2 = (s32[3,1,64]{2,1,0:T(1,128)}, s32[3,1,64]{2,1,0:T(1,128)S(1)}, u32[]{:S(2)}, u32[]{:S(2)}) collective-permute-start(s32[3,1,64]{2,1,0:T(1,128)} %m0.1), channel_id=1, source_target_pairs={{0,48},{16,0},{32,16},{48,32},{1,49},{17,1},{33,17},{49,33},{2,50}... | collective-permute-start | bytes 2312 | tf_op jit(solution)/shard_map/ppermute | solution.py:262
  34.8 8.0 %copy-start.4 = (s32[3,1,64]{2,1,0:T(1,128)}, s32[3,1,64]{2,1,0:T(1,128)S(1)}, u32[]{:S(2)}) copy-start(s32[3,1,64]{2,1,0:T(1,128)S(1)} %collective-permute-done.1.m2) | copy-start | bytes 2308
  34.8 8.0 %copy-start.5 = (s32[3,1,64]{2,1,0:T(1,128)}, s32[3,1,64]{2,1,0:T(1,128)S(1)}, u32[]{:S(2)}) copy-start(s32[3,1,64]{2,1,0:T(1,128)S(1)} %collective-permute-done.m1) | copy-start | bytes 2308
  36.1 6.8 %copy-start.6 = (s32[3,1,64]{2,1,0:T(1,128)}, s32[3,1,64]{2,1,0:T(1,128)S(1)}, u32[]{:S(2)}) copy-start(s32[3,1,64]{2,1,0:T(1,128)S(1)} %collective-permute-done.2.m3) | copy-start | bytes 2308
  42.8 0.7 copy-start.2
  46.5 20.2 %all-to-all-start.1 = ((bf16[4,32,32,128]{3,2,1,0:T(8,128)(2,1)}), bf16[4,32,32,128]{3,2,1,0:T(8,128)(2,1)S(1)}, u32[]{:S(2)}, u32[]{:S(2)}) async-start(bf16[4,32,32,128]{3,2,1,0:T(8,128)(2,1)} %get-tuple-element.12), calls=%async_computation.1 | async-start | bytes 2097152 | tf_op jit(solution)/shard_map/all_to_all | solution.py:275
  50.7 50.4 %copy-start.1 = (s32[6]{0:T(128)S(1)}, s32[6]{0:T(128)}, u32[]{:S(2)}) copy-start(s32[6]{0:T(128)} %stack.27.at_ref) | copy-start | bytes 76
  50.7 13.2 %collective-permute-start.5 = (bf16[33,16,128]{2,1,0:T(8,128)(2,1)}, bf16[33,16,128]{2,1,0:T(8,128)(2,1)S(1)}, u32[]{:S(2)}, u32[]{:S(2)}) collective-permute-start(bf16[33,16,128]{2,1,0:T(8,128)(2,1)} %get-tuple-element.11.q0), channel_id=1, source_target_pairs={{0,12},{4,0},{8,4},{12,8},{1,13},{5,1},{9,5},{13,9},{2,14},{6,2},{... | collective-permute-start | bytes 405512 | tf_op jit(solution)/shard_map/ppermute | solution.py:262
  55.2 8.7 %collective-permute-start.4 = (bf16[33,16,128]{2,1,0:T(8,128)(2,1)}, bf16[33,16,128]{2,1,0:T(8,128)(2,1)S(1)}, u32[]{:S(2)}, u32[]{:S(2)}) collective-permute-start(bf16[33,16,128]{2,1,0:T(8,128)(2,1)} %get-tuple-element.11.q0), channel_id=1, source_target_pairs={{0,8},{4,12},{8,0},{12,4},{1,9},{5,13},{9,1},{13,5},{2,10},{6,14},... | collective-permute-start | bytes 405512 | tf_op jit(solution)/shard_map/ppermute | solution.py:262
  57.6 9.1 %collective-permute-start.3 = (bf16[33,16,128]{2,1,0:T(8,128)(2,1)}, bf16[33,16,128]{2,1,0:T(8,128)(2,1)}, u32[]{:S(2)}, u32[]{:S(2)}) collective-permute-start(bf16[33,16,128]{2,1,0:T(8,128)(2,1)} %get-tuple-element.11.q0), channel_id=1, source_target_pairs={{0,4},{4,8},{8,12},{12,0},{1,5},{5,9},{9,13},{13,1},{2,6},{6,10},{... | collective-permute-start | bytes 405512 | tf_op jit(solution)/shard_map/ppermute | solution.py:262
  60.2 22.6 %collective-permute-start.6 = (bf16[384,3072]{1,0:T(8,128)(2,1)S(1)}, bf16[384,3072]{1,0:T(8,128)(2,1)}, u32[]{:S(2)}, u32[]{:S(2)}) collective-permute-start(bf16[384,3072]{1,0:T(8,128)(2,1)S(1)} %copy-done), channel_id=1, source_target_pairs={{0,64},{64,0},{1,65},{65,1},{2,66},{66,2},{3,67},{67,3},{4,68},{68... | collective-permute-start | bytes 7077896 | tf_op jit(solution)/shard_map/ppermute | solution.py:269
  63.8 2.9 %copy-start.7 = (bf16[33,16,128]{2,1,0:T(8,128)(2,1)}, bf16[33,16,128]{2,1,0:T(8,128)(2,1)S(1)}, u32[]{:S(2)}) copy-start(bf16[33,16,128]{2,1,0:T(8,128)(2,1)S(1)} %collective-permute-done.5.q3) | copy-start | bytes 405508
  63.9 0.7 copy-start.8
  66.7 1.0 copy-start.3
  77.8 23.3 %all-to-all-start.2 = ((bf16[32,72,128]{2,1,0:T(8,128)(2,1)}), bf16[32,72,128]{2,1,0:T(8,128)(2,1)S(1)}, u32[]{:S(2)}, u32[]{:S(2)}) async-start(bf16[32,72,128]{2,1,0:T(8,128)(2,1)} %bitcast.9), calls=%async_computation.2 | async-start | bytes 1179648 | tf_op jit(solution)/shard_map/all_to_all | solution.py:277
  104.3 17.4 %collective-permute-start.7 = (bf16[16,3072]{1,0:T(8,128)(2,1)S(1)}, bf16[16,3072]{1,0:T(8,128)(2,1)S(1)}, u32[]{:S(2)}, u32[]{:S(2)}) collective-permute-start(bf16[16,3072]{1,0:T(8,128)(2,1)S(1)} %get-tuple-element.14), channel_id=1, source_target_pairs={{0,128},{128,256},{256,384},{384,0},{1,129},{129,257},{257,385},{3... | collective-permute-start | bytes 294920 | tf_op jit(solution)/shard_map/ppermute | solution.py:262
  109.9 20.7 %collective-permute-start.8 = (bf16[16,3072]{1,0:T(8,128)(2,1)S(1)}, bf16[16,3072]{1,0:T(8,128)(2,1)S(1)}, u32[]{:S(2)}, u32[]{:S(2)}) collective-permute-start(bf16[16,3072]{1,0:T(8,128)(2,1)S(1)} %get-tuple-element.15), channel_id=1, source_target_pairs={{0,256},{128,384},{256,0},{384,128},{1,257},{129,385},{257,1},{385... | collective-permute-start | bytes 294920 | tf_op jit(solution)/shard_map/ppermute | solution.py:262
  117.3 18.0 %collective-permute-start.9 = (bf16[16,3072]{1,0:T(8,128)(2,1)S(1)}, bf16[16,3072]{1,0:T(8,128)(2,1)S(1)}, u32[]{:S(2)}, u32[]{:S(2)}) collective-permute-start(bf16[16,3072]{1,0:T(8,128)(2,1)S(1)} %get-tuple-element.16), channel_id=1, source_target_pairs={{0,384},{128,0},{256,128},{384,256},{1,385},{129,1},{257,129},{385... | collective-permute-start | bytes 294920 | tf_op jit(solution)/shard_map/ppermute | solution.py:262

commit v3 on v2

v3 whole, which is shorter than its diff:
```python
import jax
import jax.numpy as jnp
from jax import lax
from jax.experimental import pallas as pl
from jax.experimental.pallas import tpu as pltpu
from jax.sharding import Mesh, PartitionSpec as P

BF = jnp.bfloat16
F32 = jnp.float32
AXES = ("z_hi", "core", "z_lo", "x", "y")
LOW = -1e30
small = pltpu.CompilerParams(vmem_limit_bytes=16 * 1024 * 1024)
LOG2E = 1.4426950408889634
ROWS = 72


def pack_kernel(q_ref, k_ref, v_ref, out_ref):
    for slot in range(4):
        for core in range(2):
            for z_hi in range(4):
                head = 3 * (2 * z_hi + core) + slot
                place = slot * 8 + core * 4 + z_hi
                for part, ref in enumerate((q_ref, k_ref, v_ref)):
                    rows = slice(part * 16, part * 16 + 16)
                    if slot < 3:
                        out_ref[place, rows, :] = ref[:, head * 128 : head * 128 + 128]
                    else:
                        out_ref[place, rows, :] = jnp.zeros((16, 128), BF)


def pack(queries, keys, values):
    return pl.pallas_call(
        pack_kernel,
        out_shape=jax.ShapeDtypeStruct((32, 48, 128), BF),
        name="pack",
    )(queries, keys, values)


def choose_kernel(at_ref, m0, m1, m2, m3, out_ref):
    slot, z = at_ref[2], at_ref[5]
    for d, ref in enumerate((m0, m1, m2, m3)):
        zq = (z + 4 - d) % 4
        for x in range(4):
            row = x * 4 + zq
            count = jnp.int32(0)
            for block in range(16):
                out_ref[row, count] = block
                seen = ref[slot, 0, (block % 4) * 16 + 4 * x + block // 4]
                count = count + jnp.where(seen > 0, 1, 0)
            out_ref[row, 16] = count


def choose(at, masks):
    smem = pl.BlockSpec(memory_space=pltpu.SMEM)
    return pl.pallas_call(
        choose_kernel,
        out_shape=jax.ShapeDtypeStruct((16, 128), jnp.int32),
        in_specs=[smem] * 5,
        out_specs=smem,
        compiler_params=small,
        name="choose",
    )(at, *masks)


def spread_kernel(lists_ref, in_ref, q_ref, kv_ref):
    lane = lax.broadcasted_iota(jnp.int32, (16, 128), 1)
    q_ref[32] = jnp.where(lane < 17, lists_ref[...], 0).astype(F32).astype(BF)
    for place in range(32):
        q_ref[place] = in_ref[place, 0:16, :]
        for there in range(4):
            kv_ref[there, place] = in_ref[place, 16:48, :]


def spread(lists, mine):
    vmem = pl.BlockSpec(memory_space=pltpu.VMEM)
    return pl.pallas_call(
        spread_kernel,
        out_shape=[
            jax.ShapeDtypeStruct((33, 16, 128), BF),
            jax.ShapeDtypeStruct((4, 32, 32, 128), BF),
        ],
        in_specs=[vmem, vmem],
        out_specs=[vmem, vmem],
        compiler_params=small,
        name="spread",
    )(lists, mine)


def attend_kernel(
    at_ref, q0, q1, q2, q3, kv_in, out_ref,
    q_ref, kv_ref, vt_ref, qt_ref, rows_ref, list_ref, sems,

):
    x = at_ref[0]
    to_q = [pltpu.make_async_copy(q, q_ref.at[d], sems.at[d]) for d, q in enumerate((q0, q1, q2, q3))]
    to_kv = [pltpu.make_async_copy(kv_in.at[d], kv_ref.at[d], sems.at[4 + d]) for d in range(4)]
    for copy in to_q + to_kv:
        copy.start()
    scale = LOG2E / 128**0.5
    for dq in range(4):
        to_q[dq].wait()
        rows_ref[dq] = q_ref[dq, 32].astype(F32).astype(jnp.int32)
    to_scalars = pltpu.make_async_copy(rows_ref, list_ref, sems.at[8])
    to_scalars.start()
    for dq in range(4):
        for zq in range(4):
            qt_ref[dq * 4 + zq] = q_ref[dq, zq * 8 : zq * 8 + 8].reshape(128, 128).T
    for yk in range(4):
        to_kv[yk].wait()
        for zk in range(4):
            value = kv_ref[yk, zk * 8 : zk * 8 + 8, 16:32, :].reshape(128, 128)
            vt_ref[yk * 4 + zk] = value.T
    to_scalars.wait()

    for dq in range(4):
        xq = (x + 4 - dq) % 4
        counts = [list_ref[dq, x * 4 + zq, 16] for zq in range(4)]
        most = jnp.maximum(jnp.maximum(counts[0], counts[1]), jnp.maximum(counts[2], counts[3]))

        def fold(step, states, dq=dq, counts=counts):
            after = []
            for zq in range(4):
                largest, total, acc = states[zq]
                keys, turned, biases = [], [], []
                for part in range(4):
                    place = step * 4 + part
                    here = place < counts[zq]
                    block = jnp.where(here, list_ref[dq, x * 4 + zq, jnp.where(here, place, 0)], 0)
                    cut = pl.ds(pl.multiple_of((block % 4) * 8, 8), 8)
                    keys.append(kv_ref[block // 4, cut, 0:16, :].reshape(128, 128))
                    turned.append(vt_ref[block])
                    biases.append(jnp.where(here, 0.0, LOW))
                raw = jnp.dot(
                    jnp.concatenate(keys, axis=0), qt_ref[dq * 4 + zq], preferred_element_type=F32
                )
                scores = jnp.concatenate(
                    [raw[i * 128 : i * 128 + 128] * scale + biases[i] for i in range(4)], axis=0
                )
                new = jnp.maximum(largest, jnp.max(scores, axis=0, keepdims=True))
                weights = jnp.exp2(scores - new)
                again = jnp.exp2(largest - new)
                total = total * again + jnp.sum(weights, axis=0, keepdims=True)
                product = jnp.dot(
                    jnp.concatenate(turned, axis=1),
                    weights.astype(BF),
                    preferred_element_type=F32,
                )
                after.append((new, total, acc * again + product))
            return tuple(after)

        start = (
            jnp.full((1, 128), LOW, F32),
            jnp.zeros((1, 128), F32),
            jnp.zeros((128, 128), F32),
        )
        states = lax.fori_loop(0, (most + 3) // 4, fold, (start,) * 4)
        for zq in range(4):
            largest, total, acc = states[zq]
            empty = total == 0.0
            inverse = jnp.where(empty, 0.0, 1.0 / jnp.where(empty, 1.0, total))
            o = (acc * inverse).T.astype(BF)
            lse = largest + jnp.log2(jnp.where(empty, 1.0, total))
            hi = lse.astype(BF)
            rest = lse - hi.astype(F32)
            mid = rest.astype(BF)
            lo = (rest - mid.astype(F32)).astype(BF)
            coded = jnp.concatenate(
                [hi.astype(F32), mid.astype(F32), lo.astype(F32), jnp.zeros((5, 128), F32)], axis=0
            )
            other = jnp.concatenate([coded[:, 64:], coded[:, :64]], axis=1)
            out_ref[xq, zq * 2, 0:64, :] = o[0:64]
            out_ref[xq, zq * 2, 64:72, :] = coded.astype(BF)
            out_ref[xq, zq * 2 + 1, 0:64, :] = o[64:128]
            out_ref[xq, zq * 2 + 1, 64:72, :] = other.astype(BF)


def attend(at, qs, kv):
    smem = pl.BlockSpec(memory_space=pltpu.SMEM)
    vmem = pl.BlockSpec(memory_space=pltpu.VMEM)
    return pl.pallas_call(
        attend_kernel,
        out_shape=jax.ShapeDtypeStruct((4, 8, ROWS, 128), BF),
        in_specs=[smem] + [pl.BlockSpec(memory_space=pl.ANY)] * 5,
        out_specs=vmem,
        scratch_shapes=[
            pltpu.VMEM((4, 33, 16, 128), BF),
            pltpu.VMEM((4, 32, 32, 128), BF),
            pltpu.VMEM((16, 128, 128), BF),
            pltpu.VMEM((16, 128, 128), BF),
            pltpu.VMEM((4, 16, 128), jnp.int32),
            pltpu.SMEM((4, 16, 128), jnp.int32),
            pltpu.SemaphoreType.DMA((9,)),
        ],
        compiler_params=small,
        cost_estimate=pl.CostEstimate(flops=1 << 30, bytes_accessed=2 << 20, transcendentals=1 << 21),
        name="attend",
    )(at, *qs, kv)


def project_kernel(at_ref, parts_ref, own_ref, other_ref, y0, y1, y2, y3, att_ref):
    z_hi, core = at_ref[3], at_ref[4]
    coded = [parts_ref[i // 8, i % 8, 64:72, :].astype(F32) for i in range(32)]
    lse = jnp.concatenate([c[0:1] + c[1:2] + c[2:3] for c in coded], axis=0)
    groups = [lse[8 * i : 8 * i + 8] for i in range(4)]
    top = jnp.maximum(jnp.maximum(groups[0], groups[1]), jnp.maximum(groups[2], groups[3]))
    shares = [jnp.exp2(g - top) for g in groups]
    inverse = 1.0 / (shares[0] + shares[1] + shares[2] + shares[3])
    share = jnp.concatenate([s * inverse for s in shares], axis=0)
    share = jnp.concatenate([share, jnp.zeros((96, 128), F32)], axis=0).T
    for slot in range(3):
        for there in range(2):
            summed = None
            for xk in range(4):
                i = slot * 2 + there
                term = parts_ref[xk, i, 0:64, :].astype(F32) * share[0:64, xk * 8 + i : xk * 8 + i + 1]
                summed = term if summed is None else summed + term
            att_ref[there, :, slot * 128 : slot * 128 + 128] = summed.astype(BF)

    rows = [pl.ds(pl.multiple_of(((z_hi + d) % 4) * 16, 16), 16) for d in range(4)]
    own = jnp.concatenate([att_ref[core, r, :] for r in rows], axis=0)
    other = jnp.concatenate([att_ref[1 - core, r, :] for r in rows], axis=0)
    for cut in range(0, 3072, 512):
        columns = slice(cut, cut + 512)
        y = jnp.dot(own, own_ref[:, columns], preferred_element_type=F32)
        y = (y + jnp.dot(other, other_ref[:, columns], preferred_element_type=F32)).astype(BF)
        for d, y_ref in enumerate((y0, y1, y2, y3)):
            y_ref[:, columns] = y[d * 16 : d * 16 + 16]


def project(at, parts, own, other):
    vmem = pl.BlockSpec(memory_space=pltpu.VMEM)
    return pl.pallas_call(
        project_kernel,
        out_shape=[jax.ShapeDtypeStruct((16, 3072), BF)] * 4,
        in_specs=[pl.BlockSpec(memory_space=pltpu.SMEM), vmem, vmem, vmem],
        out_specs=[vmem] * 4,
        scratch_shapes=[pltpu.VMEM((2, 64, 384), BF)],
        compiler_params=small,
        name="project",
    )(at, parts, own, other)


def turn(array, axis, step):
    return lax.ppermute(array, axis, [(i, (i + step) % 4) for i in range(4)])


def local(queries, keys_in, values, block_mask, w_out):
    x, y, z = lax.axis_index("x"), lax.axis_index("y"), lax.axis_index("z_lo")
    z_hi, core = lax.axis_index("z_hi"), lax.axis_index("core")
    at = jnp.stack([x, y, jnp.minimum(z, 2), z_hi, core, z]).astype(jnp.int32)
    masks = [block_mask] + [turn(block_mask, "z_lo", d) for d in (1, 2, 3)]
    lists = choose(at, masks)
    packed = pack(queries, keys_in, values)
    mine = lax.all_to_all(packed, ("z_lo", "core", "z_hi"), split_axis=0, concat_axis=0, tiled=True)
    q, kv = spread(lists, mine)
    q, w_here = lax.optimization_barrier((q, w_out))
    w_other = lax.ppermute(w_here, "core", [(0, 1), (1, 0)])
    qs = [q] + [turn(q, "x", d) for d in (1, 2, 3)]
    kv = lax.all_to_all(kv, "y", split_axis=0, concat_axis=0, tiled=True)
    parts = attend(at, qs, kv)
    parts = lax.all_to_all(
        parts.reshape(32, ROWS, 128), ("x", "z_lo", "core"), split_axis=0, concat_axis=0, tiled=True
    )
    ys = project(at, parts.reshape(4, 8, ROWS, 128), w_out, w_other)
    far, right, left = [turn(ys[d], "z_hi", d).astype(F32) for d in (2, 1, 3)]
    return (((ys[0].astype(F32) + far) + right) + left).astype(BF)


def solution(mesh):
    fine = Mesh(mesh.devices.reshape(4, 2, 4, 4, 4), AXES)
    tokens = P(("z_lo", "x", "y", "z_hi", "core"), None)
    placed = (
        tokens,
        tokens,
        tokens,
        P(("z_hi", "core"), ("z_lo", "x", "y"), None),
        P(("z_hi", "core"), None),
    )
    return jax.shard_map(local, mesh=fine, in_specs=placed, out_specs=tokens, check_vma=False)
```

time: 137 us -> 129 us (0.942)
  waiting for transfers between devices: 46.1 us -> 40.5 us
  Pallas kernels: 18.1 us -> 14.4 us
  starting transfers between devices: 67.7 us -> 70.9 us
    pallas_call x1, Pallas kernels: 10.1 us -> 6.82 us  [attend(): pl.pallas_call(attend_kernel, out_shape=jax.ShapeDtypeStruct((4, 8, ROWS,...]
    all_to_all x1, waiting for transfers between devices: 6.74 us -> 3.7 us  [local(): lax.all_to_all(packed, ('z_lo', 'core', 'z_hi'), split_axis=0, concat_axi...]
    pallas_call x1, Pallas kernels: 2.89 us -> 0.15 us  [spread(): pl.pallas_call(spread_kernel, out_shape=[jax.ShapeDtypeStruct((33, 16, 12...]
    all_to_all x1, starting transfers between devices: 4.98 us -> 7.65 us  [local(): lax.all_to_all(parts.reshape(32, ROWS, 128), ('x', 'z_lo', 'core'), split...]
    ppermute x9, waiting for transfers between devices: 21.1 us -> 18.6 us  [turn(): return lax.ppermute(array, axis, [(i, (i + step) % 4) for i in range(4)])]
    pallas_call x0 -> x1, Pallas kernels: none -> 2.36 us  [choose(): pl.pallas_call(choose_kernel, out_shape=jax.ShapeDtypeStruct((16, 128), j...]
  transfers between devices with their start and end apart: 13 -> 13, of which waited for: 7 -> 8; matrix products, arithmetic and copies ran while one was open for 0% -> 0% of each run, Pallas kernels for 7% -> 7%
where the time goes in v3:
time: 129 us; the launch traced here: 128 us
  starting transfers between devices  70.9 us (55%)
  waiting for transfers between devices  40.5 us (31%)
  Pallas kernels  14.4 us (11%)
  local copies, waits for them, and re-layouts  1.74 us (1%)
    ppermute x9, starting transfers between devices, turn(): return lax.ppermute(array, axis, [(i, (i + step) % 4) for i in range(4)])  38.7 us
    ppermute x9, waiting for transfers between devices, turn(): return lax.ppermute(array, axis, [(i, (i + step) % 4) for i in range(4)])  18.6 us
    all_to_all x1, waiting for transfers between devices, local(): lax.all_to_all(parts.reshape(32, ROWS, 128), ('x', 'z_lo', 'core'), split...  18.2 us
    all_to_all x1, starting transfers between devices, local(): lax.all_to_all(packed, ('z_lo', 'core', 'z_hi'), split_axis=0, concat_axi...  16.8 us
    all_to_all x1, starting transfers between devices, local(): lax.all_to_all(parts.reshape(32, ROWS, 128), ('x', 'z_lo', 'core'), split...  7.65 us
    pallas_call x1, Pallas kernels, attend(): pl.pallas_call(attend_kernel, out_shape=jax.ShapeDtypeStruct((4, 8, ROWS,...  6.82 us
    all_to_all x1, starting transfers between devices, local(): kv = lax.all_to_all(kv, 'y', split_axis=0, concat_axis=0, tiled=True)  4.24 us
    all_to_all x1, waiting for transfers between devices, local(): lax.all_to_all(packed, ('z_lo', 'core', 'z_hi'), split_axis=0, concat_axi...  3.7 us
  transfers between devices with their start and end apart: 13, of which 8 were waited for; matrix products, arithmetic and copies ran while one was open for 0% of the time, Pallas kernels for 7%

profile of v3, /device:TPU:1, one launch (start us, length us, event | category | flops | bytes accessed | tf_op | source)
XLA Modules:
  0.0 128.4 jit_solution(10490683508700258837)
XLA Ops:
  0.0 1.9 %pack.1 = bf16[32,48,128]{2,1,0:T(8,128)(2,1)} custom-call(bf16[16,3072]{1,0:T(8,128)(2,1)} %q_ref.1, bf16[16,3072]{1,0:T(8,128)(2,1)} %k_ref.1, bf16[16,3072]{1,0:T(8,128)(2,1)} %v_ref.1), custom_call_target="tpu_custom_call" | custom-call | tf_op jit(solution)/shard_map/pack/pallas_call | solution.py:32
  2.0 16.8 %all-to-all-start = ((bf16[32,48,128]{2,1,0:T(8,128)(2,1)}), bf16[32,48,128]{2,1,0:T(8,128)(2,1)S(1)}, u32[]{:S(2)}, u32[]{:S(2)}) async-start(bf16[32,48,128]{2,1,0:T(8,128)(2,1)} %pack.1), calls=%async_computation | async-start | bytes 786432 | tf_op jit(solution)/shard_map/all_to_all | solution.py:254
  18.7 4.2 %collective-permute-start.1 = (s32[3,1,64]{2,1,0:T(1,128)}, s32[3,1,64]{2,1,0:T(1,128)S(1)}, u32[]{:S(2)}, u32[]{:S(2)}) collective-permute-start(s32[3,1,64]{2,1,0:T(1,128)} %m0.1), channel_id=1, source_target_pairs={{0,32},{16,48},{32,0},{48,16},{1,33},{17,49},{33,1},{49,17},{2,34}... | collective-permute-start | bytes 2312 | tf_op jit(solution)/shard_map/ppermute | solution.py:244
  22.9 3.1 %collective-permute-start = (s32[3,1,64]{2,1,0:T(1,128)}, s32[3,1,64]{2,1,0:T(1,128)S(1)}, u32[]{:S(2)}, u32[]{:S(2)}) collective-permute-start(s32[3,1,64]{2,1,0:T(1,128)} %m0.1), channel_id=1, source_target_pairs={{0,16},{16,32},{32,48},{48,0},{1,17},{17,33},{33,49},{49,1},{2,18}... | collective-permute-start | bytes 2312 | tf_op jit(solution)/shard_map/ppermute | solution.py:244
  26.1 3.9 %collective-permute-start.2 = (s32[3,1,64]{2,1,0:T(1,128)}, s32[3,1,64]{2,1,0:T(1,128)S(1)}, u32[]{:S(2)}, u32[]{:S(2)}) collective-permute-start(s32[3,1,64]{2,1,0:T(1,128)} %m0.1), channel_id=1, source_target_pairs={{0,48},{16,0},{32,16},{48,32},{1,49},{17,1},{33,17},{49,33},{2,50}... | collective-permute-start | bytes 2312 | tf_op jit(solution)/shard_map/ppermute | solution.py:244
  30.1 4.7 %collective-permute-done.1.m2 = s32[3,1,64]{2,1,0:T(1,128)S(1)} collective-permute-done((s32[3,1,64]{2,1,0:T(1,128)}, s32[3,1,64]{2,1,0:T(1,128)S(1)}, u32[]{:S(2)}, u32[]{:S(2)}) %collective-permute-start.1) | collective-permute-done | bytes 800 | tf_op jit(solution)/shard_map/ppermute | solution.py:244
  34.8 1.3 collective-permute-done.2.m3
  36.8 2.4 %choose.1.lists_ref = s32[16,128]{1,0:T(8,128)S(1)} custom-call(s32[6]{0:T(128)S(1)} %stack.27.at_ref, s32[3,1,64]{2,1,0:T(1,128)S(1)} %copy-done.2, s32[3,1,64]{2,1,0:T(1,128)S(1)} %collective-permute-done.m1, s32[3,1,64]{2,1,0:T(1,128)S(1)} %collective-permute-done.1.m2, s32[3,1,64]{2,1,0:T(1,128)S(1)} %collective-permute-done.2.m3), custom_call_target="tpu_custom_call" | custom-call | tf_op jit(solution)/shard_map/choose/pallas_call | solution.py:55
  39.1 3.7 %all-to-all-done.in_ref = bf16[32,48,128]{2,1,0:T(8,128)(2,1)S(1)} async-done(((bf16[32,48,128]{2,1,0:T(8,128)(2,1)}), bf16[32,48,128]{2,1,0:T(8,128)(2,1)S(1)}, u32[]{:S(2)}, u32[]{:S(2)}) %all-to-all-start) | async-done | bytes 393248 | tf_op jit(solution)/shard_map/all_to_all | solution.py:254
  43.9 4.2 %all-to-all-start.1 = ((bf16[4,32,32,128]{3,2,1,0:T(8,128)(2,1)}), bf16[4,32,32,128]{3,2,1,0:T(8,128)(2,1)}, u32[]{:S(2)}, u32[]{:S(2)}) async-start(bf16[4,32,32,128]{3,2,1,0:T(8,128)(2,1)} %copy-done.1), calls=%async_computation.1 | async-start | bytes 2097152 | tf_op jit(solution)/shard_map/all_to_all | solution.py:259
  48.2 4.4 %collective-permute-start.5 = (bf16[33,16,128]{2,1,0:T(8,128)(2,1)S(1)}, bf16[33,16,128]{2,1,0:T(8,128)(2,1)S(1)}, u32[]{:S(2)}, u32[]{:S(2)}) collective-permute-start(bf16[33,16,128]{2,1,0:T(8,128)(2,1)S(1)} %get-tuple-element.14.q0), channel_id=1, source_target_pairs={{0,12},{4,0},{8,4},{12,8},{1,13},{5,1},{9,5},{13,9},{2,14},{6,2},{... | collective-permute-start | bytes 405512 | tf_op jit(solution)/shard_map/ppermute | solution.py:244
  52.6 2.4 %collective-permute-start.4 = (bf16[33,16,128]{2,1,0:T(8,128)(2,1)S(1)}, bf16[33,16,128]{2,1,0:T(8,128)(2,1)S(1)}, u32[]{:S(2)}, u32[]{:S(2)}) collective-permute-start(bf16[33,16,128]{2,1,0:T(8,128)(2,1)S(1)} %get-tuple-element.14.q0), channel_id=1, source_target_pairs={{0,8},{4,12},{8,0},{12,4},{1,9},{5,13},{9,1},{13,5},{2,10},{6,14},... | collective-permute-start | bytes 405512 | tf_op jit(solution)/shard_map/ppermute | solution.py:244
  55.0 2.5 %collective-permute-start.3 = (bf16[33,16,128]{2,1,0:T(8,128)(2,1)S(1)}, bf16[33,16,128]{2,1,0:T(8,128)(2,1)S(1)}, u32[]{:S(2)}, u32[]{:S(2)}) collective-permute-start(bf16[33,16,128]{2,1,0:T(8,128)(2,1)S(1)} %get-tuple-element.14.q0), channel_id=1, source_target_pairs={{0,4},{4,8},{8,12},{12,0},{1,5},{5,9},{9,13},{13,1},{2,6},{6,10},{... | collective-permute-start | bytes 405512 | tf_op jit(solution)/shard_map/ppermute | solution.py:244
  57.6 3.6 %collective-permute-start.6 = (bf16[384,3072]{1,0:T(8,128)(2,1)S(1)}, bf16[384,3072]{1,0:T(8,128)(2,1)}, u32[]{:S(2)}, u32[]{:S(2)}) collective-permute-start(bf16[384,3072]{1,0:T(8,128)(2,1)S(1)} %copy-done), channel_id=1, source_target_pairs={{0,64},{64,0},{1,65},{65,1},{2,66},{66,2},{3,67},{67,3},{4,68},{68... | collective-permute-start | bytes 7077896 | tf_op jit(solution)/shard_map/ppermute | solution.py:257
  61.2 2.7 %collective-permute-done.3.q1 = bf16[33,16,128]{2,1,0:T(8,128)(2,1)S(1)} collective-permute-done((bf16[33,16,128]{2,1,0:T(8,128)(2,1)S(1)}, bf16[33,16,128]{2,1,0:T(8,128)(2,1)S(1)}, u32[]{:S(2)}, u32[]{:S(2)}) %collective-permute-start.3) | collective-permute-done | bytes 135200 | tf_op jit(solution)/shard_map/ppermute | solution.py:244
  63.9 6.8 %attend.1 = bf16[4,8,72,128]{3,2,1,0:T(8,128)(2,1)} custom-call(s32[6]{0:T(128)S(1)} %stack.27.at_ref, bf16[33,16,128]{2,1,0:T(8,128)(2,1)S(1)} %get-tuple-element.14.q0, bf16[33,16,128]{2,1,0:T(8,128)(2,1)S(1)} %collective-permute-done.3.q1, bf16[33,16,128]{2,1,0:T(8,128)(2,1)S(1)} %collective-permute-done.4.q2, ...), custom_call_target="tpu_custom_call" | custom-call | flops 1073741824 | bytes 2097152 | tf_op jit(solution)/shard_map/attend/pallas_call | solution.py:180
  70.7 7.6 %all-to-all-start.2 = ((bf16[32,72,128]{2,1,0:T(8,128)(2,1)}), bf16[32,72,128]{2,1,0:T(8,128)(2,1)S(1)}, u32[]{:S(2)}, u32[]{:S(2)}) async-start(bf16[32,72,128]{2,1,0:T(8,128)(2,1)} %bitcast.6), calls=%async_computation.2 | async-start | bytes 1179648 | tf_op jit(solution)/shard_map/all_to_all | solution.py:261
  78.4 18.2 %all-to-all-done.2 = bf16[32,72,128]{2,1,0:T(8,128)(2,1)S(1)} async-done(((bf16[32,72,128]{2,1,0:T(8,128)(2,1)}), bf16[32,72,128]{2,1,0:T(8,128)(2,1)S(1)}, u32[]{:S(2)}, u32[]{:S(2)}) %all-to-all-start.2) | async-done | bytes 589856 | tf_op jit(solution)/shard_map/all_to_all | solution.py:261
  96.6 3.1 %project.1 = (bf16[16,3072]{1,0:T(8,128)(2,1)S(1)}, bf16[16,3072]{1,0:T(8,128)(2,1)S(1)}, bf16[16,3072]{1,0:T(8,128)(2,1)S(1)}, bf16[16,3072]{1,0:T(8,128)(2,1)S(1)}) custom-call(s32[6]{0:T(128)S(1)} %stack.27.at_ref, bf16[4,8,72,128]{3,2,1,0:T(8,128)(2,1)S(1)} %bitcast.8, bf16[384,3072]{1,0:T(8,128)(2,1)S(1)} %copy-done, ...), custom_call_target="tpu_custom_call" | custom-call | tf_op jit(solution)/shard_map/project/pallas_call | solution.py:232
  99.7 8.9 %collective-permute-start.7 = (bf16[16,3072]{1,0:T(8,128)(2,1)S(1)}, bf16[16,3072]{1,0:T(8,128)(2,1)S(1)}, u32[]{:S(2)}, u32[]{:S(2)}) collective-permute-start(bf16[16,3072]{1,0:T(8,128)(2,1)S(1)} %get-tuple-element.18), channel_id=1, source_target_pairs={{0,256},{128,384},{256,0},{384,128},{1,257},{129,385},{257,1},{385... | collective-permute-start | bytes 294920 | tf_op jit(solution)/shard_map/ppermute | solution.py:244
  108.5 3.1 %collective-permute-start.8 = (bf16[16,3072]{1,0:T(8,128)(2,1)S(1)}, bf16[16,3072]{1,0:T(8,128)(2,1)S(1)}, u32[]{:S(2)}, u32[]{:S(2)}) collective-permute-start(bf16[16,3072]{1,0:T(8,128)(2,1)S(1)} %get-tuple-element.19), channel_id=1, source_target_pairs={{0,128},{128,256},{256,384},{384,0},{1,129},{129,257},{257,385},{3... | collective-permute-start | bytes 294920 | tf_op jit(solution)/shard_map/ppermute | solution.py:244
  111.7 6.1 %collective-permute-start.9 = (bf16[16,3072]{1,0:T(8,128)(2,1)S(1)}, bf16[16,3072]{1,0:T(8,128)(2,1)S(1)}, u32[]{:S(2)}, u32[]{:S(2)}) collective-permute-start(bf16[16,3072]{1,0:T(8,128)(2,1)S(1)} %get-tuple-element.20), channel_id=1, source_target_pairs={{0,384},{128,0},{256,128},{384,256},{1,385},{129,1},{257,129},{385... | collective-permute-start | bytes 294920 | tf_op jit(solution)/shard_map/ppermute | solution.py:244
  117.8 6.2 %collective-permute-done.7 = bf16[16,3072]{1,0:T(8,128)(2,1)S(1)} collective-permute-done((bf16[16,3072]{1,0:T(8,128)(2,1)S(1)}, bf16[16,3072]{1,0:T(8,128)(2,1)S(1)}, u32[]{:S(2)}, u32[]{:S(2)}) %collective-permute-start.7) | collective-permute-done | bytes 98336 | tf_op jit(solution)/shard_map/ppermute | solution.py:244
  125.1 2.6 %collective-permute-done.9 = bf16[16,3072]{1,0:T(8,128)(2,1)S(1)} collective-permute-done((bf16[16,3072]{1,0:T(8,128)(2,1)S(1)}, bf16[16,3072]{1,0:T(8,128)(2,1)S(1)}, u32[]{:S(2)}, u32[]{:S(2)}) %collective-permute-start.9) | collective-permute-done | bytes 98336 | tf_op jit(solution)/shard_map/ppermute | solution.py:244
  (15 shorter events, 3.8 us)
Async XLA Ops:
  0.0 57.5 %copy-start = (bf16[384,3072]{1,0:T(8,128)(2,1)S(1)}, bf16[384,3072]{1,0:T(8,128)(2,1)}, u32[]{:S(2)}) copy-start(bf16[384,3072]{1,0:T(8,128)(2,1)} %own_ref.1) | copy-start | bytes 7077892
  2.0 40.9 %all-to-all-start = ((bf16[32,48,128]{2,1,0:T(8,128)(2,1)}), bf16[32,48,128]{2,1,0:T(8,128)(2,1)S(1)}, u32[]{:S(2)}, u32[]{:S(2)}) async-start(bf16[32,48,128]{2,1,0:T(8,128)(2,1)} %pack.1), calls=%async_computation | async-start | bytes 786432 | tf_op jit(solution)/shard_map/all_to_all | solution.py:254
  18.7 16.1 %collective-permute-start.1 = (s32[3,1,64]{2,1,0:T(1,128)}, s32[3,1,64]{2,1,0:T(1,128)S(1)}, u32[]{:S(2)}, u32[]{:S(2)}) collective-permute-start(s32[3,1,64]{2,1,0:T(1,128)} %m0.1), channel_id=1, source_target_pairs={{0,32},{16,48},{32,0},{48,16},{1,33},{17,49},{33,1},{49,17},{2,34}... | collective-permute-start | bytes 2312 | tf_op jit(solution)/shard_map/ppermute | solution.py:244
  22.9 11.9 %collective-permute-start = (s32[3,1,64]{2,1,0:T(1,128)}, s32[3,1,64]{2,1,0:T(1,128)S(1)}, u32[]{:S(2)}, u32[]{:S(2)}) collective-permute-start(s32[3,1,64]{2,1,0:T(1,128)} %m0.1), channel_id=1, source_target_pairs={{0,16},{16,32},{32,48},{48,0},{1,17},{17,33},{33,49},{49,1},{2,18}... | collective-permute-start | bytes 2312 | tf_op jit(solution)/shard_map/ppermute | solution.py:244
  26.1 10.0 %collective-permute-start.2 = (s32[3,1,64]{2,1,0:T(1,128)}, s32[3,1,64]{2,1,0:T(1,128)S(1)}, u32[]{:S(2)}, u32[]{:S(2)}) collective-permute-start(s32[3,1,64]{2,1,0:T(1,128)} %m0.1), channel_id=1, source_target_pairs={{0,48},{16,0},{32,16},{48,32},{1,49},{17,1},{33,17},{49,33},{2,50}... | collective-permute-start | bytes 2312 | tf_op jit(solution)/shard_map/ppermute | solution.py:244
  36.1 0.7 copy-start.2
  43.0 1.0 copy-start.1
  43.9 19.9 %all-to-all-start.1 = ((bf16[4,32,32,128]{3,2,1,0:T(8,128)(2,1)}), bf16[4,32,32,128]{3,2,1,0:T(8,128)(2,1)}, u32[]{:S(2)}, u32[]{:S(2)}) async-start(bf16[4,32,32,128]{3,2,1,0:T(8,128)(2,1)} %copy-done.1), calls=%async_computation.1 | async-start | bytes 2097152 | tf_op jit(solution)/shard_map/all_to_all | solution.py:259
  48.2 13.0 %collective-permute-start.5 = (bf16[33,16,128]{2,1,0:T(8,128)(2,1)S(1)}, bf16[33,16,128]{2,1,0:T(8,128)(2,1)S(1)}, u32[]{:S(2)}, u32[]{:S(2)}) collective-permute-start(bf16[33,16,128]{2,1,0:T(8,128)(2,1)S(1)} %get-tuple-element.14.q0), channel_id=1, source_target_pairs={{0,12},{4,0},{8,4},{12,8},{1,13},{5,1},{9,5},{13,9},{2,14},{6,2},{... | collective-permute-start | bytes 405512 | tf_op jit(solution)/shard_map/ppermute | solution.py:244
  52.6 8.6 %collective-permute-start.4 = (bf16[33,16,128]{2,1,0:T(8,128)(2,1)S(1)}, bf16[33,16,128]{2,1,0:T(8,128)(2,1)S(1)}, u32[]{:S(2)}, u32[]{:S(2)}) collective-permute-start(bf16[33,16,128]{2,1,0:T(8,128)(2,1)S(1)} %get-tuple-element.14.q0), channel_id=1, source_target_pairs={{0,8},{4,12},{8,0},{12,4},{1,9},{5,13},{9,1},{13,5},{2,10},{6,14},... | collective-permute-start | bytes 405512 | tf_op jit(solution)/shard_map/ppermute | solution.py:244
  55.0 8.9 %collective-permute-start.3 = (bf16[33,16,128]{2,1,0:T(8,128)(2,1)S(1)}, bf16[33,16,128]{2,1,0:T(8,128)(2,1)S(1)}, u32[]{:S(2)}, u32[]{:S(2)}) collective-permute-start(bf16[33,16,128]{2,1,0:T(8,128)(2,1)S(1)} %get-tuple-element.14.q0), channel_id=1, source_target_pairs={{0,4},{4,8},{8,12},{12,0},{1,5},{5,9},{9,13},{13,1},{2,6},{6,10},{... | collective-permute-start | bytes 405512 | tf_op jit(solution)/shard_map/ppermute | solution.py:244
  57.6 20.8 %collective-permute-start.6 = (bf16[384,3072]{1,0:T(8,128)(2,1)S(1)}, bf16[384,3072]{1,0:T(8,128)(2,1)}, u32[]{:S(2)}, u32[]{:S(2)}) collective-permute-start(bf16[384,3072]{1,0:T(8,128)(2,1)S(1)} %copy-done), channel_id=1, source_target_pairs={{0,64},{64,0},{1,65},{65,1},{2,66},{66,2},{3,67},{67,3},{4,68},{68... | collective-permute-start | bytes 7077896 | tf_op jit(solution)/shard_map/ppermute | solution.py:257
  70.7 25.8 %all-to-all-start.2 = ((bf16[32,72,128]{2,1,0:T(8,128)(2,1)}), bf16[32,72,128]{2,1,0:T(8,128)(2,1)S(1)}, u32[]{:S(2)}, u32[]{:S(2)}) async-start(bf16[32,72,128]{2,1,0:T(8,128)(2,1)} %bitcast.6), calls=%async_computation.2 | async-start | bytes 1179648 | tf_op jit(solution)/shard_map/all_to_all | solution.py:261
  99.7 24.3 %collective-permute-start.7 = (bf16[16,3072]{1,0:T(8,128)(2,1)S(1)}, bf16[16,3072]{1,0:T(8,128)(2,1)S(1)}, u32[]{:S(2)}, u32[]{:S(2)}) collective-permute-start(bf16[16,3072]{1,0:T(8,128)(2,1)S(1)} %get-tuple-element.18), channel_id=1, source_target_pairs={{0,256},{128,384},{256,0},{384,128},{1,257},{129,385},{257,1},{385... | collective-permute-start | bytes 294920 | tf_op jit(solution)/shard_map/ppermute | solution.py:244
  108.5 16.6 %collective-permute-start.8 = (bf16[16,3072]{1,0:T(8,128)(2,1)S(1)}, bf16[16,3072]{1,0:T(8,128)(2,1)S(1)}, u32[]{:S(2)}, u32[]{:S(2)}) collective-permute-start(bf16[16,3072]{1,0:T(8,128)(2,1)S(1)} %get-tuple-element.19), channel_id=1, source_target_pairs={{0,128},{128,256},{256,384},{384,0},{1,129},{129,257},{257,385},{3... | collective-permute-start | bytes 294920 | tf_op jit(solution)/shard_map/ppermute | solution.py:244
  111.7 16.1 %collective-permute-start.9 = (bf16[16,3072]{1,0:T(8,128)(2,1)S(1)}, bf16[16,3072]{1,0:T(8,128)(2,1)S(1)}, u32[]{:S(2)}, u32[]{:S(2)}) collective-permute-start(bf16[16,3072]{1,0:T(8,128)(2,1)S(1)} %get-tuple-element.20), channel_id=1, source_target_pairs={{0,384},{128,0},{256,128},{384,256},{1,385},{129,1},{257,129},{385... | collective-permute-start | bytes 294920 | tf_op jit(solution)/shard_map/ppermute | solution.py:244

commit v4 on v3

v4 whole, which is shorter than its diff:
```python
import jax
import jax.numpy as jnp
from jax import lax
from jax.experimental import pallas as pl
from jax.experimental.pallas import tpu as pltpu
from jax.sharding import Mesh, PartitionSpec as P

BF = jnp.bfloat16
F32 = jnp.float32
AXES = ("z_hi", "core", "z_lo", "x", "y")
LOW = -1e30
small = pltpu.CompilerParams(vmem_limit_bytes=16 * 1024 * 1024)
LOG2E = 1.4426950408889634
ROWS = 72


def pack_kernel(q_in, k_in, v_in, out_ref, q_ref, k_ref, v_ref, held, sems):
    parts = ((q_in, q_ref), (k_in, k_ref), (v_in, v_ref))
    into = [pltpu.make_async_copy(a, b, sems.at[i]) for i, (a, b) in enumerate(parts)]
    for copy in into:
        copy.start()
    held[24:32] = jnp.zeros((8, 48, 128), BF)
    outs = [pltpu.make_async_copy(held.at[24:32], out_ref.at[24:32], sems.at[3])]
    outs[0].start()
    for part, (_, ref) in enumerate(parts):
        rows = slice(part * 16, part * 16 + 16)
        into[part].wait()
        for slot in range(3):
            for core in range(2):
                for z_hi in range(4):
                    head = 3 * (2 * z_hi + core) + slot
                    held[slot * 8 + core * 4 + z_hi, rows, :] = ref[:, head * 128 : head * 128 + 128]
        outs.append(
            pltpu.make_async_copy(held.at[0:24, rows], out_ref.at[0:24, rows], sems.at[4 + part])
        )
        outs[-1].start()
    for copy in outs:
        copy.wait()


def pack(queries, keys, values):
    anywhere = pl.BlockSpec(memory_space=pl.ANY)
    return pl.pallas_call(
        pack_kernel,
        out_shape=jax.ShapeDtypeStruct((32, 48, 128), BF),
        in_specs=[anywhere] * 3,
        out_specs=anywhere,
        scratch_shapes=[pltpu.VMEM((16, 3072), BF)] * 3
        + [pltpu.VMEM((32, 48, 128), BF), pltpu.SemaphoreType.DMA((7,))],
        compiler_params=pltpu.CompilerParams(vmem_limit_bytes=56 * 1024 * 1024),
        name="pack",
    )(queries, keys, values)


def choose_kernel(mask_ref, out_ref):
    for slot in range(3):
        for x in range(4):
            count = jnp.int32(0)
            for block in range(16):
                out_ref[slot, x, count] = block
                seen = mask_ref[slot, 0, (block % 4) * 16 + 4 * x + block // 4]
                count = count + jnp.where(seen > 0, 1, 0)
            out_ref[slot, x, 16] = count


def choose(mask):
    smem = pl.BlockSpec(memory_space=pltpu.SMEM)
    return pl.pallas_call(
        choose_kernel,
        out_shape=jax.ShapeDtypeStruct((3, 8, 128), jnp.int32),
        in_specs=[smem],
        out_specs=smem,
        compiler_params=small,
        name="choose",
    )(mask)


def spread_kernel(at_ref, l0, l1, l2, l3, in_ref, q_ref, kv_ref, tail):
    slot, z = at_ref[2], at_ref[5]
    used = lax.broadcasted_iota(jnp.int32, (8, 128), 0) < 4
    used = used & (lax.broadcasted_iota(jnp.int32, (8, 128), 1) < 17)
    for d, ref in enumerate((l0, l1, l2, l3)):
        tail[(z + 4 - d) % 4] = jnp.where(used, ref[slot], 0).astype(F32)
    q_ref[32:34] = tail[...].reshape(2, 16, 128).astype(BF)
    for place in range(32):
        q_ref[place] = in_ref[place, 0:16, :]
        for there in range(4):
            kv_ref[there, place] = in_ref[place, 16:48, :]


def spread(at, lists, mine):
    vmem = pl.BlockSpec(memory_space=pltpu.VMEM)
    return pl.pallas_call(
        spread_kernel,
        out_shape=[
            jax.ShapeDtypeStruct((34, 16, 128), BF),
            jax.ShapeDtypeStruct((4, 32, 32, 128), BF),
        ],
        in_specs=[pl.BlockSpec(memory_space=pltpu.SMEM)] + [vmem] * 5,
        out_specs=[vmem, vmem],
        scratch_shapes=[pltpu.VMEM((4, 8, 128), F32)],
        compiler_params=small,
        name="spread",
    )(at, *lists, mine)


def attend_kernel(
    at_ref, q0, q1, q2, q3, kv_in, out_ref,
    q_ref, kv_ref, vt_ref, qt_ref, sums_ref, acc_ref, rows_ref, list_ref, sems,

):
    x = at_ref[0]
    to_q = [pltpu.make_async_copy(q, q_ref.at[d], sems.at[d]) for d, q in enumerate((q0, q1, q2, q3))]
    to_kv = [pltpu.make_async_copy(kv_in.at[d], kv_ref.at[d], sems.at[4 + d]) for d in range(4)]
    for copy in to_q + to_kv:
        copy.start()
    scale = LOG2E / 128**0.5
    for dq in range(4):
        to_q[dq].wait()
        rows_ref[dq] = q_ref[dq, 32:34].reshape(32, 128).astype(F32).astype(jnp.int32)
    to_scalars = pltpu.make_async_copy(rows_ref, list_ref, sems.at[8])
    to_scalars.start()
    for dq in range(4):
        for zq in range(4):
            qt_ref[dq * 4 + zq] = q_ref[dq, zq * 8 : zq * 8 + 8].reshape(128, 128).T
    for yk in range(4):
        to_kv[yk].wait()
        for zk in range(4):
            value = kv_ref[yk, zk * 8 : zk * 8 + 8, 16:32, :].reshape(128, 128)
            vt_ref[yk * 4 + zk] = value.T
    to_scalars.wait()

    counts = [list_ref[at // 4, at % 4 * 8 + x, 16] for at in range(16)]

    def look(at, step, state):
        keys, turned, biases = [], [], []
        for part in range(4):
            place = step * 4 + part
            here = place < counts[at]
            block = jnp.where(here, list_ref[at // 4, at % 4 * 8 + x, jnp.where(here, place, 0)], 0)
            cut = pl.ds(pl.multiple_of((block % 4) * 8, 8), 8)
            keys.append(kv_ref[block // 4, cut, 0:16, :].reshape(128, 128))
            turned.append(vt_ref[block])
            biases.append(jnp.where(here, 0.0, LOW))
        raw = jnp.dot(jnp.concatenate(keys, axis=0), qt_ref[at], preferred_element_type=F32)
        scores = jnp.concatenate(
            [raw[i * 128 : i * 128 + 128] * scale + biases[i] for i in range(4)], axis=0
        )
        new = jnp.max(scores, axis=0, keepdims=True)
        if state is not None:
            new = jnp.maximum(state[0], new)
        weights = jnp.exp2(scores - new)
        total = jnp.sum(weights, axis=0, keepdims=True)
        acc = jnp.dot(
            jnp.concatenate(turned, axis=1), weights.astype(BF), preferred_element_type=F32
        )
        if state is not None:
            again = jnp.exp2(state[0] - new)
            total = state[1] * again + total
            acc = state[2] * again + acc
        return new, total, acc

    def keep(at, state):
        sums_ref[at, 0:1, :] = state[0]
        sums_ref[at, 1:2, :] = state[1]
        acc_ref[at] = state[2]

    def kept(at):
        return sums_ref[at, 0:1, :], sums_ref[at, 1:2, :], acc_ref[at]

    for at in range(16):
        keep(at, look(at, 0, None))

    for group in range(4):
        ats = range(group * 4, group * 4 + 4)
        most = counts[ats[0]]
        for at in ats[1:]:
            most = jnp.maximum(most, counts[at])

        @pl.loop(1, (most + 3) // 4)
        def _(step, ats=ats):
            for at in ats:
                keep(at, look(at, step, kept(at)))

    for at in range(16):
        largest, total, acc = kept(at)
        xq, zq = (x + 4 - at // 4) % 4, at % 4
        o = (acc * (1.0 / total)).T.astype(BF)
        lse = jnp.where(counts[at] > 0, largest + jnp.log2(total), LOW)
        hi = lse.astype(BF)
        rest = lse - hi.astype(F32)
        mid = rest.astype(BF)
        lo = (rest - mid.astype(F32)).astype(BF)
        coded = jnp.concatenate(
            [hi.astype(F32), mid.astype(F32), lo.astype(F32), jnp.zeros((5, 128), F32)], axis=0
        )
        other = jnp.concatenate([coded[:, 64:], coded[:, :64]], axis=1)
        out_ref[xq, zq * 2, 0:64, :] = o[0:64]
        out_ref[xq, zq * 2, 64:72, :] = coded.astype(BF)
        out_ref[xq, zq * 2 + 1, 0:64, :] = o[64:128]
        out_ref[xq, zq * 2 + 1, 64:72, :] = other.astype(BF)


def attend(at, qs, kv):
    smem = pl.BlockSpec(memory_space=pltpu.SMEM)
    vmem = pl.BlockSpec(memory_space=pltpu.VMEM)
    return pl.pallas_call(
        attend_kernel,
        out_shape=jax.ShapeDtypeStruct((4, 8, ROWS, 128), BF),
        in_specs=[smem] + [pl.BlockSpec(memory_space=pl.ANY)] * 5,
        out_specs=vmem,
        scratch_shapes=[
            pltpu.VMEM((4, 34, 16, 128), BF),
            pltpu.VMEM((4, 32, 32, 128), BF),
            pltpu.VMEM((16, 128, 128), BF),
            pltpu.VMEM((16, 128, 128), BF),
            pltpu.VMEM((16, 8, 128), F32),
            pltpu.VMEM((16, 128, 128), F32),
            pltpu.VMEM((4, 32, 128), jnp.int32),
            pltpu.SMEM((4, 32, 128), jnp.int32),
            pltpu.SemaphoreType.DMA((9,)),
        ],
        compiler_params=pltpu.CompilerParams(vmem_limit_bytes=44 * 1024 * 1024),
        cost_estimate=pl.CostEstimate(flops=1 << 30, bytes_accessed=2 << 20, transcendentals=1 << 21),
        name="attend",
    )(at, *qs, kv)


def project_kernel(at_ref, parts_ref, own_in, other_in, y0, y1, y2, y3, att_ref, own_ref, other_ref, sems):
    arriving = []
    for cut in range(6):
        columns = slice(cut * 512, cut * 512 + 512)
        for i, (a, b) in enumerate(((own_in, own_ref), (other_in, other_ref))):
            copy = pltpu.make_async_copy(a.at[:, columns], b.at[:, columns], sems.at[i, cut])
            copy.start()
            arriving.append(copy)
    z_hi, core = at_ref[3], at_ref[4]
    coded = [parts_ref[i // 8, i % 8, 64:72, :].astype(F32) for i in range(32)]
    lse = jnp.concatenate([c[0:1] + c[1:2] + c[2:3] for c in coded], axis=0)
    groups = [lse[8 * i : 8 * i + 8] for i in range(4)]
    top = jnp.maximum(jnp.maximum(groups[0], groups[1]), jnp.maximum(groups[2], groups[3]))
    shares = [jnp.exp2(g - top) for g in groups]
    inverse = 1.0 / (shares[0] + shares[1] + shares[2] + shares[3])
    share = jnp.concatenate([s * inverse for s in shares], axis=0)
    share = jnp.concatenate([share, jnp.zeros((96, 128), F32)], axis=0).T
    for slot in range(3):
        for there in range(2):
            summed = None
            for xk in range(4):
                i = slot * 2 + there
                term = parts_ref[xk, i, 0:64, :].astype(F32) * share[0:64, xk * 8 + i : xk * 8 + i + 1]
                summed = term if summed is None else summed + term
            att_ref[there, :, slot * 128 : slot * 128 + 128] = summed.astype(BF)

    rows = [pl.ds(pl.multiple_of(((z_hi + d) % 4) * 16, 16), 16) for d in range(4)]
    own = jnp.concatenate([att_ref[core, r, :] for r in rows], axis=0)
    other = jnp.concatenate([att_ref[1 - core, r, :] for r in rows], axis=0)
    for cut in range(0, 3072, 512):
        columns = slice(cut, cut + 512)
        arriving[cut // 256].wait()
        arriving[cut // 256 + 1].wait()
        y = jnp.dot(own, own_ref[:, columns], preferred_element_type=F32)
        y = (y + jnp.dot(other, other_ref[:, columns], preferred_element_type=F32)).astype(BF)
        for d, y_ref in enumerate((y0, y1, y2, y3)):
            y_ref[:, columns] = y[d * 16 : d * 16 + 16]


def project(at, parts, own, other):
    vmem = pl.BlockSpec(memory_space=pltpu.VMEM)
    return pl.pallas_call(
        project_kernel,
        out_shape=[jax.ShapeDtypeStruct((16, 3072), BF)] * 4,
        in_specs=[
            pl.BlockSpec(memory_space=pltpu.SMEM),
            vmem,
            pl.BlockSpec(memory_space=pl.ANY),
            pl.BlockSpec(memory_space=pl.ANY),
        ],
        out_specs=[vmem] * 4,
        scratch_shapes=[
            pltpu.VMEM((2, 64, 384), BF),
            pltpu.VMEM((384, 3072), BF),
            pltpu.VMEM((384, 3072), BF),
            pltpu.SemaphoreType.DMA((2, 6)),
        ],
        compiler_params=small,
        name="project",
    )(at, parts, own, other)


def turn(array, axis, step):
    return lax.ppermute(array, axis, [(i, (i + step) % 4) for i in range(4)])


def local(queries, keys_in, values, block_mask, w_out):
    x, y, z = lax.axis_index("x"), lax.axis_index("y"), lax.axis_index("z_lo")
    z_hi, core = lax.axis_index("z_hi"), lax.axis_index("core")
    at = jnp.stack([x, y, jnp.minimum(z, 2), z_hi, core, z]).astype(jnp.int32)
    chosen = choose(block_mask)
    lists = [chosen] + [turn(chosen, "z_lo", d) for d in (1, 2, 3)]
    packed = pack(queries, keys_in, values)
    mine = lax.all_to_all(packed, ("z_lo", "core", "z_hi"), split_axis=0, concat_axis=0, tiled=True)
    q, kv = spread(at, lists, mine)
    q, w_here = lax.optimization_barrier((q, w_out))
    w_other = lax.ppermute(w_here, "core", [(0, 1), (1, 0)])
    qs = [q] + [turn(q, "x", d) for d in (1, 2, 3)]
    kv = lax.all_to_all(kv, "y", split_axis=0, concat_axis=0, tiled=True)
    parts = attend(at, qs, kv)
    parts = lax.all_to_all(
        parts.reshape(32, ROWS, 128), ("x", "z_lo", "core"), split_axis=0, concat_axis=0, tiled=True
    )
    ys = project(at, parts.reshape(4, 8, ROWS, 128), w_out, w_other)
    far, right, left = [turn(ys[d], "z_hi", d).astype(F32) for d in (2, 1, 3)]
    return (((ys[0].astype(F32) + far) + right) + left).astype(BF)


def solution(mesh):
    fine = Mesh(mesh.devices.reshape(4, 2, 4, 4, 4), AXES)
    tokens = P(("z_lo", "x", "y", "z_hi", "core"), None)
    placed = (
        tokens,
        tokens,
        tokens,
        P(("z_hi", "core"), ("z_lo", "x", "y"), None),
        P(("z_hi", "core"), None),
    )
    return jax.shard_map(local, mesh=fine, in_specs=placed, out_specs=tokens, check_vma=False)
```

time: 129 us -> 129 us (level)
  waiting for transfers between devices: 40.5 us -> 44.8 us
  starting transfers between devices: 70.9 us -> 66.7 us
    ppermute x9, starting transfers between devices: 38.7 us -> 34 us  [turn(): return lax.ppermute(array, axis, [(i, (i + step) % 4) for i in range(4)])]
    ppermute x9, waiting for transfers between devices: 18.6 us -> 20.8 us  [turn(): return lax.ppermute(array, axis, [(i, (i + step) % 4) for i in range(4)])]
    all_to_all x1, waiting for transfers between devices: 3.7 us -> 5.84 us  [local(): lax.all_to_all(packed, ('z_lo', 'core', 'z_hi'), split_axis=0, concat_axi...]
  transfers between devices with their start and end apart: 13 -> 13, of which waited for: 8 -> 7; matrix products, arithmetic and copies ran while one was open for 0% -> 0% of each run, Pallas kernels for 7% -> 6%
where the time goes in v4:
time: 129 us; the launch traced here: 128 us
  starting transfers between devices  66.7 us (52%)
  waiting for transfers between devices  44.8 us (35%)
  Pallas kernels  13.5 us (10%)
  local copies, waits for them, and re-layouts  2.56 us (2%)
    ppermute x9, starting transfers between devices, turn(): return lax.ppermute(array, axis, [(i, (i + step) % 4) for i in range(4)])  34 us
    ppermute x9, waiting for transfers between devices, turn(): return lax.ppermute(array, axis, [(i, (i + step) % 4) for i in range(4)])  20.8 us
    all_to_all x1, waiting for transfers between devices, local(): lax.all_to_all(parts.reshape(32, ROWS, 128), ('x', 'z_lo', 'core'), split...  18.2 us
    all_to_all x1, starting transfers between devices, local(): lax.all_to_all(packed, ('z_lo', 'core', 'z_hi'), split_axis=0, concat_axi...  16.8 us
    all_to_all x1, starting transfers between devices, local(): lax.all_to_all(parts.reshape(32, ROWS, 128), ('x', 'z_lo', 'core'), split...  7.29 us
    all_to_all x1, waiting for transfers between devices, local(): lax.all_to_all(packed, ('z_lo', 'core', 'z_hi'), split_axis=0, concat_axi...  5.84 us
    pallas_call x1, Pallas kernels, attend(): pl.pallas_call(attend_kernel, out_shape=jax.ShapeDtypeStruct((4, 8, ROWS,...  5.75 us
    ppermute x1, starting transfers between devices, local(): w_other = lax.ppermute(w_here, 'core', [(0, 1), (1, 0)])  4.42 us
  transfers between devices with their start and end apart: 13, of which 7 were waited for; matrix products, arithmetic and copies ran while one was open for 0% of the time, Pallas kernels for 6%

profile of v4, /device:TPU:1, one launch (start us, length us, event | category | flops | bytes accessed | tf_op | source)
XLA Modules:
  0.0 128.5 jit_solution(12421443380028586536)
XLA Ops:
  0.0 1.9 %pack.1 = bf16[32,48,128]{2,1,0:T(8,128)(2,1)} custom-call(bf16[16,3072]{1,0:T(8,128)(2,1)} %q_in.1, bf16[16,3072]{1,0:T(8,128)(2,1)} %k_in.1, bf16[16,3072]{1,0:T(8,128)(2,1)} %v_in.1), custom_call_target="tpu_custom_call" | custom-call | tf_op jit(solution)/shard_map/pack/pallas_call | solution.py:43
  1.9 16.8 %all-to-all-start = ((bf16[32,48,128]{2,1,0:T(8,128)(2,1)}), bf16[32,48,128]{2,1,0:T(8,128)(2,1)S(1)}, u32[]{:S(2)}, u32[]{:S(2)}) async-start(bf16[32,48,128]{2,1,0:T(8,128)(2,1)} %pack.1), calls=%async_computation | async-start | bytes 786432 | tf_op jit(solution)/shard_map/all_to_all | solution.py:302
  19.3 1.9 %choose.1.l0 = s32[3,8,128]{2,1,0:T(8,128)S(1)} custom-call(s32[3,1,64]{2,1,0:T(1,128)S(1)} %copy-done.3), custom_call_target="tpu_custom_call" | custom-call | tf_op jit(solution)/shard_map/choose/pallas_call | solution.py:68
  21.3 5.1 %collective-permute-start.2 = (s32[3,8,128]{2,1,0:T(8,128)S(1)}, s32[3,8,128]{2,1,0:T(8,128)S(1)}, u32[]{:S(2)}, u32[]{:S(2)}) collective-permute-start(s32[3,8,128]{2,1,0:T(8,128)S(1)} %choose.1.l0), channel_id=1, source_target_pairs={{0,48},{16,0},{32,16},{48,32},{1,49},{17,1},{33,17},{49,33},{2,50}... | collective-permute-start | bytes 36872 | tf_op jit(solution)/shard_map/ppermute | solution.py:292
  26.4 1.9 %collective-permute-start.1 = (s32[3,8,128]{2,1,0:T(8,128)S(1)}, s32[3,8,128]{2,1,0:T(8,128)S(1)}, u32[]{:S(2)}, u32[]{:S(2)}) collective-permute-start(s32[3,8,128]{2,1,0:T(8,128)S(1)} %choose.1.l0), channel_id=1, source_target_pairs={{0,32},{16,48},{32,0},{48,16},{1,33},{17,49},{33,1},{49,17},{2,34}... | collective-permute-start | bytes 36872 | tf_op jit(solution)/shard_map/ppermute | solution.py:292
  28.4 2.4 %collective-permute-start = (s32[3,8,128]{2,1,0:T(8,128)S(1)}, s32[3,8,128]{2,1,0:T(8,128)S(1)}, u32[]{:S(2)}, u32[]{:S(2)}) collective-permute-start(s32[3,8,128]{2,1,0:T(8,128)S(1)} %choose.1.l0), channel_id=1, source_target_pairs={{0,16},{16,32},{32,48},{48,0},{1,17},{17,33},{33,49},{49,1},{2,18}... | collective-permute-start | bytes 36872 | tf_op jit(solution)/shard_map/ppermute | solution.py:292
  30.9 5.8 %collective-permute-done.2.l3 = s32[3,8,128]{2,1,0:T(8,128)S(1)} collective-permute-done((s32[3,8,128]{2,1,0:T(8,128)S(1)}, s32[3,8,128]{2,1,0:T(8,128)S(1)}, u32[]{:S(2)}, u32[]{:S(2)}) %collective-permute-start.2) | collective-permute-done | bytes 12320 | tf_op jit(solution)/shard_map/ppermute | solution.py:292
  36.7 5.8 %all-to-all-done.in_ref = bf16[32,48,128]{2,1,0:T(8,128)(2,1)S(1)} async-done(((bf16[32,48,128]{2,1,0:T(8,128)(2,1)}), bf16[32,48,128]{2,1,0:T(8,128)(2,1)S(1)}, u32[]{:S(2)}, u32[]{:S(2)}) %all-to-all-start) | async-done | bytes 393248 | tf_op jit(solution)/shard_map/all_to_all | solution.py:302
  43.2 1.0 copy-done.1
  44.2 4.2 %all-to-all-start.1 = ((bf16[4,32,32,128]{3,2,1,0:T(8,128)(2,1)}), bf16[4,32,32,128]{3,2,1,0:T(8,128)(2,1)}, u32[]{:S(2)}, u32[]{:S(2)}) async-start(bf16[4,32,32,128]{3,2,1,0:T(8,128)(2,1)} %copy-done.1), calls=%async_computation.1 | async-start | bytes 2097152 | tf_op jit(solution)/shard_map/all_to_all | solution.py:307
  48.5 4.4 %collective-permute-start.5 = (bf16[34,16,128]{2,1,0:T(8,128)(2,1)S(1)}, bf16[34,16,128]{2,1,0:T(8,128)(2,1)S(1)}, u32[]{:S(2)}, u32[]{:S(2)}) collective-permute-start(bf16[34,16,128]{2,1,0:T(8,128)(2,1)S(1)} %get-tuple-element.14.q0), channel_id=1, source_target_pairs={{0,12},{4,0},{8,4},{12,8},{1,13},{5,1},{9,5},{13,9},{2,14},{6,2},{... | collective-permute-start | bytes 417800 | tf_op jit(solution)/shard_map/ppermute | solution.py:292
  52.9 2.4 %collective-permute-start.4 = (bf16[34,16,128]{2,1,0:T(8,128)(2,1)S(1)}, bf16[34,16,128]{2,1,0:T(8,128)(2,1)S(1)}, u32[]{:S(2)}, u32[]{:S(2)}) collective-permute-start(bf16[34,16,128]{2,1,0:T(8,128)(2,1)S(1)} %get-tuple-element.14.q0), channel_id=1, source_target_pairs={{0,8},{4,12},{8,0},{12,4},{1,9},{5,13},{9,1},{13,5},{2,10},{6,14},... | collective-permute-start | bytes 417800 | tf_op jit(solution)/shard_map/ppermute | solution.py:292
  55.3 2.5 %collective-permute-start.3 = (bf16[34,16,128]{2,1,0:T(8,128)(2,1)S(1)}, bf16[34,16,128]{2,1,0:T(8,128)(2,1)S(1)}, u32[]{:S(2)}, u32[]{:S(2)}) collective-permute-start(bf16[34,16,128]{2,1,0:T(8,128)(2,1)S(1)} %get-tuple-element.14.q0), channel_id=1, source_target_pairs={{0,4},{4,8},{8,12},{12,0},{1,5},{5,9},{9,13},{13,1},{2,6},{6,10},{... | collective-permute-start | bytes 417800 | tf_op jit(solution)/shard_map/ppermute | solution.py:292
  57.8 4.4 %collective-permute-start.6 = (bf16[384,3072]{1,0:T(8,128)(2,1)S(1)}, bf16[384,3072]{1,0:T(8,128)(2,1)}, u32[]{:S(2)}, u32[]{:S(2)}) collective-permute-start(bf16[384,3072]{1,0:T(8,128)(2,1)S(1)} %copy-done), channel_id=1, source_target_pairs={{0,64},{64,0},{1,65},{65,1},{2,66},{66,2},{3,67},{67,3},{4,68},{68... | collective-permute-start | bytes 7077896 | tf_op jit(solution)/shard_map/ppermute | solution.py:305
  62.3 1.9 %collective-permute-done.3.q1 = bf16[34,16,128]{2,1,0:T(8,128)(2,1)S(1)} collective-permute-done((bf16[34,16,128]{2,1,0:T(8,128)(2,1)S(1)}, bf16[34,16,128]{2,1,0:T(8,128)(2,1)S(1)}, u32[]{:S(2)}, u32[]{:S(2)}) %collective-permute-start.3) | collective-permute-done | bytes 139296 | tf_op jit(solution)/shard_map/ppermute | solution.py:292
  64.2 5.7 %attend.1 = bf16[4,8,72,128]{3,2,1,0:T(8,128)(2,1)S(1)} custom-call(s32[6]{0:T(128)S(1)} %stack.27.at_ref, bf16[34,16,128]{2,1,0:T(8,128)(2,1)S(1)} %get-tuple-element.14.q0, bf16[34,16,128]{2,1,0:T(8,128)(2,1)S(1)} %collective-permute-done.3.q1, bf16[34,16,128]{2,1,0:T(8,128)(2,1)S(1)} %collective-permute-done.4.q2, ...), custom_call_target="tpu_custom_call" | custom-call | flops 1073741824 | bytes 2097152 | tf_op jit(solution)/shard_map/attend/pallas_call | solution.py:207
  70.8 7.3 %all-to-all-start.2 = ((bf16[32,72,128]{2,1,0:T(8,128)(2,1)}), bf16[32,72,128]{2,1,0:T(8,128)(2,1)S(1)}, u32[]{:S(2)}, u32[]{:S(2)}) async-start(bf16[32,72,128]{2,1,0:T(8,128)(2,1)} %bitcast.9), calls=%async_computation.2 | async-start | bytes 1179648 | tf_op jit(solution)/shard_map/all_to_all | solution.py:309
  78.1 18.2 %all-to-all-done.2 = bf16[32,72,128]{2,1,0:T(8,128)(2,1)S(1)} async-done(((bf16[32,72,128]{2,1,0:T(8,128)(2,1)}), bf16[32,72,128]{2,1,0:T(8,128)(2,1)S(1)}, u32[]{:S(2)}, u32[]{:S(2)}) %all-to-all-start.2) | async-done | bytes 589856 | tf_op jit(solution)/shard_map/all_to_all | solution.py:309
  96.3 3.3 %project.1 = (bf16[16,3072]{1,0:T(8,128)(2,1)S(1)}, bf16[16,3072]{1,0:T(8,128)(2,1)S(1)}, bf16[16,3072]{1,0:T(8,128)(2,1)S(1)}, bf16[16,3072]{1,0:T(8,128)(2,1)S(1)}) custom-call(s32[6]{0:T(128)S(1)} %stack.27.at_ref, bf16[4,8,72,128]{3,2,1,0:T(8,128)(2,1)S(1)} %bitcast.8, bf16[384,3072]{1,0:T(8,128)(2,1)S(1)} %copy-done, ...), custom_call_target="tpu_custom_call" | custom-call | tf_op jit(solution)/shard_map/project/pallas_call | solution.py:270
  99.6 6.0 %collective-permute-start.7 = (bf16[16,3072]{1,0:T(8,128)(2,1)S(1)}, bf16[16,3072]{1,0:T(8,128)(2,1)S(1)}, u32[]{:S(2)}, u32[]{:S(2)}) collective-permute-start(bf16[16,3072]{1,0:T(8,128)(2,1)S(1)} %get-tuple-element.18), channel_id=1, source_target_pairs={{0,256},{128,384},{256,0},{384,128},{1,257},{129,385},{257,1},{385... | collective-permute-start | bytes 294920 | tf_op jit(solution)/shard_map/ppermute | solution.py:292
  105.5 6.5 %collective-permute-start.8 = (bf16[16,3072]{1,0:T(8,128)(2,1)S(1)}, bf16[16,3072]{1,0:T(8,128)(2,1)S(1)}, u32[]{:S(2)}, u32[]{:S(2)}) collective-permute-start(bf16[16,3072]{1,0:T(8,128)(2,1)S(1)} %get-tuple-element.19), channel_id=1, source_target_pairs={{0,128},{128,256},{256,384},{384,0},{1,129},{129,257},{257,385},{3... | collective-permute-start | bytes 294920 | tf_op jit(solution)/shard_map/ppermute | solution.py:292
  112.1 2.6 %collective-permute-start.9 = (bf16[16,3072]{1,0:T(8,128)(2,1)S(1)}, bf16[16,3072]{1,0:T(8,128)(2,1)S(1)}, u32[]{:S(2)}, u32[]{:S(2)}) collective-permute-start(bf16[16,3072]{1,0:T(8,128)(2,1)S(1)} %get-tuple-element.20), channel_id=1, source_target_pairs={{0,384},{128,0},{256,128},{384,256},{1,385},{129,1},{257,129},{385... | collective-permute-start | bytes 294920 | tf_op jit(solution)/shard_map/ppermute | solution.py:292
  114.7 8.4 %collective-permute-done.7 = bf16[16,3072]{1,0:T(8,128)(2,1)S(1)} collective-permute-done((bf16[16,3072]{1,0:T(8,128)(2,1)S(1)}, bf16[16,3072]{1,0:T(8,128)(2,1)S(1)}, u32[]{:S(2)}, u32[]{:S(2)}) %collective-permute-start.7) | collective-permute-done | bytes 98336 | tf_op jit(solution)/shard_map/ppermute | solution.py:292
  123.5 4.3 %collective-permute-done.9 = bf16[16,3072]{1,0:T(8,128)(2,1)S(1)} collective-permute-done((bf16[16,3072]{1,0:T(8,128)(2,1)S(1)}, bf16[16,3072]{1,0:T(8,128)(2,1)S(1)}, u32[]{:S(2)}, u32[]{:S(2)}) %collective-permute-start.9) | collective-permute-done | bytes 98336 | tf_op jit(solution)/shard_map/ppermute | solution.py:292
  (17 shorter events, 3.4 us)
Async XLA Ops:
  0.0 57.8 %copy-start = (bf16[384,3072]{1,0:T(8,128)(2,1)S(1)}, bf16[384,3072]{1,0:T(8,128)(2,1)}, u32[]{:S(2)}) copy-start(bf16[384,3072]{1,0:T(8,128)(2,1)} %own_in.1) | copy-start | bytes 7077892
  1.9 40.7 %all-to-all-start = ((bf16[32,48,128]{2,1,0:T(8,128)(2,1)}), bf16[32,48,128]{2,1,0:T(8,128)(2,1)S(1)}, u32[]{:S(2)}, u32[]{:S(2)}) async-start(bf16[32,48,128]{2,1,0:T(8,128)(2,1)} %pack.1), calls=%async_computation | async-start | bytes 786432 | tf_op jit(solution)/shard_map/all_to_all | solution.py:302
  18.6 0.7 copy-start.3
  21.3 15.4 %collective-permute-start.2 = (s32[3,8,128]{2,1,0:T(8,128)S(1)}, s32[3,8,128]{2,1,0:T(8,128)S(1)}, u32[]{:S(2)}, u32[]{:S(2)}) collective-permute-start(s32[3,8,128]{2,1,0:T(8,128)S(1)} %choose.1.l0), channel_id=1, source_target_pairs={{0,48},{16,0},{32,16},{48,32},{1,49},{17,1},{33,17},{49,33},{2,50}... | collective-permute-start | bytes 36872 | tf_op jit(solution)/shard_map/ppermute | solution.py:292
  26.4 10.3 %collective-permute-start.1 = (s32[3,8,128]{2,1,0:T(8,128)S(1)}, s32[3,8,128]{2,1,0:T(8,128)S(1)}, u32[]{:S(2)}, u32[]{:S(2)}) collective-permute-start(s32[3,8,128]{2,1,0:T(8,128)S(1)} %choose.1.l0), channel_id=1, source_target_pairs={{0,32},{16,48},{32,0},{48,16},{1,33},{17,49},{33,1},{49,17},{2,34}... | collective-permute-start | bytes 36872 | tf_op jit(solution)/shard_map/ppermute | solution.py:292
  28.4 8.3 %collective-permute-start = (s32[3,8,128]{2,1,0:T(8,128)S(1)}, s32[3,8,128]{2,1,0:T(8,128)S(1)}, u32[]{:S(2)}, u32[]{:S(2)}) collective-permute-start(s32[3,8,128]{2,1,0:T(8,128)S(1)} %choose.1.l0), channel_id=1, source_target_pairs={{0,16},{16,32},{32,48},{48,0},{1,17},{17,33},{33,49},{49,1},{2,18}... | collective-permute-start | bytes 36872 | tf_op jit(solution)/shard_map/ppermute | solution.py:292
  43.2 1.0 copy-start.1
  44.2 20.0 %all-to-all-start.1 = ((bf16[4,32,32,128]{3,2,1,0:T(8,128)(2,1)}), bf16[4,32,32,128]{3,2,1,0:T(8,128)(2,1)}, u32[]{:S(2)}, u32[]{:S(2)}) async-start(bf16[4,32,32,128]{3,2,1,0:T(8,128)(2,1)} %copy-done.1), calls=%async_computation.1 | async-start | bytes 2097152 | tf_op jit(solution)/shard_map/all_to_all | solution.py:307
  48.5 13.8 %collective-permute-start.5 = (bf16[34,16,128]{2,1,0:T(8,128)(2,1)S(1)}, bf16[34,16,128]{2,1,0:T(8,128)(2,1)S(1)}, u32[]{:S(2)}, u32[]{:S(2)}) collective-permute-start(bf16[34,16,128]{2,1,0:T(8,128)(2,1)S(1)} %get-tuple-element.14.q0), channel_id=1, source_target_pairs={{0,12},{4,0},{8,4},{12,8},{1,13},{5,1},{9,5},{13,9},{2,14},{6,2},{... | collective-permute-start | bytes 417800 | tf_op jit(solution)/shard_map/ppermute | solution.py:292
  52.9 9.4 %collective-permute-start.4 = (bf16[34,16,128]{2,1,0:T(8,128)(2,1)S(1)}, bf16[34,16,128]{2,1,0:T(8,128)(2,1)S(1)}, u32[]{:S(2)}, u32[]{:S(2)}) collective-permute-start(bf16[34,16,128]{2,1,0:T(8,128)(2,1)S(1)} %get-tuple-element.14.q0), channel_id=1, source_target_pairs={{0,8},{4,12},{8,0},{12,4},{1,9},{5,13},{9,1},{13,5},{2,10},{6,14},... | collective-permute-start | bytes 417800 | tf_op jit(solution)/shard_map/ppermute | solution.py:292
  55.3 8.9 %collective-permute-start.3 = (bf16[34,16,128]{2,1,0:T(8,128)(2,1)S(1)}, bf16[34,16,128]{2,1,0:T(8,128)(2,1)S(1)}, u32[]{:S(2)}, u32[]{:S(2)}) collective-permute-start(bf16[34,16,128]{2,1,0:T(8,128)(2,1)S(1)} %get-tuple-element.14.q0), channel_id=1, source_target_pairs={{0,4},{4,8},{8,12},{12,0},{1,5},{5,9},{9,13},{13,1},{2,6},{6,10},{... | collective-permute-start | bytes 417800 | tf_op jit(solution)/shard_map/ppermute | solution.py:292
  57.8 20.3 %collective-permute-start.6 = (bf16[384,3072]{1,0:T(8,128)(2,1)S(1)}, bf16[384,3072]{1,0:T(8,128)(2,1)}, u32[]{:S(2)}, u32[]{:S(2)}) collective-permute-start(bf16[384,3072]{1,0:T(8,128)(2,1)S(1)} %copy-done), channel_id=1, source_target_pairs={{0,64},{64,0},{1,65},{65,1},{2,66},{66,2},{3,67},{67,3},{4,68},{68... | collective-permute-start | bytes 7077896 | tf_op jit(solution)/shard_map/ppermute | solution.py:305
  70.0 0.8 copy-start.2
  70.8 25.5 %all-to-all-start.2 = ((bf16[32,72,128]{2,1,0:T(8,128)(2,1)}), bf16[32,72,128]{2,1,0:T(8,128)(2,1)S(1)}, u32[]{:S(2)}, u32[]{:S(2)}) async-start(bf16[32,72,128]{2,1,0:T(8,128)(2,1)} %bitcast.9), calls=%async_computation.2 | async-start | bytes 1179648 | tf_op jit(solution)/shard_map/all_to_all | solution.py:309
  99.6 23.6 %collective-permute-start.7 = (bf16[16,3072]{1,0:T(8,128)(2,1)S(1)}, bf16[16,3072]{1,0:T(8,128)(2,1)S(1)}, u32[]{:S(2)}, u32[]{:S(2)}) collective-permute-start(bf16[16,3072]{1,0:T(8,128)(2,1)S(1)} %get-tuple-element.18), channel_id=1, source_target_pairs={{0,256},{128,384},{256,0},{384,128},{1,257},{129,385},{257,1},{385... | collective-permute-start | bytes 294920 | tf_op jit(solution)/shard_map/ppermute | solution.py:292
  105.5 18.0 %collective-permute-start.8 = (bf16[16,3072]{1,0:T(8,128)(2,1)S(1)}, bf16[16,3072]{1,0:T(8,128)(2,1)S(1)}, u32[]{:S(2)}, u32[]{:S(2)}) collective-permute-start(bf16[16,3072]{1,0:T(8,128)(2,1)S(1)} %get-tuple-element.19), channel_id=1, source_target_pairs={{0,128},{128,256},{256,384},{384,0},{1,129},{129,257},{257,385},{3... | collective-permute-start | bytes 294920 | tf_op jit(solution)/shard_map/ppermute | solution.py:292
  112.1 15.7 %collective-permute-start.9 = (bf16[16,3072]{1,0:T(8,128)(2,1)S(1)}, bf16[16,3072]{1,0:T(8,128)(2,1)S(1)}, u32[]{:S(2)}, u32[]{:S(2)}) collective-permute-start(bf16[16,3072]{1,0:T(8,128)(2,1)S(1)} %get-tuple-element.20), channel_id=1, source_target_pairs={{0,384},{128,0},{256,128},{384,256},{1,385},{129,1},{257,129},{385... | collective-permute-start | bytes 294920 | tf_op jit(solution)/shard_map/ppermute | solution.py:292

commit v5 on v4

--- a/solution.py
+++ b/solution.py
@@ -109,7 +109,7 @@
     q_ref, kv_ref, vt_ref, qt_ref, sums_ref, acc_ref, rows_ref, list_ref, sems,
 
 ):
-    x = at_ref[0]
+    x, core = at_ref[0], at_ref[4]
     to_q = [pltpu.make_async_copy(q, q_ref.at[d], sems.at[d]) for d, q in enumerate((q0, q1, q2, q3))]
     to_kv = [pltpu.make_async_copy(kv_in.at[d], kv_ref.at[d], sems.at[4 + d]) for d in range(4)]
     for copy in to_q + to_kv:
@@ -184,7 +184,7 @@
 
     for at in range(16):
         largest, total, acc = kept(at)
-        xq, zq = (x + 4 - at // 4) % 4, at % 4
+        xq, zq = (x + jnp.where(core == 0, 4 - at // 4, at // 4)) % 4, at % 4
         o = (acc * (1.0 / total)).T.astype(BF)
         lse = jnp.where(counts[at] > 0, largest + jnp.log2(total), LOW)
         hi = lse.astype(BF)
@@ -252,7 +252,10 @@
                 summed = term if summed is None else summed + term
             att_ref[there, :, slot * 128 : slot * 128 + 128] = summed.astype(BF)
 
-    rows = [pl.ds(pl.multiple_of(((z_hi + d) % 4) * 16, 16), 16) for d in range(4)]
+    rows = []
+    for d in range(4):
+        there = (z_hi + jnp.where(core == 0, d, 4 - d)) % 4
+        rows.append(pl.ds(pl.multiple_of(there * 16, 16), 16))
     own = jnp.concatenate([att_ref[core, r, :] for r in rows], axis=0)
     other = jnp.concatenate([att_ref[1 - core, r, :] for r in rows], axis=0)
     for cut in range(0, 3072, 512):
@@ -292,6 +295,16 @@
     return lax.ppermute(array, axis, [(i, (i + step) % 4) for i in range(4)])
 
 
+def turn_apart(array, axis, step):
+    names = (axis, "core") if axis == "z_hi" else ("core", axis)
+    pairs = []
+    for core in range(2):
+        for i in range(4):
+            j = (i + (step if core == 0 else -step)) % 4
+            pairs.append((2 * i + core, 2 * j + core) if axis == "z_hi" else (4 * core + i, 4 * core + j))
+    return lax.ppermute(array, names, pairs)
+
+
 def local(queries, keys_in, values, block_mask, w_out):
     x, y, z = lax.axis_index("x"), lax.axis_index("y"), lax.axis_index("z_lo")
     z_hi, core = lax.axis_index("z_hi"), lax.axis_index("core")
@@ -303,14 +316,14 @@
     q, kv = spread(at, lists, mine)
     q, w_here = lax.optimization_barrier((q, w_out))
     w_other = lax.ppermute(w_here, "core", [(0, 1), (1, 0)])
-    qs = [q] + [turn(q, "x", d) for d in (1, 2, 3)]
+    qs = [q] + [turn_apart(q, "x", d) for d in (1, 2, 3)]
     kv = lax.all_to_all(kv, "y", split_axis=0, concat_axis=0, tiled=True)
     parts = attend(at, qs, kv)
     parts = lax.all_to_all(
         parts.reshape(32, ROWS, 128), ("x", "z_lo", "core"), split_axis=0, concat_axis=0, tiled=True
     )
     ys = project(at, parts.reshape(4, 8, ROWS, 128), w_out, w_other)
-    far, right, left = [turn(ys[d], "z_hi", d).astype(F32) for d in (2, 1, 3)]
+    far, right, left = [turn_apart(ys[d], "z_hi", d).astype(F32) for d in (2, 1, 3)]
     return (((ys[0].astype(F32) + far) + right) + left).astype(BF)
 
 

time: 129 us -> 127 us (0.984)
  waiting for transfers between devices: 44.8 us -> 39.9 us
  starting transfers between devices: 66.7 us -> 69.6 us
    ppermute x0 -> x6, starting transfers between devices: none -> 25.9 us  [turn_apart(): return lax.ppermute(array, names, pairs)]
    ppermute x9 -> x3, starting transfers between devices: 34 us -> 9.48 us  [turn(): return lax.ppermute(array, axis, [(i, (i + step) % 4) for i in range(4)])]
    ppermute x9 -> x3, waiting for transfers between devices: 20.8 us -> 5.82 us  [turn(): return lax.ppermute(array, axis, [(i, (i + step) % 4) for i in range(4)])]
    ppermute x0 -> x6, waiting for transfers between devices: none -> 10.1 us  [turn_apart(): return lax.ppermute(array, names, pairs)]
    all_to_all x1, starting transfers between devices: 7.29 us -> 10 us  [local(): lax.all_to_all(parts.reshape(32, ROWS, 128), ('x', 'z_lo', 'core'), split...]
  transfers between devices with their start and end apart: 13 -> 13, of which waited for: 7 -> 5; matrix products, arithmetic and copies ran while one was open for 0% -> 0% of each run, Pallas kernels for 6% -> 6%
where the time goes in v5:
time: 127 us; the launch traced here: 126 us
  starting transfers between devices  69.6 us (55%)
  waiting for transfers between devices  39.9 us (31%)
  Pallas kernels  12.8 us (10%)
  local copies, waits for them, and re-layouts  2.56 us (2%)
    ppermute x6, starting transfers between devices, turn_apart(): return lax.ppermute(array, names, pairs)  25.9 us
    all_to_all x1, waiting for transfers between devices, local(): lax.all_to_all(parts.reshape(32, ROWS, 128), ('x', 'z_lo', 'core'), split...  18.2 us
    all_to_all x1, starting transfers between devices, local(): lax.all_to_all(packed, ('z_lo', 'core', 'z_hi'), split_axis=0, concat_axi...  16.8 us
    ppermute x6, waiting for transfers between devices, turn_apart(): return lax.ppermute(array, names, pairs)  10.1 us
    all_to_all x1, starting transfers between devices, local(): lax.all_to_all(parts.reshape(32, ROWS, 128), ('x', 'z_lo', 'core'), split...  10 us
    ppermute x3, starting transfers between devices, turn(): return lax.ppermute(array, axis, [(i, (i + step) % 4) for i in range(4)])  9.48 us
    all_to_all x1, waiting for transfers between devices, local(): lax.all_to_all(packed, ('z_lo', 'core', 'z_hi'), split_axis=0, concat_axi...  5.84 us
    ppermute x3, waiting for transfers between devices, turn(): return lax.ppermute(array, axis, [(i, (i + step) % 4) for i in range(4)])  5.82 us
  transfers between devices with their start and end apart: 13, of which 5 were waited for; matrix products, arithmetic and copies ran while one was open for 0% of the time, Pallas kernels for 6%

profile of v5, /device:TPU:1, one launch (start us, length us, event | category | flops | bytes accessed | tf_op | source)
XLA Modules:
  0.0 125.8 jit_solution(1306952713697129185)
XLA Ops:
  0.0 1.9 %pack.1 = bf16[32,48,128]{2,1,0:T(8,128)(2,1)} custom-call(bf16[16,3072]{1,0:T(8,128)(2,1)} %q_in.1, bf16[16,3072]{1,0:T(8,128)(2,1)} %k_in.1, bf16[16,3072]{1,0:T(8,128)(2,1)} %v_in.1), custom_call_target="tpu_custom_call" | custom-call | tf_op jit(solution)/shard_map/pack/pallas_call | solution.py:43
  1.9 16.8 %all-to-all-start = ((bf16[32,48,128]{2,1,0:T(8,128)(2,1)}), bf16[32,48,128]{2,1,0:T(8,128)(2,1)S(1)}, u32[]{:S(2)}, u32[]{:S(2)}) async-start(bf16[32,48,128]{2,1,0:T(8,128)(2,1)} %pack.1), calls=%async_computation | async-start | bytes 786432 | tf_op jit(solution)/shard_map/all_to_all | solution.py:315
  19.3 1.9 %choose.1.l0 = s32[3,8,128]{2,1,0:T(8,128)S(1)} custom-call(s32[3,1,64]{2,1,0:T(1,128)S(1)} %copy-done.3), custom_call_target="tpu_custom_call" | custom-call | tf_op jit(solution)/shard_map/choose/pallas_call | solution.py:68
  21.3 5.1 %collective-permute-start.2 = (s32[3,8,128]{2,1,0:T(8,128)S(1)}, s32[3,8,128]{2,1,0:T(8,128)S(1)}, u32[]{:S(2)}, u32[]{:S(2)}) collective-permute-start(s32[3,8,128]{2,1,0:T(8,128)S(1)} %choose.1.l0), channel_id=1, source_target_pairs={{0,48},{16,0},{32,16},{48,32},{1,49},{17,1},{33,17},{49,33},{2,50}... | collective-permute-start | bytes 36872 | tf_op jit(solution)/shard_map/ppermute | solution.py:295
  26.4 1.9 %collective-permute-start.1 = (s32[3,8,128]{2,1,0:T(8,128)S(1)}, s32[3,8,128]{2,1,0:T(8,128)S(1)}, u32[]{:S(2)}, u32[]{:S(2)}) collective-permute-start(s32[3,8,128]{2,1,0:T(8,128)S(1)} %choose.1.l0), channel_id=1, source_target_pairs={{0,32},{16,48},{32,0},{48,16},{1,33},{17,49},{33,1},{49,17},{2,34}... | collective-permute-start | bytes 36872 | tf_op jit(solution)/shard_map/ppermute | solution.py:295
  28.4 2.4 %collective-permute-start = (s32[3,8,128]{2,1,0:T(8,128)S(1)}, s32[3,8,128]{2,1,0:T(8,128)S(1)}, u32[]{:S(2)}, u32[]{:S(2)}) collective-permute-start(s32[3,8,128]{2,1,0:T(8,128)S(1)} %choose.1.l0), channel_id=1, source_target_pairs={{0,16},{16,32},{32,48},{48,0},{1,17},{17,33},{33,49},{49,1},{2,18}... | collective-permute-start | bytes 36872 | tf_op jit(solution)/shard_map/ppermute | solution.py:295
  30.9 5.8 %collective-permute-done.2.l3 = s32[3,8,128]{2,1,0:T(8,128)S(1)} collective-permute-done((s32[3,8,128]{2,1,0:T(8,128)S(1)}, s32[3,8,128]{2,1,0:T(8,128)S(1)}, u32[]{:S(2)}, u32[]{:S(2)}) %collective-permute-start.2) | collective-permute-done | bytes 12320 | tf_op jit(solution)/shard_map/ppermute | solution.py:295
  36.7 5.8 %all-to-all-done.in_ref = bf16[32,48,128]{2,1,0:T(8,128)(2,1)S(1)} async-done(((bf16[32,48,128]{2,1,0:T(8,128)(2,1)}), bf16[32,48,128]{2,1,0:T(8,128)(2,1)S(1)}, u32[]{:S(2)}, u32[]{:S(2)}) %all-to-all-start) | async-done | bytes 393248 | tf_op jit(solution)/shard_map/all_to_all | solution.py:315
  43.2 1.0 copy-done.1
  44.2 4.2 %all-to-all-start.1 = ((bf16[4,32,32,128]{3,2,1,0:T(8,128)(2,1)}), bf16[4,32,32,128]{3,2,1,0:T(8,128)(2,1)}, u32[]{:S(2)}, u32[]{:S(2)}) async-start(bf16[4,32,32,128]{3,2,1,0:T(8,128)(2,1)} %copy-done.1), calls=%async_computation.1 | async-start | bytes 2097152 | tf_op jit(solution)/shard_map/all_to_all | solution.py:320
  48.5 3.1 %collective-permute-start.5 = (bf16[34,16,128]{2,1,0:T(8,128)(2,1)S(1)}, bf16[34,16,128]{2,1,0:T(8,128)(2,1)S(1)}, u32[]{:S(2)}, u32[]{:S(2)}) collective-permute-start(bf16[34,16,128]{2,1,0:T(8,128)(2,1)S(1)} %get-tuple-element.14.q0), channel_id=1, source_target_pairs={{0,12},{4,0},{8,4},{12,8},{64,68},{68,72},{72,76},{76,64},{1,13},{... | collective-permute-start | bytes 417800 | tf_op jit(solution)/shard_map/ppermute | solution.py:305
  51.6 4.4 %collective-permute-start.4 = (bf16[34,16,128]{2,1,0:T(8,128)(2,1)S(1)}, bf16[34,16,128]{2,1,0:T(8,128)(2,1)S(1)}, u32[]{:S(2)}, u32[]{:S(2)}) collective-permute-start(bf16[34,16,128]{2,1,0:T(8,128)(2,1)S(1)} %get-tuple-element.14.q0), channel_id=1, source_target_pairs={{0,8},{4,12},{8,0},{12,4},{64,72},{68,76},{72,64},{76,68},{1,9},{5... | collective-permute-start | bytes 417800 | tf_op jit(solution)/shard_map/ppermute | solution.py:305
  56.0 3.1 %collective-permute-start.3 = (bf16[34,16,128]{2,1,0:T(8,128)(2,1)S(1)}, bf16[34,16,128]{2,1,0:T(8,128)(2,1)S(1)}, u32[]{:S(2)}, u32[]{:S(2)}) collective-permute-start(bf16[34,16,128]{2,1,0:T(8,128)(2,1)S(1)} %get-tuple-element.14.q0), channel_id=1, source_target_pairs={{0,4},{4,8},{8,12},{12,0},{64,76},{68,64},{72,68},{76,72},{1,5},{5... | collective-permute-start | bytes 417800 | tf_op jit(solution)/shard_map/ppermute | solution.py:305
  59.0 3.2 %collective-permute-start.6 = (bf16[384,3072]{1,0:T(8,128)(2,1)S(1)}, bf16[384,3072]{1,0:T(8,128)(2,1)}, u32[]{:S(2)}, u32[]{:S(2)}) collective-permute-start(bf16[384,3072]{1,0:T(8,128)(2,1)S(1)} %copy-done), channel_id=1, source_target_pairs={{0,64},{64,0},{1,65},{65,1},{2,66},{66,2},{3,67},{67,3},{4,68},{68... | collective-permute-start | bytes 7077896 | tf_op jit(solution)/shard_map/ppermute | solution.py:318
  62.6 5.1 %attend.1 = bf16[4,8,72,128]{3,2,1,0:T(8,128)(2,1)S(1)} custom-call(s32[6]{0:T(128)S(1)} %stack.27.at_ref, bf16[34,16,128]{2,1,0:T(8,128)(2,1)S(1)} %get-tuple-element.14.q0, bf16[34,16,128]{2,1,0:T(8,128)(2,1)S(1)} %collective-permute-done.3.q1, bf16[34,16,128]{2,1,0:T(8,128)(2,1)S(1)} %collective-permute-done.4.q2, ...), custom_call_target="tpu_custom_call" | custom-call | flops 1073741824 | bytes 2097152 | tf_op jit(solution)/shard_map/attend/pallas_call | solution.py:207
  67.7 0.8 copy-done.2
  68.5 10.0 %all-to-all-start.2 = ((bf16[32,72,128]{2,1,0:T(8,128)(2,1)}), bf16[32,72,128]{2,1,0:T(8,128)(2,1)S(1)}, u32[]{:S(2)}, u32[]{:S(2)}) async-start(bf16[32,72,128]{2,1,0:T(8,128)(2,1)} %bitcast.9), calls=%async_computation.2 | async-start | bytes 1179648 | tf_op jit(solution)/shard_map/all_to_all | solution.py:322
  78.6 18.2 %all-to-all-done.2 = bf16[32,72,128]{2,1,0:T(8,128)(2,1)S(1)} async-done(((bf16[32,72,128]{2,1,0:T(8,128)(2,1)}), bf16[32,72,128]{2,1,0:T(8,128)(2,1)S(1)}, u32[]{:S(2)}, u32[]{:S(2)}) %all-to-all-start.2) | async-done | bytes 589856 | tf_op jit(solution)/shard_map/all_to_all | solution.py:322
  96.7 3.3 %project.1 = (bf16[16,3072]{1,0:T(8,128)(2,1)S(1)}, bf16[16,3072]{1,0:T(8,128)(2,1)S(1)}, bf16[16,3072]{1,0:T(8,128)(2,1)S(1)}, bf16[16,3072]{1,0:T(8,128)(2,1)S(1)}) custom-call(s32[6]{0:T(128)S(1)} %stack.27.at_ref, bf16[4,8,72,128]{3,2,1,0:T(8,128)(2,1)S(1)} %bitcast.8, bf16[384,3072]{1,0:T(8,128)(2,1)S(1)} %copy-done, ...), custom_call_target="tpu_custom_call" | custom-call | tf_op jit(solution)/shard_map/project/pallas_call | solution.py:273
  100.0 6.2 %collective-permute-start.7 = (bf16[16,3072]{1,0:T(8,128)(2,1)S(1)}, bf16[16,3072]{1,0:T(8,128)(2,1)S(1)}, u32[]{:S(2)}, u32[]{:S(2)}) collective-permute-start(bf16[16,3072]{1,0:T(8,128)(2,1)S(1)} %get-tuple-element.18), channel_id=1, source_target_pairs={{0,256},{128,384},{256,0},{384,128},{64,320},{192,448},{320,64},{4... | collective-permute-start | bytes 294920 | tf_op jit(solution)/shard_map/ppermute | solution.py:305
  106.2 3.7 %collective-permute-start.8 = (bf16[16,3072]{1,0:T(8,128)(2,1)S(1)}, bf16[16,3072]{1,0:T(8,128)(2,1)S(1)}, u32[]{:S(2)}, u32[]{:S(2)}) collective-permute-start(bf16[16,3072]{1,0:T(8,128)(2,1)S(1)} %get-tuple-element.19), channel_id=1, source_target_pairs={{0,128},{128,256},{256,384},{384,0},{64,448},{192,64},{320,192},{4... | collective-permute-start | bytes 294920 | tf_op jit(solution)/shard_map/ppermute | solution.py:305
  109.9 5.5 %collective-permute-start.9 = (bf16[16,3072]{1,0:T(8,128)(2,1)S(1)}, bf16[16,3072]{1,0:T(8,128)(2,1)S(1)}, u32[]{:S(2)}, u32[]{:S(2)}) collective-permute-start(bf16[16,3072]{1,0:T(8,128)(2,1)S(1)} %get-tuple-element.20), channel_id=1, source_target_pairs={{0,384},{128,0},{256,128},{384,256},{64,192},{192,320},{320,448},{... | collective-permute-start | bytes 294920 | tf_op jit(solution)/shard_map/ppermute | solution.py:305
  115.4 9.7 %collective-permute-done.7 = bf16[16,3072]{1,0:T(8,128)(2,1)S(1)} collective-permute-done((bf16[16,3072]{1,0:T(8,128)(2,1)S(1)}, bf16[16,3072]{1,0:T(8,128)(2,1)S(1)}, u32[]{:S(2)}, u32[]{:S(2)}) %collective-permute-start.7) | collective-permute-done | bytes 98336 | tf_op jit(solution)/shard_map/ppermute | solution.py:305
  125.1 0.7 add_convert_fusion
  (17 shorter events, 1.8 us)
Async XLA Ops:
  0.0 59.0 %copy-start = (bf16[384,3072]{1,0:T(8,128)(2,1)S(1)}, bf16[384,3072]{1,0:T(8,128)(2,1)}, u32[]{:S(2)}) copy-start(bf16[384,3072]{1,0:T(8,128)(2,1)} %own_in.1) | copy-start | bytes 7077892
  1.9 40.7 %all-to-all-start = ((bf16[32,48,128]{2,1,0:T(8,128)(2,1)}), bf16[32,48,128]{2,1,0:T(8,128)(2,1)S(1)}, u32[]{:S(2)}, u32[]{:S(2)}) async-start(bf16[32,48,128]{2,1,0:T(8,128)(2,1)} %pack.1), calls=%async_computation | async-start | bytes 786432 | tf_op jit(solution)/shard_map/all_to_all | solution.py:315
  18.6 0.7 copy-start.3
  21.3 15.4 %collective-permute-start.2 = (s32[3,8,128]{2,1,0:T(8,128)S(1)}, s32[3,8,128]{2,1,0:T(8,128)S(1)}, u32[]{:S(2)}, u32[]{:S(2)}) collective-permute-start(s32[3,8,128]{2,1,0:T(8,128)S(1)} %choose.1.l0), channel_id=1, source_target_pairs={{0,48},{16,0},{32,16},{48,32},{1,49},{17,1},{33,17},{49,33},{2,50}... | collective-permute-start | bytes 36872 | tf_op jit(solution)/shard_map/ppermute | solution.py:295
  26.4 10.3 %collective-permute-start.1 = (s32[3,8,128]{2,1,0:T(8,128)S(1)}, s32[3,8,128]{2,1,0:T(8,128)S(1)}, u32[]{:S(2)}, u32[]{:S(2)}) collective-permute-start(s32[3,8,128]{2,1,0:T(8,128)S(1)} %choose.1.l0), channel_id=1, source_target_pairs={{0,32},{16,48},{32,0},{48,16},{1,33},{17,49},{33,1},{49,17},{2,34}... | collective-permute-start | bytes 36872 | tf_op jit(solution)/shard_map/ppermute | solution.py:295
  28.4 8.3 %collective-permute-start = (s32[3,8,128]{2,1,0:T(8,128)S(1)}, s32[3,8,128]{2,1,0:T(8,128)S(1)}, u32[]{:S(2)}, u32[]{:S(2)}) collective-permute-start(s32[3,8,128]{2,1,0:T(8,128)S(1)} %choose.1.l0), channel_id=1, source_target_pairs={{0,16},{16,32},{32,48},{48,0},{1,17},{17,33},{33,49},{49,1},{2,18}... | collective-permute-start | bytes 36872 | tf_op jit(solution)/shard_map/ppermute | solution.py:295
  43.2 1.0 copy-start.1
  44.2 18.4 %all-to-all-start.1 = ((bf16[4,32,32,128]{3,2,1,0:T(8,128)(2,1)}), bf16[4,32,32,128]{3,2,1,0:T(8,128)(2,1)}, u32[]{:S(2)}, u32[]{:S(2)}) async-start(bf16[4,32,32,128]{3,2,1,0:T(8,128)(2,1)} %copy-done.1), calls=%async_computation.1 | async-start | bytes 2097152 | tf_op jit(solution)/shard_map/all_to_all | solution.py:320
  48.5 13.8 %collective-permute-start.5 = (bf16[34,16,128]{2,1,0:T(8,128)(2,1)S(1)}, bf16[34,16,128]{2,1,0:T(8,128)(2,1)S(1)}, u32[]{:S(2)}, u32[]{:S(2)}) collective-permute-start(bf16[34,16,128]{2,1,0:T(8,128)(2,1)S(1)} %get-tuple-element.14.q0), channel_id=1, source_target_pairs={{0,12},{4,0},{8,4},{12,8},{64,68},{68,72},{72,76},{76,64},{1,13},{... | collective-permute-start | bytes 417800 | tf_op jit(solution)/shard_map/ppermute | solution.py:305
  51.6 10.7 %collective-permute-start.4 = (bf16[34,16,128]{2,1,0:T(8,128)(2,1)S(1)}, bf16[34,16,128]{2,1,0:T(8,128)(2,1)S(1)}, u32[]{:S(2)}, u32[]{:S(2)}) collective-permute-start(bf16[34,16,128]{2,1,0:T(8,128)(2,1)S(1)} %get-tuple-element.14.q0), channel_id=1, source_target_pairs={{0,8},{4,12},{8,0},{12,4},{64,72},{68,76},{72,64},{76,68},{1,9},{5... | collective-permute-start | bytes 417800 | tf_op jit(solution)/shard_map/ppermute | solution.py:305
  56.0 6.7 %collective-permute-start.3 = (bf16[34,16,128]{2,1,0:T(8,128)(2,1)S(1)}, bf16[34,16,128]{2,1,0:T(8,128)(2,1)S(1)}, u32[]{:S(2)}, u32[]{:S(2)}) collective-permute-start(bf16[34,16,128]{2,1,0:T(8,128)(2,1)S(1)} %get-tuple-element.14.q0), channel_id=1, source_target_pairs={{0,4},{4,8},{8,12},{12,0},{64,76},{68,64},{72,68},{76,72},{1,5},{5... | collective-permute-start | bytes 417800 | tf_op jit(solution)/shard_map/ppermute | solution.py:305
  59.0 19.5 %collective-permute-start.6 = (bf16[384,3072]{1,0:T(8,128)(2,1)S(1)}, bf16[384,3072]{1,0:T(8,128)(2,1)}, u32[]{:S(2)}, u32[]{:S(2)}) collective-permute-start(bf16[384,3072]{1,0:T(8,128)(2,1)S(1)} %copy-done), channel_id=1, source_target_pairs={{0,64},{64,0},{1,65},{65,1},{2,66},{66,2},{3,67},{67,3},{4,68},{68... | collective-permute-start | bytes 7077896 | tf_op jit(solution)/shard_map/ppermute | solution.py:318
  67.7 0.8 copy-start.2
  68.5 28.2 %all-to-all-start.2 = ((bf16[32,72,128]{2,1,0:T(8,128)(2,1)}), bf16[32,72,128]{2,1,0:T(8,128)(2,1)S(1)}, u32[]{:S(2)}, u32[]{:S(2)}) async-start(bf16[32,72,128]{2,1,0:T(8,128)(2,1)} %bitcast.9), calls=%async_computation.2 | async-start | bytes 1179648 | tf_op jit(solution)/shard_map/all_to_all | solution.py:322
  100.0 25.1 %collective-permute-start.7 = (bf16[16,3072]{1,0:T(8,128)(2,1)S(1)}, bf16[16,3072]{1,0:T(8,128)(2,1)S(1)}, u32[]{:S(2)}, u32[]{:S(2)}) collective-permute-start(bf16[16,3072]{1,0:T(8,128)(2,1)S(1)} %get-tuple-element.18), channel_id=1, source_target_pairs={{0,256},{128,384},{256,0},{384,128},{64,320},{192,448},{320,64},{4... | collective-permute-start | bytes 294920 | tf_op jit(solution)/shard_map/ppermute | solution.py:305
  106.2 19.0 %collective-permute-start.8 = (bf16[16,3072]{1,0:T(8,128)(2,1)S(1)}, bf16[16,3072]{1,0:T(8,128)(2,1)S(1)}, u32[]{:S(2)}, u32[]{:S(2)}) collective-permute-start(bf16[16,3072]{1,0:T(8,128)(2,1)S(1)} %get-tuple-element.19), channel_id=1, source_target_pairs={{0,128},{128,256},{256,384},{384,0},{64,448},{192,64},{320,192},{4... | collective-permute-start | bytes 294920 | tf_op jit(solution)/shard_map/ppermute | solution.py:305
  109.9 15.2 %collective-permute-start.9 = (bf16[16,3072]{1,0:T(8,128)(2,1)S(1)}, bf16[16,3072]{1,0:T(8,128)(2,1)S(1)}, u32[]{:S(2)}, u32[]{:S(2)}) collective-permute-start(bf16[16,3072]{1,0:T(8,128)(2,1)S(1)} %get-tuple-element.20), channel_id=1, source_target_pairs={{0,384},{128,0},{256,128},{384,256},{64,192},{192,320},{320,448},{... | collective-permute-start | bytes 294920 | tf_op jit(solution)/shard_map/ppermute | solution.py:305

commit v6 on v5

--- a/solution.py
+++ b/solution.py
@@ -226,14 +226,14 @@
     )(at, *qs, kv)
 
 
-def project_kernel(at_ref, parts_ref, own_in, other_in, y0, y1, y2, y3, att_ref, own_ref, other_ref, sems):
+def project_kernel(at_ref, parts_ref, own_ref, other_in, y0, y1, y2, y3, att_ref, other_ref, sems):
     arriving = []
     for cut in range(6):
         columns = slice(cut * 512, cut * 512 + 512)
-        for i, (a, b) in enumerate(((own_in, own_ref), (other_in, other_ref))):
-            copy = pltpu.make_async_copy(a.at[:, columns], b.at[:, columns], sems.at[i, cut])
-            copy.start()
-            arriving.append(copy)
+        arriving.append(
+            pltpu.make_async_copy(other_in.at[:, columns], other_ref.at[:, columns], sems.at[cut])
+        )
+        arriving[-1].start()
     z_hi, core = at_ref[3], at_ref[4]
     coded = [parts_ref[i // 8, i % 8, 64:72, :].astype(F32) for i in range(32)]
     lse = jnp.concatenate([c[0:1] + c[1:2] + c[2:3] for c in coded], axis=0)
@@ -260,9 +260,8 @@
     other = jnp.concatenate([att_ref[1 - core, r, :] for r in rows], axis=0)
     for cut in range(0, 3072, 512):
         columns = slice(cut, cut + 512)
-        arriving[cut // 256].wait()
-        arriving[cut // 256 + 1].wait()
         y = jnp.dot(own, own_ref[:, columns], preferred_element_type=F32)
+        arriving[cut // 512].wait()
         y = (y + jnp.dot(other, other_ref[:, columns], preferred_element_type=F32)).astype(BF)
         for d, y_ref in enumerate((y0, y1, y2, y3)):
             y_ref[:, columns] = y[d * 16 : d * 16 + 16]
@@ -276,15 +275,14 @@
         in_specs=[
             pl.BlockSpec(memory_space=pltpu.SMEM),
             vmem,
-            pl.BlockSpec(memory_space=pl.ANY),
+            vmem,
             pl.BlockSpec(memory_space=pl.ANY),
         ],
         out_specs=[vmem] * 4,
         scratch_shapes=[
             pltpu.VMEM((2, 64, 384), BF),
             pltpu.VMEM((384, 3072), BF),
-            pltpu.VMEM((384, 3072), BF),
-            pltpu.SemaphoreType.DMA((2, 6)),
+            pltpu.SemaphoreType.DMA((6,)),
         ],
         compiler_params=small,
         name="project",

time: 127 us -> 127 us (level)
  no operation moved by 1% of the time
where the time goes in v6:
time: 127 us; the launch traced here: 126 us
  starting transfers between devices  68.9 us (54%)
  waiting for transfers between devices  40.8 us (32%)
  Pallas kernels  12.9 us (10%)
  local copies, waits for them, and re-layouts  2.56 us (2%)
    ppermute x6, starting transfers between devices, turn_apart(): return lax.ppermute(array, names, pairs)  25.3 us
    all_to_all x1, waiting for transfers between devices, local(): lax.all_to_all(parts.reshape(32, ROWS, 128), ('x', 'z_lo', 'core'), split...  18.2 us
    all_to_all x1, starting transfers between devices, local(): lax.all_to_all(packed, ('z_lo', 'core', 'z_hi'), split_axis=0, concat_axi...  16.8 us
    ppermute x6, waiting for transfers between devices, turn_apart(): return lax.ppermute(array, names, pairs)  10.9 us
    all_to_all x1, starting transfers between devices, local(): lax.all_to_all(parts.reshape(32, ROWS, 128), ('x', 'z_lo', 'core'), split...  9.97 us
    ppermute x3, starting transfers between devices, turn(): return lax.ppermute(array, axis, [(i, (i + step) % 4) for i in range(4)])  9.48 us
    all_to_all x1, waiting for transfers between devices, local(): lax.all_to_all(packed, ('z_lo', 'core', 'z_hi'), split_axis=0, concat_axi...  5.84 us
    ppermute x3, waiting for transfers between devices, turn(): return lax.ppermute(array, axis, [(i, (i + step) % 4) for i in range(4)])  5.82 us
  transfers between devices with their start and end apart: 13, of which 5 were waited for; matrix products, arithmetic and copies ran while one was open for 0% of the time, Pallas kernels for 6%

profile of v6, /device:TPU:1, one launch (start us, length us, event | category | flops | bytes accessed | tf_op | source)
XLA Modules:
  0.0 126.0 jit_solution(9518213778528162454)
XLA Ops:
  0.0 1.9 %pack.1 = bf16[32,48,128]{2,1,0:T(8,128)(2,1)} custom-call(bf16[16,3072]{1,0:T(8,128)(2,1)} %q_in.1, bf16[16,3072]{1,0:T(8,128)(2,1)} %k_in.1, bf16[16,3072]{1,0:T(8,128)(2,1)} %v_in.1), custom_call_target="tpu_custom_call" | custom-call | tf_op jit(solution)/shard_map/pack/pallas_call | solution.py:43
  1.9 16.8 %all-to-all-start = ((bf16[32,48,128]{2,1,0:T(8,128)(2,1)}), bf16[32,48,128]{2,1,0:T(8,128)(2,1)S(1)}, u32[]{:S(2)}, u32[]{:S(2)}) async-start(bf16[32,48,128]{2,1,0:T(8,128)(2,1)} %pack.1), calls=%async_computation | async-start | bytes 786432 | tf_op jit(solution)/shard_map/all_to_all | solution.py:313
  19.3 1.9 %choose.1.l0 = s32[3,8,128]{2,1,0:T(8,128)S(1)} custom-call(s32[3,1,64]{2,1,0:T(1,128)S(1)} %copy-done.3), custom_call_target="tpu_custom_call" | custom-call | tf_op jit(solution)/shard_map/choose/pallas_call | solution.py:68
  21.3 5.1 %collective-permute-start.2 = (s32[3,8,128]{2,1,0:T(8,128)S(1)}, s32[3,8,128]{2,1,0:T(8,128)S(1)}, u32[]{:S(2)}, u32[]{:S(2)}) collective-permute-start(s32[3,8,128]{2,1,0:T(8,128)S(1)} %choose.1.l0), channel_id=1, source_target_pairs={{0,48},{16,0},{32,16},{48,32},{1,49},{17,1},{33,17},{49,33},{2,50}... | collective-permute-start | bytes 36872 | tf_op jit(solution)/shard_map/ppermute | solution.py:293
  26.4 1.9 %collective-permute-start.1 = (s32[3,8,128]{2,1,0:T(8,128)S(1)}, s32[3,8,128]{2,1,0:T(8,128)S(1)}, u32[]{:S(2)}, u32[]{:S(2)}) collective-permute-start(s32[3,8,128]{2,1,0:T(8,128)S(1)} %choose.1.l0), channel_id=1, source_target_pairs={{0,32},{16,48},{32,0},{48,16},{1,33},{17,49},{33,1},{49,17},{2,34}... | collective-permute-start | bytes 36872 | tf_op jit(solution)/shard_map/ppermute | solution.py:293
  28.4 2.4 %collective-permute-start = (s32[3,8,128]{2,1,0:T(8,128)S(1)}, s32[3,8,128]{2,1,0:T(8,128)S(1)}, u32[]{:S(2)}, u32[]{:S(2)}) collective-permute-start(s32[3,8,128]{2,1,0:T(8,128)S(1)} %choose.1.l0), channel_id=1, source_target_pairs={{0,16},{16,32},{32,48},{48,0},{1,17},{17,33},{33,49},{49,1},{2,18}... | collective-permute-start | bytes 36872 | tf_op jit(solution)/shard_map/ppermute | solution.py:293
  30.9 5.8 %collective-permute-done.2.l3 = s32[3,8,128]{2,1,0:T(8,128)S(1)} collective-permute-done((s32[3,8,128]{2,1,0:T(8,128)S(1)}, s32[3,8,128]{2,1,0:T(8,128)S(1)}, u32[]{:S(2)}, u32[]{:S(2)}) %collective-permute-start.2) | collective-permute-done | bytes 12320 | tf_op jit(solution)/shard_map/ppermute | solution.py:293
  36.7 5.8 %all-to-all-done.in_ref = bf16[32,48,128]{2,1,0:T(8,128)(2,1)S(1)} async-done(((bf16[32,48,128]{2,1,0:T(8,128)(2,1)}), bf16[32,48,128]{2,1,0:T(8,128)(2,1)S(1)}, u32[]{:S(2)}, u32[]{:S(2)}) %all-to-all-start) | async-done | bytes 393248 | tf_op jit(solution)/shard_map/all_to_all | solution.py:313
  43.2 1.0 copy-done.1
  44.2 4.2 %all-to-all-start.1 = ((bf16[4,32,32,128]{3,2,1,0:T(8,128)(2,1)}), bf16[4,32,32,128]{3,2,1,0:T(8,128)(2,1)}, u32[]{:S(2)}, u32[]{:S(2)}) async-start(bf16[4,32,32,128]{3,2,1,0:T(8,128)(2,1)} %copy-done.1), calls=%async_computation.1 | async-start | bytes 2097152 | tf_op jit(solution)/shard_map/all_to_all | solution.py:318
  48.5 3.1 %collective-permute-start.5 = (bf16[34,16,128]{2,1,0:T(8,128)(2,1)S(1)}, bf16[34,16,128]{2,1,0:T(8,128)(2,1)S(1)}, u32[]{:S(2)}, u32[]{:S(2)}) collective-permute-start(bf16[34,16,128]{2,1,0:T(8,128)(2,1)S(1)} %get-tuple-element.14.q0), channel_id=1, source_target_pairs={{0,12},{4,0},{8,4},{12,8},{64,68},{68,72},{72,76},{76,64},{1,13},{... | collective-permute-start | bytes 417800 | tf_op jit(solution)/shard_map/ppermute | solution.py:303
  51.6 4.4 %collective-permute-start.4 = (bf16[34,16,128]{2,1,0:T(8,128)(2,1)S(1)}, bf16[34,16,128]{2,1,0:T(8,128)(2,1)S(1)}, u32[]{:S(2)}, u32[]{:S(2)}) collective-permute-start(bf16[34,16,128]{2,1,0:T(8,128)(2,1)S(1)} %get-tuple-element.14.q0), channel_id=1, source_target_pairs={{0,8},{4,12},{8,0},{12,4},{64,72},{68,76},{72,64},{76,68},{1,9},{5... | collective-permute-start | bytes 417800 | tf_op jit(solution)/shard_map/ppermute | solution.py:303
  56.0 3.1 %collective-permute-start.3 = (bf16[34,16,128]{2,1,0:T(8,128)(2,1)S(1)}, bf16[34,16,128]{2,1,0:T(8,128)(2,1)S(1)}, u32[]{:S(2)}, u32[]{:S(2)}) collective-permute-start(bf16[34,16,128]{2,1,0:T(8,128)(2,1)S(1)} %get-tuple-element.14.q0), channel_id=1, source_target_pairs={{0,4},{4,8},{8,12},{12,0},{64,76},{68,64},{72,68},{76,72},{1,5},{5... | collective-permute-start | bytes 417800 | tf_op jit(solution)/shard_map/ppermute | solution.py:303
  59.0 3.2 %collective-permute-start.6 = (bf16[384,3072]{1,0:T(8,128)(2,1)S(1)}, bf16[384,3072]{1,0:T(8,128)(2,1)}, u32[]{:S(2)}, u32[]{:S(2)}) collective-permute-start(bf16[384,3072]{1,0:T(8,128)(2,1)S(1)} %copy-done), channel_id=1, source_target_pairs={{0,64},{64,0},{1,65},{65,1},{2,66},{66,2},{3,67},{67,3},{4,68},{68... | collective-permute-start | bytes 7077896 | tf_op jit(solution)/shard_map/ppermute | solution.py:316
  62.6 5.1 %attend.1 = bf16[4,8,72,128]{3,2,1,0:T(8,128)(2,1)S(1)} custom-call(s32[6]{0:T(128)S(1)} %stack.27.at_ref, bf16[34,16,128]{2,1,0:T(8,128)(2,1)S(1)} %get-tuple-element.14.q0, bf16[34,16,128]{2,1,0:T(8,128)(2,1)S(1)} %collective-permute-done.3.q1, bf16[34,16,128]{2,1,0:T(8,128)(2,1)S(1)} %collective-permute-done.4.q2, ...), custom_call_target="tpu_custom_call" | custom-call | flops 1073741824 | bytes 2097152 | tf_op jit(solution)/shard_map/attend/pallas_call | solution.py:207
  67.7 0.8 copy-done.2
  68.5 10.0 %all-to-all-start.2 = ((bf16[32,72,128]{2,1,0:T(8,128)(2,1)}), bf16[32,72,128]{2,1,0:T(8,128)(2,1)S(1)}, u32[]{:S(2)}, u32[]{:S(2)}) async-start(bf16[32,72,128]{2,1,0:T(8,128)(2,1)} %bitcast.9), calls=%async_computation.2 | async-start | bytes 1179648 | tf_op jit(solution)/shard_map/all_to_all | solution.py:320
  78.5 18.2 %all-to-all-done.2 = bf16[32,72,128]{2,1,0:T(8,128)(2,1)S(1)} async-done(((bf16[32,72,128]{2,1,0:T(8,128)(2,1)}), bf16[32,72,128]{2,1,0:T(8,128)(2,1)S(1)}, u32[]{:S(2)}, u32[]{:S(2)}) %all-to-all-start.2) | async-done | bytes 589856 | tf_op jit(solution)/shard_map/all_to_all | solution.py:320
  96.7 3.3 %project.1 = (bf16[16,3072]{1,0:T(8,128)(2,1)S(1)}, bf16[16,3072]{1,0:T(8,128)(2,1)S(1)}, bf16[16,3072]{1,0:T(8,128)(2,1)S(1)}, bf16[16,3072]{1,0:T(8,128)(2,1)S(1)}) custom-call(s32[6]{0:T(128)S(1)} %stack.27.at_ref, bf16[4,8,72,128]{3,2,1,0:T(8,128)(2,1)S(1)} %bitcast.8, bf16[384,3072]{1,0:T(8,128)(2,1)S(1)} %copy-done, ...), custom_call_target="tpu_custom_call" | custom-call | tf_op jit(solution)/shard_map/project/pallas_call | solution.py:272
  100.0 5.5 %collective-permute-start.7 = (bf16[16,3072]{1,0:T(8,128)(2,1)S(1)}, bf16[16,3072]{1,0:T(8,128)(2,1)S(1)}, u32[]{:S(2)}, u32[]{:S(2)}) collective-permute-start(bf16[16,3072]{1,0:T(8,128)(2,1)S(1)} %get-tuple-element.18), channel_id=1, source_target_pairs={{0,256},{128,384},{256,0},{384,128},{64,320},{192,448},{320,64},{4... | collective-permute-start | bytes 294920 | tf_op jit(solution)/shard_map/ppermute | solution.py:303
  105.6 4.4 %collective-permute-start.8 = (bf16[16,3072]{1,0:T(8,128)(2,1)S(1)}, bf16[16,3072]{1,0:T(8,128)(2,1)S(1)}, u32[]{:S(2)}, u32[]{:S(2)}) collective-permute-start(bf16[16,3072]{1,0:T(8,128)(2,1)S(1)} %get-tuple-element.19), channel_id=1, source_target_pairs={{0,128},{128,256},{256,384},{384,0},{64,448},{192,64},{320,192},{4... | collective-permute-start | bytes 294920 | tf_op jit(solution)/shard_map/ppermute | solution.py:303
  109.9 4.8 %collective-permute-start.9 = (bf16[16,3072]{1,0:T(8,128)(2,1)S(1)}, bf16[16,3072]{1,0:T(8,128)(2,1)S(1)}, u32[]{:S(2)}, u32[]{:S(2)}) collective-permute-start(bf16[16,3072]{1,0:T(8,128)(2,1)S(1)} %get-tuple-element.20), channel_id=1, source_target_pairs={{0,384},{128,0},{256,128},{384,256},{64,192},{192,320},{320,448},{... | collective-permute-start | bytes 294920 | tf_op jit(solution)/shard_map/ppermute | solution.py:303
  114.8 10.6 %collective-permute-done.7 = bf16[16,3072]{1,0:T(8,128)(2,1)S(1)} collective-permute-done((bf16[16,3072]{1,0:T(8,128)(2,1)S(1)}, bf16[16,3072]{1,0:T(8,128)(2,1)S(1)}, u32[]{:S(2)}, u32[]{:S(2)}) %collective-permute-start.7) | collective-permute-done | bytes 98336 | tf_op jit(solution)/shard_map/ppermute | solution.py:303
  125.3 0.7 add_convert_fusion
  (17 shorter events, 1.8 us)
Async XLA Ops:
  0.0 59.0 %copy-start = (bf16[384,3072]{1,0:T(8,128)(2,1)S(1)}, bf16[384,3072]{1,0:T(8,128)(2,1)}, u32[]{:S(2)}) copy-start(bf16[384,3072]{1,0:T(8,128)(2,1)} %own_ref.1) | copy-start | bytes 7077892
  1.9 40.7 %all-to-all-start = ((bf16[32,48,128]{2,1,0:T(8,128)(2,1)}), bf16[32,48,128]{2,1,0:T(8,128)(2,1)S(1)}, u32[]{:S(2)}, u32[]{:S(2)}) async-start(bf16[32,48,128]{2,1,0:T(8,128)(2,1)} %pack.1), calls=%async_computation | async-start | bytes 786432 | tf_op jit(solution)/shard_map/all_to_all | solution.py:313
  18.6 0.7 copy-start.3
  21.3 15.4 %collective-permute-start.2 = (s32[3,8,128]{2,1,0:T(8,128)S(1)}, s32[3,8,128]{2,1,0:T(8,128)S(1)}, u32[]{:S(2)}, u32[]{:S(2)}) collective-permute-start(s32[3,8,128]{2,1,0:T(8,128)S(1)} %choose.1.l0), channel_id=1, source_target_pairs={{0,48},{16,0},{32,16},{48,32},{1,49},{17,1},{33,17},{49,33},{2,50}... | collective-permute-start | bytes 36872 | tf_op jit(solution)/shard_map/ppermute | solution.py:293
  26.4 10.3 %collective-permute-start.1 = (s32[3,8,128]{2,1,0:T(8,128)S(1)}, s32[3,8,128]{2,1,0:T(8,128)S(1)}, u32[]{:S(2)}, u32[]{:S(2)}) collective-permute-start(s32[3,8,128]{2,1,0:T(8,128)S(1)} %choose.1.l0), channel_id=1, source_target_pairs={{0,32},{16,48},{32,0},{48,16},{1,33},{17,49},{33,1},{49,17},{2,34}... | collective-permute-start | bytes 36872 | tf_op jit(solution)/shard_map/ppermute | solution.py:293
  28.4 8.3 %collective-permute-start = (s32[3,8,128]{2,1,0:T(8,128)S(1)}, s32[3,8,128]{2,1,0:T(8,128)S(1)}, u32[]{:S(2)}, u32[]{:S(2)}) collective-permute-start(s32[3,8,128]{2,1,0:T(8,128)S(1)} %choose.1.l0), channel_id=1, source_target_pairs={{0,16},{16,32},{32,48},{48,0},{1,17},{17,33},{33,49},{49,1},{2,18}... | collective-permute-start | bytes 36872 | tf_op jit(solution)/shard_map/ppermute | solution.py:293
  43.2 1.0 copy-start.1
  44.2 18.4 %all-to-all-start.1 = ((bf16[4,32,32,128]{3,2,1,0:T(8,128)(2,1)}), bf16[4,32,32,128]{3,2,1,0:T(8,128)(2,1)}, u32[]{:S(2)}, u32[]{:S(2)}) async-start(bf16[4,32,32,128]{3,2,1,0:T(8,128)(2,1)} %copy-done.1), calls=%async_computation.1 | async-start | bytes 2097152 | tf_op jit(solution)/shard_map/all_to_all | solution.py:318
  48.5 13.8 %collective-permute-start.5 = (bf16[34,16,128]{2,1,0:T(8,128)(2,1)S(1)}, bf16[34,16,128]{2,1,0:T(8,128)(2,1)S(1)}, u32[]{:S(2)}, u32[]{:S(2)}) collective-permute-start(bf16[34,16,128]{2,1,0:T(8,128)(2,1)S(1)} %get-tuple-element.14.q0), channel_id=1, source_target_pairs={{0,12},{4,0},{8,4},{12,8},{64,68},{68,72},{72,76},{76,64},{1,13},{... | collective-permute-start | bytes 417800 | tf_op jit(solution)/shard_map/ppermute | solution.py:303
  51.6 10.7 %collective-permute-start.4 = (bf16[34,16,128]{2,1,0:T(8,128)(2,1)S(1)}, bf16[34,16,128]{2,1,0:T(8,128)(2,1)S(1)}, u32[]{:S(2)}, u32[]{:S(2)}) collective-permute-start(bf16[34,16,128]{2,1,0:T(8,128)(2,1)S(1)} %get-tuple-element.14.q0), channel_id=1, source_target_pairs={{0,8},{4,12},{8,0},{12,4},{64,72},{68,76},{72,64},{76,68},{1,9},{5... | collective-permute-start | bytes 417800 | tf_op jit(solution)/shard_map/ppermute | solution.py:303
  56.0 6.7 %collective-permute-start.3 = (bf16[34,16,128]{2,1,0:T(8,128)(2,1)S(1)}, bf16[34,16,128]{2,1,0:T(8,128)(2,1)S(1)}, u32[]{:S(2)}, u32[]{:S(2)}) collective-permute-start(bf16[34,16,128]{2,1,0:T(8,128)(2,1)S(1)} %get-tuple-element.14.q0), channel_id=1, source_target_pairs={{0,4},{4,8},{8,12},{12,0},{64,76},{68,64},{72,68},{76,72},{1,5},{5... | collective-permute-start | bytes 417800 | tf_op jit(solution)/shard_map/ppermute | solution.py:303
  59.0 19.5 %collective-permute-start.6 = (bf16[384,3072]{1,0:T(8,128)(2,1)S(1)}, bf16[384,3072]{1,0:T(8,128)(2,1)}, u32[]{:S(2)}, u32[]{:S(2)}) collective-permute-start(bf16[384,3072]{1,0:T(8,128)(2,1)S(1)} %copy-done), channel_id=1, source_target_pairs={{0,64},{64,0},{1,65},{65,1},{2,66},{66,2},{3,67},{67,3},{4,68},{68... | collective-permute-start | bytes 7077896 | tf_op jit(solution)/shard_map/ppermute | solution.py:316
  67.7 0.8 copy-start.2
  68.5 28.2 %all-to-all-start.2 = ((bf16[32,72,128]{2,1,0:T(8,128)(2,1)}), bf16[32,72,128]{2,1,0:T(8,128)(2,1)S(1)}, u32[]{:S(2)}, u32[]{:S(2)}) async-start(bf16[32,72,128]{2,1,0:T(8,128)(2,1)} %bitcast.9), calls=%async_computation.2 | async-start | bytes 1179648 | tf_op jit(solution)/shard_map/all_to_all | solution.py:320
  100.0 25.3 %collective-permute-start.7 = (bf16[16,3072]{1,0:T(8,128)(2,1)S(1)}, bf16[16,3072]{1,0:T(8,128)(2,1)S(1)}, u32[]{:S(2)}, u32[]{:S(2)}) collective-permute-start(bf16[16,3072]{1,0:T(8,128)(2,1)S(1)} %get-tuple-element.18), channel_id=1, source_target_pairs={{0,256},{128,384},{256,0},{384,128},{64,320},{192,448},{320,64},{4... | collective-permute-start | bytes 294920 | tf_op jit(solution)/shard_map/ppermute | solution.py:303
  105.6 19.8 %collective-permute-start.8 = (bf16[16,3072]{1,0:T(8,128)(2,1)S(1)}, bf16[16,3072]{1,0:T(8,128)(2,1)S(1)}, u32[]{:S(2)}, u32[]{:S(2)}) collective-permute-start(bf16[16,3072]{1,0:T(8,128)(2,1)S(1)} %get-tuple-element.19), channel_id=1, source_target_pairs={{0,128},{128,256},{256,384},{384,0},{64,448},{192,64},{320,192},{4... | collective-permute-start | bytes 294920 | tf_op jit(solution)/shard_map/ppermute | solution.py:303
  109.9 15.4 %collective-permute-start.9 = (bf16[16,3072]{1,0:T(8,128)(2,1)S(1)}, bf16[16,3072]{1,0:T(8,128)(2,1)S(1)}, u32[]{:S(2)}, u32[]{:S(2)}) collective-permute-start(bf16[16,3072]{1,0:T(8,128)(2,1)S(1)} %get-tuple-element.20), channel_id=1, source_target_pairs={{0,384},{128,0},{256,128},{384,256},{64,192},{192,320},{320,448},{... | collective-permute-start | bytes 294920 | tf_op jit(solution)/shard_map/ppermute | solution.py:303
